TPU v7x, 32 devices: a whole 2x2x4 slice. The times are simulated.
32 devices in a mesh: dp: 8 (over z, y), tensor: 4 (over x, core).
Axes of the slice: x: 2, y: 2, z: 4, core: 2. Of those that a mesh axis runs over, the one named last changes fastest.
Arguments:
- hidden_rows: bfloat16 [2048, 8, 768], P('tensor', 'dp'), may hold values from -6 to 6
- out_grad: bfloat16 [2048, 8, 768], P('tensor', 'dp'), may hold values from -6 to 6
- doc_lengths: int32 [8, 4], P('dp'), may hold values from 1 to 2045, as said below
- zx_weight: bfloat16 [2, 768, 1536], P(None, 'dp', 'tensor'), may hold values from -0.21875 to 0.21875
- step_weight: bfloat16 [768, 24], P('dp', 'tensor'), may hold values from -0.21875 to 0.21875
- bc_weight: bfloat16 [768, 256], P('dp'), may hold values from -0.21875 to 0.21875
- conv_inner: bfloat16 [24, 256], P('tensor', 'dp'), may hold values from -3 to 3
- conv_shared: bfloat16 [1024], P('dp'), may hold values from -3 to 3
- out_weight: bfloat16 [1536, 768], P('tensor', 'dp'), may hold values from -0.15625 to 0.15625
- decay_log: float32 [24], P('tensor'), may hold values from 0 to 2.77
- step_bias: float32 [24], P('tensor'), may hold values from -6.5 to -2.3
- skip_gain: float32 [24], P('tensor'), may hold values from 0.5 to 1.5
- norm_gain: bfloat16 [768], P('dp'), may hold values from 0.5 to 1.5
- gate_gain: float32 [1536], P('tensor'), may hold values from 0.5 to 1.5
Outputs:
- block_out: bfloat16 [2048, 8, 768], P('tensor', 'dp')
- hidden_grad: bfloat16 [2048, 8, 768], P('tensor', 'dp')
- zx_weight_grad: float32 [2, 768, 1536], P(None, 'dp', 'tensor')
- step_weight_grad: float32 [768, 24], P('dp', 'tensor')
- bc_weight_grad: float32 [768, 256], P('dp')
- conv_inner_grad: float32 [24, 256], P('tensor', 'dp')
- conv_shared_grad: float32 [1024], P('dp')
- out_weight_grad: float32 [1536, 768], P('tensor', 'dp')
- decay_log_grad: float32 [24], P('tensor')
- step_bias_grad: float32 [24], P('tensor')
- skip_gain_grad: float32 [24], P('tensor')
- norm_gain_grad: float32 [768], P('dp')
- gate_gain_grad: float32 [1536], P('tensor')
Inputs may be any that keep to these rules, and one draw needn't show every extreme that they name: `doc_lengths`: each row's 4 lengths add up to 2048; one document of each row, at a place drawn from the seed, is longer than 1536; in some row it is 2045 long and the others are 1 long.
All inputs are finite; a program needn't handle non-finite values.
Results may differ from a plain program's by a relative error of at most 0.013.
Values may be sent and summed in bfloat16 or wider, within the bound.
No kernel may reach another device: no remote copies, remote signals or barrier semaphores. Data moves between devices by JAX's collectives and lax.ppermute only.
A program may use at most 128 MiB of HBM per device.

v0:
```python
import jax
import jax.numpy as jnp
from jax import lax
from jax.sharding import PartitionSpec as P

INNER = 1536
CONV = 4
SPAN = 256


epsilon = 1e-05


def rounded(values):
    narrow = lax.optimization_barrier(values.astype(jnp.bfloat16)).astype(jnp.float32)
    return values + lax.stop_gradient(narrow - values)


def doc_ids(lengths, total_len):
    doc_ends = jnp.cumsum(lengths)[:-1]
    position = jnp.arange(total_len, dtype=jnp.int32)
    return jnp.sum((position[:, None] >= doc_ends[None, :]).astype(jnp.int32), axis=1)


def causal_conv(signal, tap_table, doc_row):
    tap_count = tap_table.shape[1]
    total = signal * tap_table[:, tap_count - 1]
    for offset in range(1, tap_count):
        shifted = jnp.pad(signal, ((offset, 0), (0, 0)))[:-offset]
        before = jnp.pad(doc_row, (offset, 0), constant_values=-1)[:-offset]
        total = (
            total
            + jnp.where((before == doc_row)[:, None], shifted, 0.0)
            * tap_table[:, tap_count - 1 - offset]
        )
    return total


def state_space(inner_seq, input_map, output_map, step_size, rates, skip_gain, doc_row):
    length, head_count, head_width = inner_seq.shape
    block_count = length // SPAN
    state_count = input_map.shape[1]
    blocks_x = inner_seq.reshape(block_count, SPAN, head_count, head_width)
    blocks_b = input_map.reshape(block_count, SPAN, state_count)
    blocks_c = output_map.reshape(block_count, SPAN, state_count)
    blocks_dt = step_size.reshape(block_count, SPAN, head_count)
    blocks_doc = doc_row.reshape(block_count, SPAN)
    cumulative = jnp.cumsum(-blocks_dt * rates, axis=1)
    scores = jnp.einsum(
        "cin,cjn->cij",
        blocks_c.astype(jnp.bfloat16),
        blocks_b.astype(jnp.bfloat16),
        preferred_element_type=jnp.float32,
    )
    position = jnp.arange(SPAN)
    visible = (position[None, :, None] >= position[None, None, :]) & (
        blocks_doc[:, :, None] == blocks_doc[:, None, :]
    )
    gaps = cumulative[:, :, None, :] - cumulative[:, None, :, :]
    decays = jnp.exp(jnp.where(visible[..., None], gaps, 0.0)) * visible[..., None]
    mixing = rounded(scores[..., None] * decays * blocks_dt[:, None, :, :])
    inside = jnp.einsum("cijh,cjhp->cihp", mixing, blocks_x, preferred_element_type=jnp.float32)
    final_cum = cumulative[:, -1, :]
    tail_doc = blocks_doc == blocks_doc[:, -1:]
    weight_in = jnp.exp(final_cum[:, None, :] - cumulative) * tail_doc[..., None] * blocks_dt
    scaled = rounded(blocks_x * weight_in[..., None])
    states = jnp.einsum("cjhp,cjn->chpn", scaled, blocks_b, preferred_element_type=jnp.float32)
    before = jnp.concatenate([jnp.full((1,), -1, jnp.int32), blocks_doc[:-1, -1]])
    carry_keep = blocks_doc[:, -1] == before

    def advance(running, packed):
        incoming, drop_log, survives = packed
        following = jnp.exp(drop_log)[:, None, None] * jnp.where(survives, running, 0.0) + incoming
        return (following, running)

    initial = jnp.zeros((head_count, head_width, state_count), jnp.float32)
    _, entering = lax.scan(advance, initial, (states, final_cum, carry_keep))
    head_keep = blocks_doc == before[:, None]
    outside = jnp.einsum(
        "chpn,cin->cihp", rounded(entering), blocks_c, preferred_element_type=jnp.float32
    )
    outside = outside * (jnp.exp(cumulative) * head_keep[..., None])[..., None]
    result = inside + outside + skip_gain[None, None, :, None] * blocks_x
    return result.reshape(length, head_count, head_width)


def mixer_row(
    gate_in,
    inner_in,
    step_in,
    shared_in,
    doc_row,
    taps_inner,
    taps_shared,
    decay_log,
    step_bias,
    skip_gain,
):
    head_count = step_in.shape[1]
    inner_act = jax.nn.silu(causal_conv(inner_in, taps_inner, doc_row))
    shared_act = jax.nn.silu(causal_conv(shared_in, taps_shared, doc_row))
    inner_seq = rounded(inner_act).reshape(inner_act.shape[0], head_count, -1)
    state_count = shared_act.shape[1] // 2
    input_map = rounded(shared_act[:, :state_count])
    output_map = rounded(shared_act[:, state_count:])
    step_size = jax.nn.softplus(step_in + step_bias)
    result = state_space(
        inner_seq, input_map, output_map, step_size, jnp.exp(decay_log), skip_gain, doc_row
    )
    return result.reshape(inner_act.shape) * jax.nn.silu(gate_in)


def per_device(
    hidden_rows,
    out_grad,
    doc_lengths,
    zx_weight,
    step_weight,
    bc_weight,
    conv_inner,
    conv_shared,
    out_weight,
    decay_log,
    step_bias,
    skip_gain,
    norm_gain,
    gate_gain,
):
    piece_len = hidden_rows.shape[0]
    full_len = piece_len * lax.axis_size("tensor")
    fetched = (
        lax.all_gather(zx_weight, "dp", axis=1, tiled=True),
        lax.all_gather(step_weight, "dp", axis=0, tiled=True),
        lax.all_gather(bc_weight, "dp", axis=0, tiled=True),
        lax.all_gather(conv_inner, "dp", axis=1, tiled=True),
        lax.all_gather(conv_shared, "dp", axis=0, tiled=True),
        lax.all_gather(out_weight, "dp", axis=1, tiled=True),
        lax.all_gather(norm_gain, "dp", axis=0, tiled=True),
    )
    zx_full, step_full, bc_full, inner_taps, shared_taps, out_full, gain_full = fetched
    residual = hidden_rows.astype(jnp.float32)
    gain = gain_full.astype(jnp.float32)
    row_scale = lax.rsqrt(jnp.mean(residual * residual, axis=2, keepdims=True) + epsilon)
    normed = (residual * row_scale * gain).astype(jnp.bfloat16)
    normed_all = lax.all_gather(normed, "tensor", axis=0, tiled=True)
    gate_in = jnp.einsum("srd,di->sri", normed_all, zx_full[0], preferred_element_type=jnp.float32)
    inner_in = jnp.einsum("srd,di->sri", normed_all, zx_full[1], preferred_element_type=jnp.float32)
    step_in = jnp.einsum("srd,dh->srh", normed_all, step_full, preferred_element_type=jnp.float32)
    shared_in = jnp.einsum("srd,dn->srn", normed_all, bc_full, preferred_element_type=jnp.float32)
    doc_table = jax.vmap(lambda lengths: doc_ids(lengths, full_len))(doc_lengths)
    taps_inner = inner_taps.astype(jnp.float32).reshape(-1, CONV)
    taps_shared = shared_taps.astype(jnp.float32).reshape(-1, CONV)

    def mixer(
        gate_val,
        inner_val,
        step_val,
        shared_val,
        inner_tab,
        shared_tab,
        decay_val,
        bias_val,
        skip_val,
    ):

        def one_row(gate_row, inner_row, step_row, shared_row, doc_row):
            return mixer_row(
                gate_row,
                inner_row,
                step_row,
                shared_row,
                doc_row,
                inner_tab,
                shared_tab,
                decay_val,
                bias_val,
                skip_val,
            )

        return jax.vmap(jax.checkpoint(one_row), in_axes=(1, 1, 1, 1, 0), out_axes=1)(
            gate_val, inner_val, step_val, shared_val, doc_table
        )

    mixed, mixer_back = jax.vjp(
        mixer,
        gate_in,
        inner_in,
        step_in,
        shared_in,
        taps_inner,
        taps_shared,
        decay_log,
        step_bias,
        skip_gain,
    )
    squares = lax.psum(jnp.sum(mixed * mixed, axis=2), "tensor")
    gate_scale = lax.rsqrt(squares / INNER + epsilon)[..., None]
    gated = (mixed * gate_scale * gate_gain).astype(jnp.bfloat16)
    branch = lax.psum_scatter(
        jnp.einsum("sri,id->srd", gated, out_full, preferred_element_type=jnp.float32).astype(
            jnp.bfloat16
        ),
        "tensor",
        scatter_dimension=0,
        tiled=True,
    ).astype(jnp.float32)
    block_out = (residual + branch).astype(jnp.bfloat16)
    grad_all = lax.all_gather(out_grad, "tensor", axis=0, tiled=True)
    gated_grad = jnp.einsum("srd,id->sri", grad_all, out_full, preferred_element_type=jnp.float32)
    out_weight_grad = jnp.einsum("sri,srd->id", gated, grad_all, preferred_element_type=jnp.float32)
    weighted = gated_grad * gate_gain
    gate_gain_grad = jnp.sum(gated_grad * mixed * gate_scale, axis=(0, 1))
    crossed = lax.psum(jnp.sum(weighted * mixed, axis=2), "tensor")
    mixed_grad = gate_scale * weighted - mixed * gate_scale**3 * crossed[..., None] / INNER
    (
        gate_grad,
        inner_grad,
        step_grad,
        shared_grad,
        taps_inner_grad,
        taps_shared_grad,
        decay_log_grad,
        step_bias_grad,
        skip_gain_grad,
    ) = mixer_back(mixed_grad)
    gate_narrow = gate_grad.astype(jnp.bfloat16)
    inner_narrow = inner_grad.astype(jnp.bfloat16)
    step_narrow = step_grad.astype(jnp.bfloat16)
    shared_narrow = shared_grad.astype(jnp.bfloat16)
    total = jnp.einsum("sri,di->srd", gate_narrow, zx_full[0], preferred_element_type=jnp.float32)
    total = total + jnp.einsum(
        "sri,di->srd", inner_narrow, zx_full[1], preferred_element_type=jnp.float32
    )
    total = total + jnp.einsum(
        "srh,dh->srd", step_narrow, step_full, preferred_element_type=jnp.float32
    )
    total = total + jnp.einsum(
        "srn,dn->srd", shared_narrow, bc_full, preferred_element_type=jnp.float32
    )
    normed_grad = lax.psum_scatter(
        total.astype(jnp.bfloat16), "tensor", scatter_dimension=0, tiled=True
    ).astype(jnp.float32)
    zx_weight_grad = jnp.stack(
        [
            jnp.einsum("srd,sri->di", normed_all, gate_narrow, preferred_element_type=jnp.float32),
            jnp.einsum("srd,sri->di", normed_all, inner_narrow, preferred_element_type=jnp.float32),
        ]
    )
    step_weight_grad = jnp.einsum(
        "srd,srh->dh", normed_all, step_narrow, preferred_element_type=jnp.float32
    )
    bc_weight_grad = jnp.einsum(
        "srd,srn->dn", normed_all, shared_narrow, preferred_element_type=jnp.float32
    )
    scaled_grad = normed_grad * gain
    norm_gain_grad = jnp.sum(normed_grad * residual * row_scale, axis=(0, 1))
    hidden_grad = row_scale * scaled_grad - residual * row_scale**3 * jnp.mean(
        scaled_grad * residual, axis=2, keepdims=True
    )
    hidden_grad = hidden_grad + out_grad.astype(jnp.float32)
    conv_inner_grad = taps_inner_grad.reshape(inner_taps.shape)
    conv_shared_grad = taps_shared_grad.reshape(-1)
    zx_part, step_part, bc_part, inner_part, shared_part, norm_part, out_weight_part = (
        lax.psum_scatter(zx_weight_grad, "dp", scatter_dimension=1, tiled=True),
        lax.psum_scatter(step_weight_grad, "dp", scatter_dimension=0, tiled=True),
        lax.psum_scatter(bc_weight_grad, "dp", scatter_dimension=0, tiled=True),
        lax.psum_scatter(conv_inner_grad, "dp", scatter_dimension=1, tiled=True),
        lax.psum_scatter(conv_shared_grad, "dp", scatter_dimension=0, tiled=True),
        lax.psum_scatter(norm_gain_grad, "dp", scatter_dimension=0, tiled=True),
        lax.psum_scatter(out_weight_grad, "dp", scatter_dimension=1, tiled=True),
    )
    bc_part, shared_part, norm_part = lax.psum((bc_part, shared_part, norm_part), "tensor")
    decay_log_grad, step_bias_grad, skip_gain_grad, gate_gain_grad = lax.psum(
        (decay_log_grad, step_bias_grad, skip_gain_grad, gate_gain_grad), "dp"
    )
    return (
        block_out,
        hidden_grad.astype(jnp.bfloat16),
        zx_part,
        step_part,
        bc_part,
        inner_part,
        shared_part,
        out_weight_part,
        decay_log_grad,
        step_bias_grad,
        skip_gain_grad,
        norm_part,
        gate_gain_grad,
    )


def solution(mesh):
    in_specs = (
        P("tensor", "dp", None),
        P("tensor", "dp", None),
        P("dp", None),
        P(None, "dp", "tensor"),
        P("dp", "tensor"),
        P("dp", None),
        P("tensor", "dp"),
        P("dp"),
        P("tensor", "dp"),
        P("tensor"),
        P("tensor"),
        P("tensor"),
        P("dp"),
        P("tensor"),
    )
    out_specs = (
        P("tensor", "dp", None),
        P("tensor", "dp", None),
        P(None, "dp", "tensor"),
        P("dp", "tensor"),
        P("dp", None),
        P("tensor", "dp"),
        P("dp"),
        P("tensor", "dp"),
        P("tensor"),
        P("tensor"),
        P("tensor"),
        P("dp"),
        P("tensor"),
    )
    return jax.shard_map(
        per_device, mesh=mesh, in_specs=in_specs, out_specs=out_specs, check_vma=False
    )
```

profile of v0, /device:TPU:0, one launch (start us, length us, event | category | flops | bytes accessed | tf_op | source)
XLA Modules:
  0.0 1094.9 jit_solution(710980090005897226)
XLA Ops:
  11.5 23.1 %all-reduce.35 = bf16[768]{0:T(1024)(128)(2,1)S(1)} all-reduce(bf16[768]{0:T(1024)(128)(2,1)S(1)} %dynamic-update-slice), channel_id=1, replica_groups=mesh['dp'=8,'tensor'=4] {'dp'}, use_global_device_ids=true, to_apply=%add.35 | all-reduce | flops 768 | bytes 3072
  41.0 16.2 %all-gather.1 = bf16[8,1,128]{2,1,0:T(2,128)(2,1)S(1)} all-gather(bf16[1,1,128]{2,1,0:T(2,128)(2,1)S(1)} %bitcast.878), channel_id=1, replica_groups=mesh['dp'=8,'tensor'=4] {'dp'}, dimensions={0}, use_global_device_ids=true | all-gather | bytes 2304 | tf_op jit(solution)/shard_map/all_gather | solution.py:136
  57.9 26.1 %all-gather.2 = bf16[8,96,6]{1,2,0:T(8,128)(2,1)S(1)} all-gather(bf16[1,96,6]{1,2,0:T(8,128)(2,1)S(1)} %bitcast.872), channel_id=1, replica_groups=mesh['dp'=8,'tensor'=4] {'dp'}, dimensions={0}, use_global_device_ids=true | all-gather | bytes 10368 | tf_op jit(solution)/shard_map/all_gather | solution.py:133
  84.6 26.1 %all-gather = bf16[8,32,6]{1,2,0:T(8,128)(2,1)S(1)} all-gather(bf16[1,32,6]{1,2,0:T(8,128)(2,1)S(1)} %bitcast.873), channel_id=1, replica_groups=mesh['dp'=8,'tensor'=4] {'dp'}, dimensions={0}, use_global_device_ids=true | all-gather | bytes 3456 | tf_op jit(solution)/shard_map/all_gather | solution.py:135
  113.2 33.2 %all_gather.31 = bf16[768,256]{1,0:T(8,128)(2,1)} all-gather(bf16[96,256]{1,0:T(8,128)(2,1)S(1)} %copy-done.100), channel_id=1, replica_groups=mesh['dp'=8,'tensor'=4] {'dp'}, dimensions={0}, use_global_device_ids=true | all-gather | bytes 442368 | tf_op jit(solution)/shard_map/all_gather | solution.py:134
  146.4 33.5 %all_gather.34 = bf16[384,768]{0,1:T(8,128)(2,1)} all-gather(bf16[384,96]{0,1:T(8,128)(2,1)S(1)} %copy-done.93), channel_id=1, replica_groups=mesh['dp'=8,'tensor'=4] {'dp'}, dimensions={1}, use_global_device_ids=true | all-gather | bytes 663552 | tf_op jit(solution)/shard_map/all_gather | solution.py:137
  183.1 3.6 compare_select_fusion.3
  188.0 7.2 reduce-window.20
  219.0 3.6 copy.456
  222.6 3.3 copy.555
  233.1 34.3 %while.55 = (s32[]{:T(128)}, f32[1,6,64,128]{3,2,1,0:T(8,128)S(1)}, f32[8,1,6,64,128]{4,3,2,1,0:T(8,128)}, f32[8,1,6]{2,1,0:T(1,128)}, pred[8,1]{0,1:T(4,128)(4,...) while((s32[]{:T(128)}, f32[1,6,64,128]{3,2,1,0:T(8,128)S(1)}, ...), condition=%wide.region_6.7_spmd.clone, body=%wide.region_5.6_spmd.clone.sunk | while | flops 245763 | bytes 983235 | solution.py:77
  273.4 5.4 fusion.17
  278.7 4.6 divide_multiply_fusion
  283.4 3.7 copy.476
  287.1 3.5 copy.559
  290.6 9.5 fusion.8
  307.7 3.5 copy.475
  311.2 5.7 psum.63
  317.1 9.7 multiply_reduce_fusion.1
  326.7 7.3 psum.64
  334.0 4.5 subtract_bitcast_fusion
  347.2 7.2 reduce-window.24
  371.5 3.4 fusion.141
  376.2 3.2 fusion.220
  379.4 4.2 multiply_reduce_fusion.2
  383.6 3.6 copy.478
  387.2 5.0 copy.561
  392.2 3.6 copy.499
  395.9 3.5 copy.565
  403.6 14.7 %fusion.23 = (f32[8,256,6]{1,2,0:T(8,128)}, f32[8,256,6]{1,2,0:T(8,128)}, f32[8,256,6]{1,2,0:T(8,128)}, bf16[8,256,256]{2,1,0:T(8,128)(2,1)S(1)}, bf16[1,8,256,256,6]{3,2,4,1,0:T(8,128)(2,1)}) fusion(f32[8,256,6]{1,2,0:T(8,128)S(1)} %copy.485, f32[8,256,256]{2,1,0:T(8,128)} %get-tuple-element.767, f32[8,256,6]{1,2,0:T(8,128)S(1)} %copy.483, ...), kind=kOutput, calls=%fused_computation.47 | convolution fusion | flops 455569408 | bytes 18595840 | tf_op jit(solution)/shard_map/transpose(jvp(vmap(jvp(vmap()))))/checkpoint/cijh,cjhp->cihp/dot_general | solution.py:62
  429.2 64.1 %while.56 = (s32[]{:T(128)}, f32[1,6,64,128]{3,2,1,0:T(8,128)S(1)}, f32[8,1,6,64,128]{4,3,2,1,0:T(8,128)}, f32[8,1,6]{2,1,0:T(1,128)}, f32[8,1,6,64,128]{4,3,2,1...) while((s32[]{:T(128)}, f32[1,6,64,128]{3,2,1,0:T(8,128)S(1)}, ...), condition=%wide.region_15.16_spmd.clone, body=%wide.region_14.15_spmd.clone.sunk | while | flops 294915 | bytes 1232083 | solution.py:77
  493.3 4.2 fusion.182
  497.6 25.2 %while.57 = (s32[]{:T(128)}, f32[1,6,64,128]{3,2,1,0:T(8,128)S(1)}, bf16[8,1,6,64,128]{4,3,2,1,0:T(8,128)(2,1)}, f32[8,1,6]{2,1,0:T(1,128)S(1)}, f32[8,1,6,64,12...) while((s32[]{:T(128)}, f32[1,6,64,128]{3,2,1,0:T(8,128)S(1)}, ...), condition=%wide.region_18.19_spmd.clone, body=%wide.region_16.18_spmd.clone.sunk | while | flops 344068 | bytes 1131804 | solution.py:77
  522.8 3.7 fusion.73
  526.5 9.7 bitcast_add_fusion.3
  536.2 3.4 copy.505
  539.6 4.6 reshape.4190
  544.2 4.6 reshape.4178
  552.3 5.7 multiply_reduce_fusion.6
  558.0 10.0 fusion.70
  568.0 3.5 copy.497
  571.5 4.6 reshape.4172
  576.1 3.5 copy.498
  581.3 15.5 %reduce-window.26 = f32[1,8,6,2,128]{4,1,2,3,0:T(8,128)S(1)} reduce-window(f32[1,8,6,2,128]{4,1,2,3,0:T(8,128)} %copy.523, f32[]{:T(128)} %constant.163.clone.1), window={size=1x1x1x1x128 pad=0_0x0_0x0_0x0_0x0_127}, to_apply=%region_25.26 | reduce-window | flops 1560576 | bytes 98308 | tf_op jit(solution)/shard_map/reduce-window.4
  599.6 5.2 fusion.205
  609.9 3.5 copy.506
  613.5 3.6 copy.531
  617.1 9.3 multiply_reduce_fusion.5
  626.5 6.2 multiply_select_fusion.1
  632.8 4.1 fusion.255
  646.7 5.0 multiply_select_fusion.2
  658.0 6.0 fusion.60
  671.8 5.5 fusion.104
  677.4 27.2 %reduce-scatter.18.cloned.1.call-done = f32[96,256]{1,0:T(8,128)} async-done(((f32[768,256]{1,0:T(8,128)}), f32[96,256]{1,0:T(8,128)}) %reduce-scatter.18.cloned.1.call-update) | async-done | bytes 98320 | tf_op jit(solution)/shard_map/reduce_scatter | solution.py:266
  704.7 5.8 fusion.78
  710.6 3.3 fusion.190
  719.3 48.6 %reduce-scatter.24.cloned.1.call-done = f32[32,6]{1,0:T(8,128)} async-done(((f32[256,6]{1,0:T(8,128)}), f32[32,6]{1,0:T(8,128)}) %reduce-scatter.24.cloned.1.call-update) | async-done | bytes 784
  769.4 63.1 %reduce-scatter.22.cloned.1.call-done = f32[96,6]{1,0:T(8,128)} async-done(((f32[768,6]{1,0:T(8,128)}), f32[96,6]{1,0:T(8,128)}) %reduce-scatter.22.cloned.1.call-update) | async-done | bytes 2320
  833.9 38.3 %reduce-scatter.14.cloned.1.call-done = bf16[512,1,768]{2,0,1:T(8,128)(2,1)} async-done(((bf16[2048,1,768]{2,0,1:T(8,128)(2,1)}), bf16[512,1,768]{2,0,1:T(8,128)(2,1)}) %reduce-scatter.14.cloned.1.call-update) | async-done | bytes 786448 | tf_op jit(solution)/shard_map/reduce_scatter | solution.py:240
  874.1 37.1 %all-reduce.38 = (f32[1024]{0:T(1024)S(1)}, f32[6]{0:T(128)}, f32[6]{0:T(128)}, f32[6]{0:T(128)}, f32[768]{0:T(1024)S(1)}, /*index=5*/f32[384]{0:T(512)}) all-reduce(f32[1024]{0:T(1024)S(1)} %reshape.4192, f32[6]{0:T(128)S(1)} %exponential_multiply_fusion, ...), channel_id=8, replica_groups=mesh['dp'=8,'tensor'=4] {'dp'}, use_global_device_ids=true, to_apply=%region_43.44.clone | all-reduce | flops 2194 | bytes 17552
  911.3 6.4 all-reduce.39
  920.9 25.5 %all-reduce.42.cloned.1.call-done = f32[96,256]{1,0:T(8,128)} async-done(((f32[96,256]{1,0:T(8,128)}), f32[96,256]{1,0:T(8,128)}) %all-reduce.42.cloned.1.call-update) | async-done | bytes 98320 | tf_op jit(solution)/shard_map/psum | solution.py:272
  946.4 67.9 %reduce-scatter.20.cloned.1.call-done = f32[384,96]{0,1:T(8,128)} async-done(((f32[384,768]{0,1:T(8,128)}), f32[384,96]{0,1:T(8,128)}) %reduce-scatter.20.cloned.1.call-update) | async-done | bytes 147472 | tf_op jit(solution)/shard_map/reduce_scatter | solution.py:270
  1014.4 72.3 %reduce-scatter.16.cloned.1.call-done = f32[2,96,384]{2,1,0:T(8,128)} async-done(((f32[2,768,384]{2,1,0:T(8,128)}), f32[2,96,384]{2,1,0:T(8,128)}) %reduce-scatter.16.cloned.1.call-update) | async-done | bytes 294928 | tf_op jit(solution)/shard_map/reduce_scatter | solution.py:264
  (608 shorter events, 277.8 us)
Async XLA Ops:
  7.2 31.9 %copy-start.150 = (s32[1,4]{1,0:T(1,128)S(1)}, s32[1,4]{1,0:T(1,128)}, u32[]{:S(2)}) copy-start(s32[1,4]{1,0:T(1,128)} %param.22) | copy-start | bytes 52
  7.2 33.8 %copy-start.151 = (f32[6]{0:T(128)S(1)}, f32[6]{0:T(128)}, u32[]{:S(2)}) copy-start(f32[6]{0:T(128)} %param.29) | copy-start | bytes 76
  7.2 33.8 %copy-start.149 = (bf16[128]{0:T(256)(128)(2,1)S(1)}, bf16[128]{0:T(256)(128)(2,1)}, u32[]{:S(2)}) copy-start(bf16[128]{0:T(256)(128)(2,1)} %param.27) | copy-start | bytes 772
  7.2 50.6 %copy-start.145 = (bf16[96,6]{0,1:T(8,128)(2,1)S(1)}, bf16[96,6]{0,1:T(8,128)(2,1)}, u32[]{:S(2)}) copy-start(bf16[96,6]{0,1:T(8,128)(2,1)} %param.24) | copy-start | bytes 3460
  7.2 77.4 %copy-start.146 = (bf16[6,32]{1,0:T(8,128)(2,1)S(1)}, bf16[6,32]{1,0:T(8,128)(2,1)}, u32[]{:S(2)}) copy-start(bf16[6,32]{1,0:T(8,128)(2,1)} %param.26) | copy-start | bytes 1156
  7.2 175.8 %all-gather.7.cloned.1.call-start = ((), (), s32[]{:S(2)}) async-start(), calls=%async_computation.7 | async-start | bytes 3932160 | tf_op jit(solution)/shard_map/all_gather | solution.py:145
  8.7 104.6 %copy-start.100 = (bf16[96,256]{1,0:T(8,128)(2,1)S(1)}, bf16[96,256]{1,0:T(8,128)(2,1)}, u32[]{:S(2)}) copy-start(bf16[96,256]{1,0:T(8,128)(2,1)} %param.25) | copy-start | bytes 147460
  34.6 23.2 %copy-start.98 = (f32[768]{0:T(1024)}, f32[768]{0:T(1024)S(1)}, u32[]{:S(2)}) copy-start(f32[768]{0:T(1024)S(1)} %convert_element_type.302) | copy-start | bytes 9220
  35.2 22.6 %copy-start.103 = (f32[512]{0:T(512)}, f32[512]{0:T(512)S(1)}, u32[]{:S(2)}) copy-start(f32[512]{0:T(512)S(1)} %get-tuple-element.775) | copy-start | bytes 6148
  35.2 111.2 %copy-start.93 = (bf16[384,96]{0,1:T(8,128)(2,1)S(1)}, bf16[384,96]{0,1:T(8,128)(2,1)}, u32[]{:S(2)}) copy-start(bf16[384,96]{0,1:T(8,128)(2,1)} %param.28) | copy-start | bytes 221188
  37.6 173.3 %all-gather.9.cloned.1.call-start = ((), (), s32[]{:S(2)}) async-start(), calls=%async_computation.8 | async-start | bytes 1327104 | tf_op jit(solution)/shard_map/all_gather | solution.py:132
  38.3 278.7 %all-gather.11.cloned.1.call-start = ((), (), s32[]{:S(2)}) async-start(), calls=%async_computation.10 | async-start | bytes 3932160 | tf_op jit(solution)/shard_map/all_gather | solution.py:208
  39.1 665.5 %reduce-scatter.18.cloned.1.call-start = ((), (), s32[]{:S(2)}) async-start(), calls=%async_computation.13 | async-start | bytes 884736 | tf_op jit(solution)/shard_map/reduce_scatter | solution.py:266
  39.8 142.0 %copy-start.75 = (pred[256,256]{1,0:T(8,128)(4,1)}, pred[256,256]{1,0:T(8,128)(4,1)S(1)}, u32[]{:S(2)}) copy-start(pred[256,256]{1,0:T(8,128)(4,1)S(1)} %iota_compare_fusion) | copy-start | bytes 196612
  39.9 143.2 %copy-start.101 = (f32[6]{0:T(128)S(1)}, f32[6]{0:T(128)}, u32[]{:S(2)}) copy-start(f32[6]{0:T(128)} %param.30) | copy-start | bytes 76
  112.2 70.9 %copy-start.23 = (f32[384,4]{1,0:T(8,128)}, f32[384,4]{1,0:T(8,128)S(1)}, u32[]{:S(2)}) copy-start(f32[384,4]{1,0:T(8,128)S(1)} %reshape.4195) | copy-start | bytes 18436
  183.1 21.6 %copy-start = (bf16[2048,1,768]{2,0,1:T(8,128)(2,1)S(1)}, bf16[2048,1,768]{2,0,1:T(8,128)(2,1)}, u32[]{:S(2)}) copy-start(bf16[2048,1,768]{2,0,1:T(8,128)(2,1)} %all-gather.7.cloned.1.call-done) | copy-start | bytes 9437188
  267.3 6.0 copy-start.40
  267.3 6.0 copy-start.57
  267.4 6.0 copy-start.68
  273.3 5.4 copy-start.42
  273.3 5.4 copy-start.69
  290.6 9.5 copy-start.18
  290.6 9.5 copy-start.43
  290.6 9.5 copy-start.45
  290.6 9.5 copy-start.142
  307.7 9.4 copy-start.129
  317.0 17.0 %copy-start.81 = (f32[2048,1]{0,1:T(1,128)}, f32[2048,1]{0,1:T(1,128)S(1)}, u32[]{:S(2)}) copy-start(f32[2048,1]{0,1:T(1,128)S(1)} %add_rsqrt_fusion) | copy-start | bytes 24580
  338.5 32.0 %copy-start.24 = (f32[384,4]{1,0:T(8,128)S(1)}, f32[384,4]{1,0:T(8,128)}, u32[]{:S(2)}) copy-start(f32[384,4]{1,0:T(8,128)} %copy-done.23) | copy-start | bytes 18436
  370.9 5.2 copy-start.106
  370.9 5.2 copy-start.108
  371.4 28.8 %copy-start.94 = (f32[8,256,6]{1,2,0:T(8,128)}, f32[8,256,6]{1,2,0:T(8,128)S(1)}, u32[]{:S(2)}) copy-start(f32[8,256,6]{1,2,0:T(8,128)S(1)} %copy.483) | copy-start | bytes 147460
  371.4 28.7 %copy-start.96 = (f32[8,256,6]{1,2,0:T(8,128)}, f32[8,256,6]{1,2,0:T(8,128)S(1)}, u32[]{:S(2)}) copy-start(f32[8,256,6]{1,2,0:T(8,128)S(1)} %copy.485) | copy-start | bytes 147460
  399.7 18.6 %copy-start.30 = (bf16[1,2048,128]{2,1,0:T(8,128)(2,1)}, bf16[1,2048,128]{2,1,0:T(8,128)(2,1)S(1)}, u32[]{:S(2)}) copy-start(bf16[1,2048,128]{2,1,0:T(8,128)(2,1)S(1)} %get-tuple-element.757) | copy-start | bytes 1572868
  399.7 23.9 %copy-start.31 = (bf16[1,2048,128]{2,1,0:T(8,128)(2,1)}, bf16[1,2048,128]{2,1,0:T(8,128)(2,1)S(1)}, u32[]{:S(2)}) copy-start(bf16[1,2048,128]{2,1,0:T(8,128)(2,1)S(1)} %get-tuple-element.756) | copy-start | bytes 1572868
  544.2 7.1 copy-start.47
  544.2 7.1 copy-start.65
  552.3 5.8 copy-start.2
  552.3 5.8 copy-start.74
  576.1 20.9 %copy-start.144 = (f32[6]{0:T(128)S(1)}, f32[6]{0:T(128)}, u32[]{:S(2)}) copy-start(f32[6]{0:T(128)} %exp.259) | copy-start | bytes 76
  617.0 9.4 copy-start.5
  617.1 9.4 copy-start.35
  617.1 9.4 copy-start.107
  617.1 9.4 copy-start.109
  617.1 9.4 copy-start.111
  617.1 9.4 copy-start.119
  626.5 6.3 copy-start.87
  645.6 122.4 %reduce-scatter.24.cloned.1.call-start = ((), (), s32[]{:S(2)}) async-start(), calls=%async_computation.17 | async-start | bytes 147456
  646.7 6.1 copy-start.33
  646.7 7.0 copy-start.34
  656.1 176.3 %reduce-scatter.22.cloned.1.call-start = ((), (), s32[]{:S(2)}) async-start(), calls=%async_computation.16 | async-start | bytes 442368
  658.0 214.2 %reduce-scatter.14.cloned.1.call-start = ((), (), s32[]{:S(2)}) async-start(), calls=%async_computation.11 | async-start | bytes 3932160 | tf_op jit(solution)/shard_map/reduce_scatter | solution.py:240
  658.0 6.0 copy-start.20
  658.0 6.0 copy-start.70
  671.1 246.6 %reduce-scatter.12.cloned.1.call-start = ((), (), s32[]{:S(2)}) async-start(), calls=%async_computation.9 | async-start | bytes 3932160 | tf_op jit(solution)/shard_map/reduce_scatter | solution.py:199
  677.3 269.1 %all-reduce.42.cloned.1.call-start = ((), (), s32[]{:S(2)}) async-start(), calls=%async_computation.14 | async-start | bytes 196608 | tf_op jit(solution)/shard_map/psum | solution.py:272
  704.6 309.8 %reduce-scatter.20.cloned.1.call-start = ((), (), s32[]{:S(2)}) async-start(), calls=%async_computation.15 | async-start | bytes 1327104 | tf_op jit(solution)/shard_map/reduce_scatter | solution.py:270
  710.5 376.1 %reduce-scatter.16.cloned.1.call-start = ((), (), s32[]{:S(2)}) async-start(), calls=%async_computation.12 | async-start | bytes 2654208 | tf_op jit(solution)/shard_map/reduce_scatter | solution.py:264
  715.8 156.4 %copy-start.36 = (bf16[512,1,768]{2,0,1:T(8,128)(2,1)S(1)}, bf16[512,1,768]{2,0,1:T(8,128)(2,1)}, u32[]{:S(2)}) copy-start(bf16[512,1,768]{2,0,1:T(8,128)(2,1)} %param.20) | copy-start | bytes 2359300
  715.8 156.4 %copy-start.99 = (f32[768]{0:T(1024)S(1)}, f32[768]{0:T(1024)}, u32[]{:S(2)}) copy-start(f32[768]{0:T(1024)} %copy-done.98) | copy-start | bytes 9220
  715.8 156.4 %copy-start.104 = (f32[512]{0:T(512)S(1)}, f32[512]{0:T(512)}, u32[]{:S(2)}) copy-start(f32[512]{0:T(512)} %copy-done.103) | copy-start | bytes 6148
  717.5 156.6 %copy-start.148 = (f32[384]{0:T(512)S(1)}, f32[384]{0:T(512)}, u32[]{:S(2)}) copy-start(f32[384]{0:T(512)} %get-tuple-element.632) | copy-start | bytes 4612
  717.5 200.3 %copy-start.55 = (bf16[512,1,768]{2,0,1:T(8,128)(2,1)S(1)}, bf16[512,1,768]{2,0,1:T(8,128)(2,1)}, u32[]{:S(2)}) copy-start(bf16[512,1,768]{2,0,1:T(8,128)(2,1)} %param.21) | copy-start | bytes 2359300
  717.5 200.3 %copy-start.135 = (f32[512]{0:T(512)S(1)}, f32[512]{0:T(512)}, u32[]{:S(2)}) copy-start(f32[512]{0:T(512)} %get-tuple-element.774) | copy-start | bytes 6148
  (102 other events, 322.8 us)
Sparse Core Ops, SparseCore 0:
  37.7 25.9 all-gather.6
  65.8 41.3 all-gather.8
  108.8 27.3 all-gather.10
  645.7 58.8 reduce-scatter.17
  708.1 59.8 reduce-scatter.23
  772.0 60.3 reduce-scatter.21
  835.1 36.9 reduce-scatter.13
  874.7 37.9 reduce-scatter.11
  915.1 31.2 all-reduce.41
  950.3 64.0 reduce-scatter.19
  1018.5 68.1 reduce-scatter.15
where the time goes:
time: 1100 us; the launch traced here: 1090 us
  waiting for transfers between devices  344 us (31%)
  blocking collectives  215 us (20%)
  other arithmetic  200 us (18%)
  local copies, waits for them, and re-layouts  187 us (17%)
  matrix products  130 us (12%)
  between operations  18.1 us (2%)
    unnamed x13, waiting for transfers between devices  113 us
    reduce_scatter x1, waiting for transfers between devices, per_device(): lax.psum_scatter(zx_weight_grad, 'dp', scatter_dimension=1, tiled=True)  72.3 us
    reduce_scatter x1, waiting for transfers between devices, per_device(): lax.psum_scatter(out_weight_grad, 'dp', scatter_dimension=1, tiled=True)  67.9 us
    unnamed x2, blocking collectives  60.2 us
    dot_general x4, matrix products, state_space(): jnp.einsum('cijh,cjhp->cihp', mixing, blocks_x, preferred_element_type=jn...  43.9 us
    unnamed x328, local copies, waits for them, and re-layouts  42.8 us
    reduce_scatter x1, waiting for transfers between devices, per_device(): lax.psum_scatter(total.astype(jnp.bfloat16), 'tensor', scatter_dimension=...  38.3 us
    another operation x9, other arithmetic  33.7 us
  transfers between devices with their start and end apart: 11, of which 7 were waited for; matrix products, arithmetic and copies ran while one was open for 17% of the time, Pallas kernels for 0%

commit v1 on v0

v1 whole, which is shorter than its diff:
```python
import functools

import jax
import jax.numpy as jnp
from jax import lax
from jax.experimental import pallas as pl
from jax.experimental.pallas import tpu as pltpu
from jax.sharding import PartitionSpec as P

CONV = 4
SPAN = 256
LANES = 128
epsilon = 1e-05
bf16 = jnp.bfloat16
f32 = jnp.float32
NN = (((1,), (0,)), ((), ()))
NT = (((1,), (1,)), ((), ()))
TN = (((0,), (0,)), ((), ()))


def mm(left, right, dims=NN):
    return lax.dot_general(left, right, dims, preferred_element_type=f32)


def split(values, parts):
    pieces = []
    for _ in range(parts):
        piece = values.astype(bf16)
        pieces.append(piece)
        values = values - piece.astype(f32)
    return pieces


def mm_left_exact(left, right, parts):
    return sum(mm(left, piece) for piece in split(right, parts))


def mm_right_exact(left, right, parts):
    return sum(mm(piece, right) for piece in split(left, parts))


def sigmoid(values):
    return 1.0 / (1.0 + jnp.exp(-values))


def softplus(values):
    return jnp.maximum(values, 0.0) + jnp.log1p(jnp.exp(-jnp.abs(values)))


def doc_start(position, ends):
    start = jnp.zeros_like(position)
    for end in ends:
        start = jnp.where(position >= end, end, start)
    return start


def scalar_start(position, ends):
    start = jnp.int32(0)
    for end in ends:
        start = jnp.where(position >= end, end, start)
    return start


def iota(shape, dim):
    return lax.broadcasted_iota(jnp.int32, shape, dim)


def conv_block(ext_ref, taps_ref, position, start, width):
    masks = [None] + [(position - k >= start).astype(f32) for k in range(1, CONV)]
    groups = []
    for at in range(0, width, LANES):
        cols = slice(at, at + LANES)
        total = ext_ref[8 : 8 + SPAN, cols] * taps_ref[CONV - 1 : CONV, cols]
        for k in range(1, CONV):
            total = total + ext_ref[8 - k : 8 - k + SPAN, cols] * masks[k] * (
                taps_ref[CONV - 1 - k : CONV - k, cols]
            )
        groups.append(total)
    return jnp.concatenate(groups, axis=1)


def wide(mask, width):
    return jnp.concatenate([mask] * (width // LANES), axis=1)


def forward_kernel(
    inner,
    state_count,
    heads,
    info_ref,
    hidden_ref,
    weight_ref,
    taps_ref,
    chan_ref,
    head_ref,
    gain_ref,
    expand_ref,
    normed_ref,
    pre_ref,
    y_ref,
    mixed_ref,
    cum_ref,
    entering_ref,
    ext_ref,
    state_ref,
):
    block = pl.program_id(0)
    conv_width = inner + 2 * state_count
    step_at = inner + conv_width
    ends = [info_ref[k] for k in range(3)]
    base = block * SPAN

    @pl.when(block == 0)
    def _():
        ext_ref[...] = jnp.zeros_like(ext_ref)
        state_ref[...] = jnp.zeros_like(state_ref)

    residual = hidden_ref[0].astype(f32)
    row_scale = lax.rsqrt(jnp.mean(residual * residual, axis=1, keepdims=True) + epsilon)
    normed = (residual * row_scale * gain_ref[0:1, :]).astype(bf16)
    normed_ref[...] = normed
    pre = mm(normed, weight_ref[...])
    pre_ref[...] = pre

    ext_ref[0:8, :] = ext_ref[SPAN : SPAN + 8, :]
    ext_ref[8 : 8 + SPAN, :] = pre[:, inner:step_at]
    position = base + iota((SPAN, LANES), 0)
    start = doc_start(position, ends)
    conv = conv_block(ext_ref, taps_ref, position, start, conv_width)
    active = conv * sigmoid(conv)
    x_val = active[:, :inner].astype(bf16).astype(f32)
    in_map = active[:, inner : inner + state_count].astype(bf16)
    out_map = active[:, inner + state_count :].astype(bf16)

    step_size = softplus(pre[:, step_at:] + head_ref[1:2, :])
    log_decay = step_size * head_ref[0:1, :]
    row_at = iota((SPAN, SPAN), 0)
    col_at = iota((SPAN, SPAN), 1)
    lower = (col_at <= row_at).astype(f32).astype(bf16)
    cum = mm_left_exact(lower, log_decay, 3)
    cum_ref[...] = cum
    cum_rows = cum.T

    start_last = scalar_start(base + SPAN - 1, ends)
    keep = (start < base).astype(f32)
    tail = (position >= start_last).astype(f32)
    survives = (start_last < base).astype(f32)
    expand = expand_ref[...]
    step_wide = mm_right_exact(step_size, expand, 2)
    decay_wide = mm_right_exact(jnp.exp(cum), expand, 2)
    into_wide = mm_right_exact(jnp.exp(cum[SPAN - 1 :, :] - cum) * tail, expand, 2)

    x_step = x_val * step_wide
    x_step_low = x_step.astype(bf16)
    state = state_ref[...]
    entering_ref[...] = state
    outside = mm(out_map, state.astype(bf16)) * (decay_wide * wide(keep, inner))
    visible = (col_at <= row_at) & (base + col_at >= wide(start, SPAN))
    scores = jnp.where(visible, mm(out_map, in_map, NT), 0.0)
    upper_half = iota((SPAN, LANES), 1) >= LANES // 2
    inside = []
    for pair in range(heads // 2):
        x_pair = x_step_low[:, pair * LANES : (pair + 1) * LANES]
        total = None
        for which in range(2):
            head = 2 * pair + which
            gap = cum[:, head : head + 1] - cum_rows[head : head + 1, :]
            mixing = (scores * jnp.exp(jnp.minimum(gap, 0.0))).astype(bf16)
            chosen = upper_half if which else jnp.logical_not(upper_half)
            part = mm(mixing, jnp.where(chosen, x_pair, jnp.zeros_like(x_pair)))
            total = part if total is None else total + part
        inside.append(total)
    y_val = jnp.concatenate(inside, axis=1) + outside + chan_ref[0:1, :] * x_val
    y_ref[...] = y_val
    gate = pre[:, :inner]
    mixed_ref[...] = y_val * (gate * sigmoid(gate))

    scaled = (x_step * into_wide).astype(bf16)
    state_ref[...] = (decay_wide[SPAN - 1 :, :] * survives) * state + mm(in_map, scaled, TN)


def branch_kernel(mixed_ref, grad_ref, out_ref, chan_ref, branch_ref, stats_ref):
    mixed = mixed_ref[...]
    out_w = out_ref[...]
    gain = chan_ref[1:2, :]
    branch_ref[0] = mm((mixed * gain).astype(bf16), out_w, NT).astype(bf16)
    weighted = mm(grad_ref[0], out_w) * gain
    squares = jnp.sum(mixed * mixed, axis=1, keepdims=True)
    crossed = jnp.sum(weighted * mixed, axis=1, keepdims=True)
    lane = iota((SPAN, LANES), 1)
    both = jnp.where(lane == 0, squares, jnp.where(lane == 1, crossed, 0.0))
    stats_ref[...] = both.T[0:8, :]


def backward_kernel(
    inner,
    state_count,
    heads,
    inner_total,
    info_ref,
    stats_ref,
    grad_ref,
    normed_ref,
    weight_ref,
    out_ref,
    pre_ref,
    halo_ref,
    y_ref,
    cum_ref,
    entering_ref,
    taps_ref,
    chan_ref,
    head_ref,
    gain_ref,
    expand_ref,
    gather_ref,
    total_ref,
    wide_grad_ref,
    small_ref,
    ext_ref,
    next_ref,
    state_grad_ref,
    weight_acc,
    out_acc,
    pre_grad_ref,
):
    step = pl.program_id(0)
    blocks = pl.num_programs(0)
    block = blocks - 1 - step
    base = block * SPAN
    conv_width = inner + 2 * state_count
    step_at = inner + conv_width
    ends = [info_ref[k] for k in range(3)]

    @pl.when(step == 0)
    def _():
        next_ref[...] = jnp.zeros_like(next_ref)
        state_grad_ref[...] = jnp.zeros_like(state_grad_ref)
        weight_acc[...] = jnp.zeros_like(weight_acc)
        out_acc[...] = jnp.zeros_like(out_acc)
        small_ref[...] = jnp.zeros_like(small_ref)

    stats = stats_ref[...].T
    gate_scale = lax.rsqrt(stats[:, 0:1] / inner_total + epsilon)
    crossed = stats[:, 1:2] / inner_total
    gate = pre_ref[:, :inner]
    gate_sig = sigmoid(gate)
    gate_act = gate * gate_sig
    y_val = y_ref[...]
    mixed = y_val * gate_act
    grad = grad_ref[0]
    gain = chan_ref[1:2, :]
    skip = chan_ref[0:1, :]
    gated_grad = mm(grad, out_ref[...])
    scaled_mixed = mixed * gate_scale
    out_acc[...] += mm(grad, (scaled_mixed * gain).astype(bf16), TN)
    gain_grad = jnp.sum(gated_grad * scaled_mixed, axis=0, keepdims=True)
    mixed_grad = gate_scale * (gated_grad * gain) - scaled_mixed * (
        gate_scale * gate_scale * crossed
    )
    gate_grad = mixed_grad * y_val * (gate_sig * (1.0 + gate * (1.0 - gate_sig)))
    pre_grad_ref[:, :inner] = gate_grad.astype(bf16)
    y_grad = mixed_grad * gate_act

    ext_ref[0:8, :] = halo_ref[:, inner:step_at]
    ext_ref[8 : 8 + SPAN, :] = pre_ref[:, inner:step_at]
    position = base + iota((SPAN, LANES), 0)
    start = doc_start(position, ends)
    conv = conv_block(ext_ref, taps_ref, position, start, conv_width)
    conv_sig = sigmoid(conv)
    active = conv * conv_sig
    act_slope = conv_sig * (1.0 + conv * (1.0 - conv_sig))
    x_val = active[:, :inner].astype(bf16).astype(f32)
    in_map = active[:, inner : inner + state_count].astype(bf16)
    out_map = active[:, inner + state_count :].astype(bf16)

    step_pre = pre_ref[:, step_at:] + head_ref[1:2, :]
    step_size = softplus(step_pre)
    rates = head_ref[0:1, :]
    cum = cum_ref[...]
    cum_rows = cum.T
    start_last = scalar_start(base + SPAN - 1, ends)
    keep = (start < base).astype(f32)
    tail = (position >= start_last).astype(f32)
    survives = (start_last < base).astype(f32)
    expand = expand_ref[...]
    step_wide = mm_right_exact(step_size, expand, 2)
    decay_wide = mm_right_exact(jnp.exp(cum), expand, 2)
    into_wide = mm_right_exact(jnp.exp(cum[SPAN - 1 :, :] - cum) * tail, expand, 2)
    keep_decay = decay_wide * wide(keep, inner)
    last_decay = decay_wide[SPAN - 1 :, :] * survives

    x_step = x_val * step_wide
    x_step_low = x_step.astype(bf16)
    scaled = (x_step * into_wide).astype(bf16)
    entering = entering_ref[...]
    entering_low = entering.astype(bf16)
    y_grad_low = y_grad.astype(bf16)
    state_grad = state_grad_ref[...]
    state_grad_low = state_grad.astype(bf16)

    outside = mm(out_map, entering_low)
    outside_grad = (y_grad * keep_decay).astype(bf16)
    scaled_grad = mm(in_map, state_grad_low)
    out_map_grad = mm(outside_grad, entering_low, NT)
    in_map_grad = mm(scaled, state_grad_low, NT)
    state_grad_ref[...] = last_decay * state_grad + mm(out_map, outside_grad, TN)

    row_at = iota((SPAN, SPAN), 0)
    col_at = iota((SPAN, SPAN), 1)
    col_start = doc_start(base + col_at, ends)
    visible = (row_at <= col_at) & (base + row_at >= col_start)
    scores = jnp.where(visible, mm(in_map, out_map, NT), 0.0)
    upper_half = iota((SPAN, LANES), 1) >= LANES // 2
    score_grad = jnp.zeros((SPAN, SPAN), f32)
    x_step_grads = []
    for pair in range(heads // 2):
        x_pair = x_step_low[:, pair * LANES : (pair + 1) * LANES]
        grad_pair = y_grad_low[:, pair * LANES : (pair + 1) * LANES]
        total = None
        for which in range(2):
            head = 2 * pair + which
            chosen = upper_half if which else jnp.logical_not(upper_half)
            grad_head = jnp.where(chosen, grad_pair, jnp.zeros_like(grad_pair))
            gap = cum_rows[head : head + 1, :] - cum[:, head : head + 1]
            decays = jnp.exp(jnp.minimum(gap, 0.0))
            score_grad = score_grad + mm(x_pair, grad_head, NT) * decays
            part = mm((scores * decays).astype(bf16), grad_head)
            total = part if total is None else total + part
        x_step_grads.append(total)
    x_step_grad = jnp.concatenate(x_step_grads, axis=1)
    score_grad = jnp.where(visible, score_grad, 0.0).astype(bf16)
    in_map_grad = in_map_grad + mm(score_grad, out_map)
    out_map_grad = out_map_grad + mm(score_grad, in_map, TN)

    inside = y_val - skip * x_val - keep_decay * outside
    into_terms = scaled.astype(f32) * scaled_grad
    cum_terms = (
        y_grad_low.astype(f32) * inside
        + outside_grad.astype(f32) * outside
        - x_step_low.astype(f32) * x_step_grad
        - into_terms
    )
    last_terms = jnp.sum(into_terms, axis=0, keepdims=True) + last_decay * jnp.sum(
        state_grad * entering, axis=0, keepdims=True
    )
    last_row = iota((SPAN, inner), 0) == SPAN - 1
    cum_terms = cum_terms + jnp.where(last_row, last_terms, 0.0)
    x_step_grad = x_step_grad + into_wide * scaled_grad
    gather = gather_ref[...]
    cum_grad = mm_right_exact(cum_terms, gather, 2)
    step_grad = mm_right_exact(x_val * x_step_grad, gather, 2)
    upper = (row_at <= col_at).astype(f32).astype(bf16)
    log_grad = mm_left_exact(upper, cum_grad, 3)
    step_grad = (step_grad + log_grad * rates) * sigmoid(step_pre)
    pre_grad_ref[:, step_at:] = step_grad.astype(bf16)
    x_grad = skip * y_grad + step_wide * x_step_grad

    small_ref[4:5, :inner] += jnp.sum(y_grad * x_val, axis=0, keepdims=True)
    small_ref[5:6, :inner] += gain_grad
    small_ref[6:7, :LANES] += jnp.sum(step_size * rates * log_grad, axis=0, keepdims=True)
    small_ref[7:8, :LANES] += jnp.sum(step_grad, axis=0, keepdims=True)

    conv_grad = jnp.concatenate([x_grad, in_map_grad, out_map_grad], axis=1) * act_slope
    next_ref[SPAN : SPAN + 8, :] = next_ref[0:8, :]
    next_ref[0:SPAN, :] = conv_grad
    back = [None] + [(position - k >= start).astype(f32) for k in range(1, CONV)]
    ahead = [None] + [
        (position >= doc_start(position + k, ends)).astype(f32) for k in range(1, CONV)
    ]
    for at in range(0, conv_width, LANES):
        cols = slice(at, at + LANES)
        grad_here = next_ref[0:SPAN, cols]
        total = grad_here * taps_ref[CONV - 1 : CONV, cols]
        small_ref[CONV - 1 : CONV, cols] += jnp.sum(
            grad_here * ext_ref[8 : 8 + SPAN, cols], axis=0, keepdims=True
        )
        for k in range(1, CONV):
            total = total + next_ref[k : k + SPAN, cols] * ahead[k] * (
                taps_ref[CONV - 1 - k : CONV - k, cols]
            )
            small_ref[CONV - 1 - k : CONV - k, cols] += jnp.sum(
                grad_here * back[k] * ext_ref[8 - k : 8 - k + SPAN, cols], axis=0, keepdims=True
            )
        pre_grad_ref[:, inner + at : inner + at + LANES] = total.astype(bf16)

    pre_grads = pre_grad_ref[...]
    total_ref[0] = mm(pre_grads, weight_ref[...], NT).astype(bf16)
    weight_acc[...] += mm(normed_ref[...], pre_grads, TN)

    @pl.when(step == blocks - 1)
    def _():
        span = weight_acc.shape[1]
        wide_grad_ref[:, :span] = weight_acc[...].astype(bf16)
        wide_grad_ref[:, span:] = out_acc[...].astype(bf16)
        products = weight_acc[...] * weight_ref[...].astype(f32)
        ones = jnp.ones((8, span), bf16)
        sums = sum(mm(ones, piece, NT) for piece in split(products, 3))
        width = gain_ref.shape[1]
        small_ref[0:1, conv_width : conv_width + width] = sums[0:1, :] / gain_ref[0:1, :]


def swap(values, axis, bit):
    size = lax.axis_size(axis)
    return lax.ppermute(values, axis, [(i, i ^ bit) for i in range(size)])


def bits_of(size):
    return [1 << k for k in range(size.bit_length() - 1)]


def sum_over(values, axis):
    for bit in bits_of(lax.axis_size(axis)):
        values = values + swap(values, axis, bit)
    return values


def gather_relative(values, axis):
    pieces = {0: values}
    for bit in reversed(bits_of(lax.axis_size(axis))):
        pieces.update({k | bit: swap(piece, axis, bit) for k, piece in list(pieces.items())})
    return jnp.stack([pieces[k] for k in range(len(pieces))])


def scatter_relative(pieces, axis):
    kept = [pieces[k] for k in range(pieces.shape[0])]
    for bit in bits_of(lax.axis_size(axis)):
        half = range(0, len(kept), 2)
        kept = [
            kept[k].astype(f32) + swap(kept[k + 1], axis, bit).astype(f32) for k in reversed(half)
        ][::-1]
        if len(kept) > 1:
            kept = [piece.astype(bf16) for piece in kept]
    return kept[0]


def line_gather(values, axis):
    size = lax.axis_size(axis)
    length = size // 2
    place = lax.axis_index(axis)
    at, side = place // 2, place % 2
    ahead, behind = [values], [values]
    for s in range(1, length):
        ahead.append(
            lax.ppermute(ahead[-1], axis, [(i, i + 2) for i in range(size - 2) if i // 2 >= s - 1])
        )
        behind.append(
            lax.ppermute(
                behind[-1], axis, [(i + 2, i) for i in range(size - 2) if i // 2 < length - s]
            )
        )
    result = jnp.zeros((length, 2) + values.shape, values.dtype)
    for s in range(length):
        if s == 0:
            piece, other = values, swap(values, axis, 1)
        else:
            over = lambda v, ok: lax.ppermute(
                v, axis, [(i, i ^ 1) for i in range(size) if ok(i // 2)]
            )
            piece = jnp.where(at >= s, ahead[s], behind[length - s])
            other = jnp.where(
                at >= s,
                over(ahead[s], lambda h: h >= s),
                over(behind[length - s], lambda h: h < s),
            )
        slot = lax.rem(at - s + length, length)
        for block, row in ((piece, side), (other, 1 - side)):
            result = lax.dynamic_update_slice(
                result, block[None, None], (slot, row) + (0,) * values.ndim
            )
    return result.reshape((size,) + values.shape)


def line_scatter(pieces, axis):
    size = lax.axis_size(axis)
    length = size // 2
    place = lax.axis_index(axis)
    at, side = place // 2, place % 2
    pieces = pieces.reshape((length, 2) + pieces.shape[1:])
    mine = lax.dynamic_index_in_dim(pieces, side, 1, keepdims=False)
    theirs = lax.dynamic_index_in_dim(pieces, 1 - side, 1, keepdims=False)
    folded = (mine.astype(f32) + swap(theirs, axis, 1).astype(f32)).astype(bf16)
    own = lambda where: lax.dynamic_index_in_dim(
        folded, jnp.clip(where, 0, length - 1), 0, keepdims=False
    ).astype(f32)
    ahead = behind = None
    for s in range(1, length):
        right = own(at + length - s)
        left = own(at - length + s)
        if s > 1:
            right = right + ahead.astype(f32)
            left = left + behind.astype(f32)
        ahead = lax.ppermute(
            right.astype(bf16), axis, [(i, i + 2) for i in range(size - 2) if i // 2 < s]
        )
        behind = lax.ppermute(
            left.astype(bf16), axis, [(i + 2, i) for i in range(size - 2) if i // 2 + 1 >= length - s]
        )
    result = own(at)
    if length > 1:
        result = result + ahead.astype(f32) + behind.astype(f32)
    return result


def per_device(
    hidden_rows,
    out_grad,
    doc_lengths,
    zx_weight,
    step_weight,
    bc_weight,
    conv_inner,
    conv_shared,
    out_weight,
    decay_log,
    step_bias,
    skip_gain,
    norm_gain,
    gate_gain,
):
    piece_len, _, width = hidden_rows.shape
    tensor = lax.axis_size("tensor")
    data = lax.axis_size("dp")
    full_len = piece_len * tensor
    blocks = full_len // SPAN
    per_piece = piece_len // SPAN
    share = zx_weight.shape[1]
    inner = zx_weight.shape[2]
    heads = step_weight.shape[1]
    head_dim = inner // heads
    state_count = bc_weight.shape[1] // 2
    conv_width = inner + 2 * state_count
    step_at = inner + conv_width
    span = step_at + LANES
    inner_total = float(inner * tensor)
    mine = lax.axis_index("tensor")

    hidden = hidden_rows[:, 0, :]
    grad_local = out_grad[:, 0, :]
    hidden_all = gather_relative(hidden, "tensor")
    shard = jnp.concatenate(
        [
            zx_weight[0],
            zx_weight[1],
            bc_weight,
            jnp.pad(step_weight, ((0, 0), (0, LANES - heads))),
            out_weight.T,
        ],
        axis=1,
    )
    params = jnp.concatenate([norm_gain, conv_inner.reshape(-1), conv_shared])[None, :]
    params_all = line_gather(params, "dp").reshape(data, -1).astype(f32)
    weights = line_gather(shard, "dp").reshape(width, -1)
    weight_in = weights[:, :span]
    weight_out = weights[:, span:]
    grad_all = gather_relative(grad_local, "tensor")

    gain_row = params_all[:, :share].reshape(1, width)
    inner_size = conv_inner.size
    taps_inner = (
        params_all[:, share : share + inner_size]
        .reshape(data, heads, -1)
        .transpose(1, 0, 2)
        .reshape(inner, CONV)
    )
    taps_shared = params_all[:, share + inner_size :].reshape(2 * state_count, CONV)
    taps = jnp.pad(jnp.concatenate([taps_inner, taps_shared]).T, ((0, 4), (0, 0)))
    chan = jnp.pad(
        jnp.stack([jnp.repeat(skip_gain, head_dim), gate_gain]), ((0, 6), (0, 0))
    )
    head_rows = jnp.pad(
        jnp.stack([-jnp.exp(decay_log), step_bias]), ((0, 6), (0, LANES - heads))
    )
    gain_rows = jnp.broadcast_to(gain_row, (8, width))
    expand = (
        jnp.arange(LANES)[:, None] == jnp.arange(inner)[None, :] // head_dim
    ).astype(bf16)
    gather = expand.T
    ends = jnp.cumsum(doc_lengths[0].astype(jnp.int32))[:3]
    info = jnp.concatenate([ends, mine[None].astype(jnp.int32)])

    fixed = lambda shape: pl.BlockSpec(shape, lambda i, info: (0,) * len(shape))
    limits = pltpu.CompilerParams(
        dimension_semantics=("arbitrary",), vmem_limit_bytes=56 * 1024 * 1024
    )
    piece_spec = pl.BlockSpec(
        (1, SPAN, width),
        lambda i, info: ((i // per_piece) ^ info[3], i % per_piece, 0),
    )
    rows = lambda cols: pl.BlockSpec((SPAN, cols), lambda i, info: (i, 0))
    shaped = jax.ShapeDtypeStruct
    normed, pre, y_val, mixed, cum, entering = pl.pallas_call(
        functools.partial(forward_kernel, inner, state_count, heads),
        grid_spec=pltpu.PrefetchScalarGridSpec(
            num_scalar_prefetch=1,
            grid=(blocks,),
            in_specs=[
                piece_spec,
                fixed((width, span)),
                fixed(taps.shape),
                fixed(chan.shape),
                fixed(head_rows.shape),
                fixed(gain_rows.shape),
                fixed(expand.shape),
            ],
            out_specs=[
                rows(width),
                rows(span),
                rows(inner),
                rows(inner),
                rows(LANES),
                pl.BlockSpec((state_count, inner), lambda i, info: (i, 0)),
            ],
            scratch_shapes=[
                pltpu.VMEM((SPAN + 8, conv_width), f32),
                pltpu.VMEM((state_count, inner), f32),
            ],
        ),
        out_shape=[
            shaped((full_len, width), bf16),
            shaped((full_len, span), f32),
            shaped((full_len, inner), f32),
            shaped((full_len, inner), f32),
            shaped((full_len, LANES), f32),
            shaped((blocks * state_count, inner), f32),
        ],
        compiler_params=limits,
        name="forward",
    )(info, hidden_all, weight_in, taps, chan, head_rows, gain_rows, expand)

    branch, stats = pl.pallas_call(
        lambda info_ref, *refs: branch_kernel(*refs),
        grid_spec=pltpu.PrefetchScalarGridSpec(
            num_scalar_prefetch=1,
            grid=(blocks,),
            in_specs=[rows(inner), piece_spec, fixed((width, inner)), fixed(chan.shape)],
            out_specs=[piece_spec, pl.BlockSpec((8, SPAN), lambda i, info: (0, i))],
        ),
        out_shape=[
            shaped((tensor, piece_len, width), bf16),
            shaped((8, full_len), f32),
        ],
        compiler_params=limits,
        name="branch",
    )(info, mixed, grad_all, weight_out, chan)

    stats = sum_over(stats, "tensor")
    branch_local = scatter_relative(branch, "tensor")
    gate_scale = lax.rsqrt(
        lax.dynamic_slice_in_dim(stats[0], mine * piece_len, piece_len) / inner_total + epsilon
    )
    residual = hidden.astype(f32)
    block_out = (residual + branch_local * gate_scale[:, None]).astype(bf16)

    back = lambda i: blocks - 1 - i
    back_piece = pl.BlockSpec(
        (1, SPAN, width),
        lambda i, info: ((back(i) // per_piece) ^ info[3], back(i) % per_piece, 0),
    )
    back_rows = lambda cols: pl.BlockSpec((SPAN, cols), lambda i, info: (back(i), 0))
    small_width = conv_width + width
    total, wide_grad, small = pl.pallas_call(
        functools.partial(backward_kernel, inner, state_count, heads, inner_total),
        grid_spec=pltpu.PrefetchScalarGridSpec(
            num_scalar_prefetch=1,
            grid=(blocks,),
            in_specs=[
                pl.BlockSpec((8, SPAN), lambda i, info: (0, back(i))),
                back_piece,
                back_rows(width),
                fixed((width, span)),
                fixed((width, inner)),
                back_rows(span),
                pl.BlockSpec(
                    (8, span), lambda i, info: (jnp.maximum(back(i) * (SPAN // 8) - 1, 0), 0)
                ),
                back_rows(inner),
                back_rows(LANES),
                pl.BlockSpec((state_count, inner), lambda i, info: (back(i), 0)),
                fixed(taps.shape),
                fixed(chan.shape),
                fixed(head_rows.shape),
                fixed(gain_rows.shape),
                fixed(expand.shape),
                fixed(gather.shape),
            ],
            out_specs=[
                back_piece,
                fixed((width, span + inner)),
                fixed((8, small_width)),
            ],
            scratch_shapes=[
                pltpu.VMEM((SPAN + 8, conv_width), f32),
                pltpu.VMEM((SPAN + 8, conv_width), f32),
                pltpu.VMEM((state_count, inner), f32),
                pltpu.VMEM((width, span), f32),
                pltpu.VMEM((width, inner), f32),
                pltpu.VMEM((SPAN, span), bf16),
            ],
        ),
        out_shape=[
            shaped((tensor, piece_len, width), bf16),
            shaped((width, span + inner), bf16),
            shaped((8, small_width), f32),
        ],
        compiler_params=limits,
        name="backward",
    )(
        info,
        stats,
        grad_all,
        normed,
        weight_in,
        weight_out,
        pre,
        pre,
        y_val,
        cum,
        entering,
        taps,
        chan,
        head_rows,
        gain_rows,
        expand,
        gather,
    )

    normed_grad = scatter_relative(total, "tensor")
    parts = line_scatter(wide_grad.reshape(data, share, span + inner), "dp")
    small = sum_over(small, "dp")
    shared_small = sum_over(small[:, inner:], "tensor")
    bc_part = sum_over(parts[:, 2 * inner : step_at], "tensor")

    row_scale = lax.rsqrt(jnp.mean(residual * residual, axis=1, keepdims=True) + epsilon)
    scaled_grad = normed_grad * gain_row
    hidden_grad = row_scale * scaled_grad - residual * row_scale**3 * jnp.mean(
        scaled_grad * residual, axis=1, keepdims=True
    )
    hidden_grad = (hidden_grad + grad_local.astype(f32)).astype(bf16)

    place = lax.axis_index("dp")
    local = lambda values: lax.dynamic_slice_in_dim(
        values, place * (values.shape[-1] // data), values.shape[-1] // data, values.ndim - 1
    )
    inner_grad = local(small[:CONV, :inner].T.reshape(heads, -1))
    shared_grad = local(shared_small[:CONV, : 2 * state_count].T.reshape(-1))
    norm_grad = local(shared_small[0, 2 * state_count :])
    return (
        block_out[:, None, :],
        hidden_grad[:, None, :],
        jnp.stack([parts[:, :inner], parts[:, inner : 2 * inner]]),
        parts[:, step_at : step_at + heads],
        bc_part,
        inner_grad,
        shared_grad,
        parts[:, span:].T,
        small[6, :heads],
        small[7, :heads],
        jnp.sum(small[4, :inner].reshape(heads, head_dim), axis=1),
        norm_grad,
        small[5, :inner],
    )


def solution(mesh):
    in_specs = (
        P("tensor", "dp", None),
        P("tensor", "dp", None),
        P("dp", None),
        P(None, "dp", "tensor"),
        P("dp", "tensor"),
        P("dp", None),
        P("tensor", "dp"),
        P("dp"),
        P("tensor", "dp"),
        P("tensor"),
        P("tensor"),
        P("tensor"),
        P("dp"),
        P("tensor"),
    )
    out_specs = (
        P("tensor", "dp", None),
        P("tensor", "dp", None),
        P(None, "dp", "tensor"),
        P("dp", "tensor"),
        P("dp", None),
        P("tensor", "dp"),
        P("dp"),
        P("tensor", "dp"),
        P("tensor"),
        P("tensor"),
        P("tensor"),
        P("dp"),
        P("tensor"),
    )
    return jax.shard_map(
        per_device, mesh=mesh, in_specs=in_specs, out_specs=out_specs, check_vma=False
    )
```

time: 1100 us -> 288 us (0.26)
  waiting for transfers between devices: 344 us -> 73.3 us
  blocking collectives: 215 us -> 0 us
  other arithmetic: 200 us -> 29.2 us
  local copies, waits for them, and re-layouts: 187 us -> 30.4 us
  matrix products: 130 us -> 0 us
  Pallas kernels: 0 us -> 80.4 us
  starting transfers between devices: 0.62 us -> 71.5 us
  between operations: 18.1 us -> 1.48 us
    reduce_scatter x5 -> x0, waiting for transfers between devices: 206 us -> none  [the longest x1 72.3 us: per_device(): lax.psum_scatter(zx_weight_grad, 'dp', scatter_dimension=1, tiled=True)]
    all_gather x5 -> x0, blocking collectives: 135 us -> none  [the longest x1 33.5 us: per_device(): lax.all_gather(out_weight, 'dp', axis=1, tiled=True)]
    dot_general x30 -> x0, matrix products: 128 us -> none  [the longest x4 43.9 us: state_space(): jnp.einsum('cijh,cjhp->cihp', mixing, blocks_x, preferred_element_type=jn...]
    unnamed x13 -> x0, waiting for transfers between devices: 113 us -> none
    pallas_call x0 -> x3, Pallas kernels: none -> 80.4 us  [the longest x1 48.2 us: per_device(): pl.pallas_call(functools.partial(backward_kernel, inner, state_count, hea...]
    ppermute x0 -> x54, waiting for transfers between devices: none -> 73.3 us  [the longest x24 38.5 us: swap(): return lax.ppermute(values, axis, [(i, i ^ bit) for i in range(size)])]
    ppermute x0 -> x54, starting transfers between devices: none -> 71.5 us  [the longest x12 22.5 us: line_gather(): lax.ppermute(v, axis, [(i, i ^ 1) for i in range(size) if ok(i // 2)])]
    unnamed x2 -> x0, blocking collectives: 60.2 us -> none
  transfers between devices with their start and end apart: 11 -> 54, of which waited for: 7 -> 19; matrix products, arithmetic and copies ran while one was open for 17% -> 17% of each run, Pallas kernels for 0% -> 17%
where the time goes in v1:
time: 288 us; the launch traced here: 286 us
  Pallas kernels  80.4 us (28%)
  waiting for transfers between devices  73.3 us (25%)
  starting transfers between devices  71.5 us (25%)
  local copies, waits for them, and re-layouts  30.4 us (11%)
  other arithmetic  29.2 us (10%)
    pallas_call x1, Pallas kernels, per_device(): pl.pallas_call(functools.partial(backward_kernel, inner, state_count, hea...  48.2 us
    ppermute x24, waiting for transfers between devices, swap(): return lax.ppermute(values, axis, [(i, i ^ bit) for i in range(size)])  38.5 us
    ppermute x12, starting transfers between devices, line_gather(): lax.ppermute(v, axis, [(i, i ^ 1) for i in range(size) if ok(i // 2)])  22.5 us
    pallas_call x1, Pallas kernels, per_device(): pl.pallas_call(functools.partial(forward_kernel, inner, state_count, head...  22.2 us
    ppermute x6, waiting for transfers between devices, line_gather(): lax.ppermute(behind[-1], axis, [(i + 2, i) for i in range(size - 2) if i...  19.4 us
    ppermute x6, starting transfers between devices, line_gather(): lax.ppermute(ahead[-1], axis, [(i, i + 2) for i in range(size - 2) if i /...  16.4 us
    ppermute x12, waiting for transfers between devices, line_gather(): lax.ppermute(v, axis, [(i, i ^ 1) for i in range(size) if ok(i // 2)])  14.5 us
    ppermute x24, starting transfers between devices, swap(): return lax.ppermute(values, axis, [(i, i ^ bit) for i in range(size)])  13.6 us
  transfers between devices with their start and end apart: 54, of which 19 were waited for; matrix products, arithmetic and copies ran while one was open for 17% of the time, Pallas kernels for 17%

profile of v1, /device:TPU:0, one launch (start us, length us, event | category | flops | bytes accessed | tf_op | source)
XLA Modules:
  0.0 286.3 jit_solution(4811748390890036641)
XLA Ops:
  0.7 1.6 bitcast_dynamic-update-slice_fusion.10
  2.3 1.5 bitcast_dynamic-update-slice_fusion.9
  4.6 1.4 constant_dynamic-update-slice_fusion
  6.6 1.5 bitcast_dynamic-update-slice_fusion.8
  8.1 3.0 %collective-permute-start.3 = (bf16[96,1536]{1,0:T(8,128)(2,1)}, bf16[96,1536]{1,0:T(8,128)(2,1)}, u32[]{:S(2)}, u32[]{:S(2)}) collective-permute-start(bf16[96,1536]{1,0:T(8,128)(2,1)} %bitcast_dynamic-update-slice_fusion.8), channel_id=1, source_target_pairs={{0,4},{4,0},{8,12},{12,8},{16,20},{20,16},{24,28},{28,24},{1,5},{5... | collective-permute-start | bytes 884744 | tf_op jit(solution)/shard_map/ppermute | solution.py:405
  11.1 1.3 collective-permute-start.5
  13.9 1.3 collective-permute-start.18
  15.2 5.2 %collective-permute-start.17 = (bf16[1,416]{1,0:T(2,128)(2,1)S(1)}, bf16[1,416]{1,0:T(2,128)(2,1)S(1)}, u32[]{:S(2)}, u32[]{:S(2)}) collective-permute-start(bf16[1,416]{1,0:T(2,128)(2,1)S(1)} %broadcast_in_dim.89), channel_id=1, source_target_pairs={{0,8},{4,12},{8,16},{12,20},{16,24},{20,28},{1,9},{5,13},{9,17},{1... | collective-permute-start | bytes 2504 | tf_op jit(solution)/shard_map/ppermute | solution.py:445
  25.4 1.3 select_maximum_fusion.1.head_ref
  26.8 1.0 bitcast_dynamic-update-slice_fusion.7
  27.9 1.3 collective-permute-start.19
  30.0 8.5 %collective-permute-start.4 = (bf16[96,1536]{1,0:T(8,128)(2,1)}, bf16[96,1536]{1,0:T(8,128)(2,1)}, u32[]{:S(2)}, u32[]{:S(2)}) collective-permute-start(bf16[96,1536]{1,0:T(8,128)(2,1)} %bitcast_dynamic-update-slice_fusion.8), channel_id=1, source_target_pairs={{0,8},{4,12},{8,16},{12,20},{16,24},{20,28},{1,9},{5,13},{9,17},{1... | collective-permute-start | bytes 884744 | tf_op jit(solution)/shard_map/ppermute | solution.py:445
  38.5 1.3 collective-permute-start.20
  40.5 3.5 %collective-permute-done.20 = bf16[1,416]{1,0:T(2,128)(2,1)S(1)} collective-permute-done((bf16[1,416]{1,0:T(2,128)(2,1)S(1)}, bf16[1,416]{1,0:T(2,128)(2,1)S(1)}, u32[]{:S(2)}, u32[]{:S(2)}) %collective-permute-start.20) | collective-permute-done | bytes 864 | tf_op jit(solution)/shard_map/ppermute | solution.py:448
  44.0 3.9 %collective-permute-start.25 = (bf16[1,416]{1,0:T(2,128)(2,1)S(1)}, bf16[1,416]{1,0:T(2,128)(2,1)S(1)}, u32[]{:S(2)}, u32[]{:S(2)}) collective-permute-start(bf16[1,416]{1,0:T(2,128)(2,1)S(1)} %collective-permute-done.19), channel_id=1, source_target_pairs={{0,4},{4,0},{8,12},{12,8},{1,5},{5,1},{9,13},{13,9},{2,6},{6,2},{1... | collective-permute-start | bytes 2504 | tf_op jit(solution)/shard_map/ppermute | solution.py:457
  50.2 3.9 %collective-permute-start.22 = (bf16[1,416]{1,0:T(2,128)(2,1)S(1)}, bf16[1,416]{1,0:T(2,128)(2,1)S(1)}, u32[]{:S(2)}, u32[]{:S(2)}) collective-permute-start(bf16[1,416]{1,0:T(2,128)(2,1)S(1)} %collective-permute-done.20), channel_id=1, source_target_pairs={{0,4},{4,0},{1,5},{5,1},{2,6},{6,2},{3,7},{7,3}} | collective-permute-start | bytes 2504 | tf_op jit(solution)/shard_map/ppermute | solution.py:457
  54.1 2.0 collective-permute-start.28
  57.0 2.6 collective-permute-done.28
  59.6 1.5 collective-permute-start.1
  61.1 1.3 collective-permute-start.6
  65.2 7.5 %collective-permute-done.6 = bf16[96,1536]{1,0:T(8,128)(2,1)} collective-permute-done((bf16[96,1536]{1,0:T(8,128)(2,1)}, bf16[96,1536]{1,0:T(8,128)(2,1)}, u32[]{:S(2)}, u32[]{:S(2)}) %collective-permute-start.6) | collective-permute-done | bytes 294944 | tf_op jit(solution)/shard_map/ppermute | solution.py:448
  72.7 1.3 collective-permute-start.7
  74.0 1.0 bitcast_dynamic-update-slice_fusion.6
  75.0 8.4 %collective-permute-done.7 = bf16[96,1536]{1,0:T(8,128)(2,1)S(1)} collective-permute-done((bf16[96,1536]{1,0:T(8,128)(2,1)}, bf16[96,1536]{1,0:T(8,128)(2,1)S(1)}, u32[]{:S(2)}, u32[]{:S(2)}) %collective-permute-start.7) | collective-permute-done | bytes 294944 | tf_op jit(solution)/shard_map/ppermute | solution.py:448
  83.4 2.4 collective-permute-start.9
  86.1 3.9 %collective-permute-start.12 = (bf16[96,1536]{1,0:T(8,128)(2,1)}, bf16[96,1536]{1,0:T(8,128)(2,1)S(1)}, u32[]{:S(2)}, u32[]{:S(2)}) collective-permute-start(bf16[96,1536]{1,0:T(8,128)(2,1)} %collective-permute-done.6), channel_id=1, source_target_pairs={{0,4},{4,0},{8,12},{12,8},{1,5},{5,1},{9,13},{13,9},{2,6},{6,2},{1... | collective-permute-start | bytes 884744 | tf_op jit(solution)/shard_map/ppermute | solution.py:457
  90.0 5.3 %collective-permute-done.9 = bf16[96,1536]{1,0:T(8,128)(2,1)S(1)} collective-permute-done((bf16[96,1536]{1,0:T(8,128)(2,1)S(1)}, bf16[96,1536]{1,0:T(8,128)(2,1)S(1)}, u32[]{:S(2)}, u32[]{:S(2)}) %collective-permute-start.9) | collective-permute-done | bytes 294944 | tf_op jit(solution)/shard_map/ppermute | solution.py:457
  96.0 1.0 bitcast_dynamic-update-slice_fusion.3
  97.1 2.4 collective-permute-start.15
  99.5 1.7 collective-permute-done.12
  102.0 3.9 %collective-permute-done.15 = bf16[96,1536]{1,0:T(8,128)(2,1)S(1)} collective-permute-done((bf16[96,1536]{1,0:T(8,128)(2,1)}, bf16[96,1536]{1,0:T(8,128)(2,1)S(1)}, u32[]{:S(2)}, u32[]{:S(2)}) %collective-permute-start.15) | collective-permute-done | bytes 294944 | tf_op jit(solution)/shard_map/ppermute | solution.py:457
  107.4 1.0 bitcast_dynamic-update-slice_fusion.1
  108.5 1.4 slice.124.weight_ref
  110.8 3.0 %pad_maximum_fusion.hidden_ref = bf16[4,512,768]{2,1,0:T(8,128)(2,1)} fusion(bf16[1,512,768]{2,1,0:T(8,128)(2,1)S(1)} %bitcast.148, bf16[1,512,768]{2,1,0:T(8,128)(2,1)} %bitcast.6, bf16[1,512,768]{2,1,0:T(8,128)(2,1)} %bitcast.5, bf16[1,512,768]{2,1,0:T(8,128)(2,1)S(1)} %bitcast.139), kind=kLoop, calls=%fused_computation | loop fusion | flops 4718592 | bytes 6291456 | tf_op jit(solution)/shard_map/stack | solution.py:422
  113.9 1.9 pad_maximum_fusion.1.refs_1_.grad_ref
  116.4 22.2 %forward.1 = (bf16[2048,768]{1,0:T(8,128)(2,1)}, f32[2048,1152]{1,0:T(8,128)}, f32[2048,384]{1,0:T(8,128)}, f32[2048,384]{1,0:T(8,128)}, f32[2048,128]{1,0:T(8,128)}, /*index=5*/f32[1024,384]{1,0:T(8,128)}) custom-call(s32[4]{0:T(128)} %pad_add_fusion.info_ref, bf16[4,512,768]{2,1,0:T(8,128)(2,1)} %pad_maximum_fusion.hidden_ref, ...), custom_call_target="tpu_custom_call" | custom-call | tf_op jit(solution)/shard_map/forward/pallas_call | solution.py:592
  138.6 9.9 %branch.1 = (bf16[4,512,768]{2,1,0:T(8,128)(2,1)}, f32[8,2048]{1,0:T(8,128)}) custom-call(s32[4]{0:T(128)} %pad_add_fusion.info_ref, f32[2048,384]{1,0:T(8,128)} %get-tuple-element.24.refs_0_, bf16[4,512,768]{2,1,0:T(8,128)(2,1)} %pad_maximum_fusion.1.refs_1_.grad_ref, bf16[768,384]{1,0:T(8,128)(2,1)} %slice.128.refs_2_.out_ref, ...), custom_call_target="tpu_custom_call" | custom-call | tf_op jit(solution)/shard_map/branch/pallas_call | solution.py:631
  151.5 2.6 slice_bitcast_fusion.3
  154.3 1.1 collective-permute-done.36
  156.0 48.2 %backward.1 = (bf16[4,512,768]{2,1,0:T(8,128)(2,1)}, bf16[768,1536]{1,0:T(8,128)(2,1)}, f32[8,1408]{1,0:T(8,128)}) custom-call(s32[4]{0:T(128)} %pad_add_fusion.info_ref, f32[8,2048]{1,0:T(8,128)} %add.254.stats_ref, bf16[4,512,768]{2,1,0:T(8,128)(2,1)} %pad_maximum_fusion.1.refs_1_.grad_ref, bf16[2048,768]{1,0:T(8,128)(2,1)} %get-tuple-element.27.normed_ref, ...), custom_call_target="tpu_custom_call" | custom-call | tf_op jit(solution)/shard_map/backward/pallas_call | solution.py:662
  204.8 1.4 dynamic-slice_bitcast_fusion
  206.1 1.6 collective-permute-start.40
  207.7 1.2 collective-permute-done.49
  209.1 2.6 slice_bitcast_fusion.1
  212.2 0.9 collective-permute-done.50
  213.6 4.6 %collective-permute-done.51 = f32[8,1408]{1,0:T(8,128)S(1)} collective-permute-done((f32[8,1408]{1,0:T(8,128)S(1)}, f32[8,1408]{1,0:T(8,128)S(1)}, u32[]{:S(2)}, u32[]{:S(2)}) %collective-permute-start.51) | collective-permute-done | bytes 45088 | tf_op jit(solution)/shard_map/ppermute | solution.py:405
  221.3 2.4 collective-permute-done.53
  223.7 10.2 %collective-permute-done.40 = bf16[4,96,1536]{2,1,0:T(8,128)(2,1)} collective-permute-done((bf16[4,96,1536]{2,1,0:T(8,128)(2,1)S(1)}, bf16[4,96,1536]{2,1,0:T(8,128)(2,1)}, u32[]{:S(2)}, u32[]{:S(2)}) %collective-permute-start.40) | collective-permute-done | bytes 1179680 | tf_op jit(solution)/shard_map/ppermute | solution.py:405
  233.9 1.9 fusion
  236.6 1.3 collective-permute-start.41
  237.9 2.4 fusion.8
  241.2 1.4 collective-permute-start.44
  244.1 5.1 %collective-permute-start.42 = (bf16[96,1536]{1,0:T(8,128)(2,1)}, bf16[96,1536]{1,0:T(8,128)(2,1)}, u32[]{:S(2)}, u32[]{:S(2)}) collective-permute-start(bf16[96,1536]{1,0:T(8,128)(2,1)} %fusion.16), channel_id=1, source_target_pairs={{0,8},{4,12},{8,16},{12,20},{1,9},{5,13},{9,17},{13,21},{2,10},{6,... | collective-permute-start | bytes 884744 | tf_op jit(solution)/shard_map/ppermute | solution.py:493
  250.6 1.0 reshape.149
  252.3 1.9 fusion.10
  254.1 1.4 collective-permute-start.34
  255.6 1.2 fusion.17
  257.6 2.9 %collective-permute-done.39 = bf16[512,768]{1,0:T(8,128)(2,1)S(1)} collective-permute-done((bf16[512,768]{1,0:T(8,128)(2,1)}, bf16[512,768]{1,0:T(8,128)(2,1)S(1)}, u32[]{:S(2)}, u32[]{:S(2)}) %collective-permute-start.39) | collective-permute-done | bytes 786464 | tf_op jit(solution)/shard_map/ppermute | solution.py:405
  261.2 1.3 collective-permute-start.43
  262.6 1.3 collective-permute-start.46
  263.9 11.7 %collective-permute-done.34 = bf16[512,768]{1,0:T(8,128)(2,1)S(1)} collective-permute-done((bf16[512,768]{1,0:T(8,128)(2,1)S(1)}, bf16[512,768]{1,0:T(8,128)(2,1)S(1)}, u32[]{:S(2)}, u32[]{:S(2)}) %collective-permute-start.34) | collective-permute-done | bytes 786464 | tf_op jit(solution)/shard_map/ppermute | solution.py:405
  275.7 3.1 %fusion.12 = (bf16[512,1,768]{2,0,1:T(8,128)(2,1)}, bf16[512,1,768]{2,0,1:T(8,128)(2,1)}) fusion(bf16[512,768]{1,0:T(8,128)(2,1)S(1)} %collective-permute-done.39, f32[512]{0:T(512)S(1)} %get-tuple-element.82, f32[512]{0:T(512)S(1)} %get-tuple-element.81, f32[768]{0:T(1024)S(1)} %broadcast_in_dim.98, f32[512]{0:T(512)S(1)} %get-tuple-element.80, ...), kind=kLoop, calls=%fused_computation.25 | loop fusion | flops 10223616 | bytes 7875584 | tf_op jit(solution)/shard_map/broadcast_in_dim | solution.py:750
  280.4 1.4 collective-permute-start.48
  282.6 3.1 %collective-permute-done.48 = f32[96,256]{1,0:T(8,128)S(1)} collective-permute-done((f32[96,256]{1,0:T(8,128)S(1)}, f32[96,256]{1,0:T(8,128)S(1)}, u32[]{:S(2)}, u32[]{:S(2)}) %collective-permute-start.48) | collective-permute-done | bytes 98336 | tf_op jit(solution)/shard_map/ppermute | solution.py:405
  (167 shorter events, 38.2 us)
Async XLA Ops:
  0.6 59.0 %copy-start = (bf16[512,1,768]{2,0,1:T(8,128)(2,1)S(1)}, bf16[512,1,768]{2,0,1:T(8,128)(2,1)}, u32[]{:S(2)}) copy-start(bf16[512,1,768]{2,0,1:T(8,128)(2,1)} %param.14) | copy-start | bytes 2359300
  8.1 56.4 %collective-permute-start.3 = (bf16[96,1536]{1,0:T(8,128)(2,1)}, bf16[96,1536]{1,0:T(8,128)(2,1)}, u32[]{:S(2)}, u32[]{:S(2)}) collective-permute-start(bf16[96,1536]{1,0:T(8,128)(2,1)} %bitcast_dynamic-update-slice_fusion.8), channel_id=1, source_target_pairs={{0,4},{4,0},{8,12},{12,8},{16,20},{20,16},{24,28},{28,24},{1,5},{5... | collective-permute-start | bytes 884744 | tf_op jit(solution)/shard_map/ppermute | solution.py:405
  11.1 50.0 %collective-permute-start.5 = (bf16[96,1536]{1,0:T(8,128)(2,1)}, bf16[96,1536]{1,0:T(8,128)(2,1)}, u32[]{:S(2)}, u32[]{:S(2)}) collective-permute-start(bf16[96,1536]{1,0:T(8,128)(2,1)} %bitcast_dynamic-update-slice_fusion.8), channel_id=1, source_target_pairs={{8,0},{12,4},{16,8},{20,12},{24,16},{28,20},{9,1},{13,5},{17,9},{2... | collective-permute-start | bytes 884744 | tf_op jit(solution)/shard_map/ppermute | solution.py:448
  13.9 16.0 %collective-permute-start.16 = (bf16[1,416]{1,0:T(2,128)(2,1)S(1)}, bf16[1,416]{1,0:T(2,128)(2,1)S(1)}, u32[]{:S(2)}, u32[]{:S(2)}) collective-permute-start(bf16[1,416]{1,0:T(2,128)(2,1)S(1)} %broadcast_in_dim.89), channel_id=1, source_target_pairs={{0,4},{4,0},{8,12},{12,8},{16,20},{20,16},{24,28},{28,24},{1,5},{5... | collective-permute-start | bytes 2504 | tf_op jit(solution)/shard_map/ppermute | solution.py:405
  13.9 13.9 %collective-permute-start.18 = (bf16[1,416]{1,0:T(2,128)(2,1)S(1)}, bf16[1,416]{1,0:T(2,128)(2,1)S(1)}, u32[]{:S(2)}, u32[]{:S(2)}) collective-permute-start(bf16[1,416]{1,0:T(2,128)(2,1)S(1)} %broadcast_in_dim.89), channel_id=1, source_target_pairs={{8,0},{12,4},{16,8},{20,12},{24,16},{28,20},{9,1},{13,5},{17,9},{2... | collective-permute-start | bytes 2504 | tf_op jit(solution)/shard_map/ppermute | solution.py:448
  15.2 13.9 %collective-permute-start.17 = (bf16[1,416]{1,0:T(2,128)(2,1)S(1)}, bf16[1,416]{1,0:T(2,128)(2,1)S(1)}, u32[]{:S(2)}, u32[]{:S(2)}) collective-permute-start(bf16[1,416]{1,0:T(2,128)(2,1)S(1)} %broadcast_in_dim.89), channel_id=1, source_target_pairs={{0,8},{4,12},{8,16},{12,20},{16,24},{20,28},{1,9},{5,13},{9,17},{1... | collective-permute-start | bytes 2504 | tf_op jit(solution)/shard_map/ppermute | solution.py:445
  27.9 10.7 %collective-permute-start.19 = (bf16[1,416]{1,0:T(2,128)(2,1)S(1)}, bf16[1,416]{1,0:T(2,128)(2,1)S(1)}, u32[]{:S(2)}, u32[]{:S(2)}) collective-permute-start(bf16[1,416]{1,0:T(2,128)(2,1)S(1)} %collective-permute-done.18), channel_id=1, source_target_pairs={{8,0},{12,4},{16,8},{20,12},{9,1},{13,5},{17,9},{21,13},{10,2},{14... | collective-permute-start | bytes 2504 | tf_op jit(solution)/shard_map/ppermute | solution.py:448
  29.2 10.7 %collective-permute-start.23 = (bf16[1,416]{1,0:T(2,128)(2,1)S(1)}, bf16[1,416]{1,0:T(2,128)(2,1)S(1)}, u32[]{:S(2)}, u32[]{:S(2)}) collective-permute-start(bf16[1,416]{1,0:T(2,128)(2,1)S(1)} %collective-permute-done.17), channel_id=1, source_target_pairs={{8,16},{12,20},{16,24},{20,28},{9,17},{13,21},{17,25},{21,29},{10,... | collective-permute-start | bytes 2504 | tf_op jit(solution)/shard_map/ppermute | solution.py:445
  30.0 33.9 %collective-permute-start.4 = (bf16[96,1536]{1,0:T(8,128)(2,1)}, bf16[96,1536]{1,0:T(8,128)(2,1)}, u32[]{:S(2)}, u32[]{:S(2)}) collective-permute-start(bf16[96,1536]{1,0:T(8,128)(2,1)} %bitcast_dynamic-update-slice_fusion.8), channel_id=1, source_target_pairs={{0,8},{4,12},{8,16},{12,20},{16,24},{20,28},{1,9},{5,13},{9,17},{1... | collective-permute-start | bytes 884744 | tf_op jit(solution)/shard_map/ppermute | solution.py:445
  38.5 5.5 %collective-permute-start.20 = (bf16[1,416]{1,0:T(2,128)(2,1)S(1)}, bf16[1,416]{1,0:T(2,128)(2,1)S(1)}, u32[]{:S(2)}, u32[]{:S(2)}) collective-permute-start(bf16[1,416]{1,0:T(2,128)(2,1)S(1)} %collective-permute-done.19), channel_id=1, source_target_pairs={{8,0},{12,4},{9,1},{13,5},{10,2},{14,6},{11,3},{15,7}} | collective-permute-start | bytes 2504 | tf_op jit(solution)/shard_map/ppermute | solution.py:448
  39.9 8.1 %collective-permute-start.24 = (bf16[1,416]{1,0:T(2,128)(2,1)S(1)}, bf16[1,416]{1,0:T(2,128)(2,1)S(1)}, u32[]{:S(2)}, u32[]{:S(2)}) collective-permute-start(bf16[1,416]{1,0:T(2,128)(2,1)S(1)} %collective-permute-done.23), channel_id=1, source_target_pairs={{16,20},{20,16},{24,28},{28,24},{17,21},{21,17},{25,29},{29,25},{1... | collective-permute-start | bytes 2504 | tf_op jit(solution)/shard_map/ppermute | solution.py:457
  44.0 5.5 %collective-permute-start.25 = (bf16[1,416]{1,0:T(2,128)(2,1)S(1)}, bf16[1,416]{1,0:T(2,128)(2,1)S(1)}, u32[]{:S(2)}, u32[]{:S(2)}) collective-permute-start(bf16[1,416]{1,0:T(2,128)(2,1)S(1)} %collective-permute-done.19), channel_id=1, source_target_pairs={{0,4},{4,0},{8,12},{12,8},{1,5},{5,1},{9,13},{13,9},{2,6},{6,2},{1... | collective-permute-start | bytes 2504 | tf_op jit(solution)/shard_map/ppermute | solution.py:457
  47.9 6.2 %collective-permute-start.21 = (bf16[1,416]{1,0:T(2,128)(2,1)S(1)}, bf16[1,416]{1,0:T(2,128)(2,1)S(1)}, u32[]{:S(2)}, u32[]{:S(2)}) collective-permute-start(bf16[1,416]{1,0:T(2,128)(2,1)S(1)} %collective-permute-done.17), channel_id=1, source_target_pairs={{8,12},{12,8},{16,20},{20,16},{24,28},{28,24},{9,13},{13,9},{17,21... | collective-permute-start | bytes 2504 | tf_op jit(solution)/shard_map/ppermute | solution.py:457
  49.5 0.7 collective-permute-start.26
  50.2 5.9 %collective-permute-start.22 = (bf16[1,416]{1,0:T(2,128)(2,1)S(1)}, bf16[1,416]{1,0:T(2,128)(2,1)S(1)}, u32[]{:S(2)}, u32[]{:S(2)}) collective-permute-start(bf16[1,416]{1,0:T(2,128)(2,1)S(1)} %collective-permute-done.20), channel_id=1, source_target_pairs={{0,4},{4,0},{1,5},{5,1},{2,6},{6,2},{3,7},{7,3}} | collective-permute-start | bytes 2504 | tf_op jit(solution)/shard_map/ppermute | solution.py:457
  54.1 5.5 %collective-permute-start.28 = (bf16[1,416]{1,0:T(2,128)(2,1)S(1)}, bf16[1,416]{1,0:T(2,128)(2,1)S(1)}, u32[]{:S(2)}, u32[]{:S(2)}) collective-permute-start(bf16[1,416]{1,0:T(2,128)(2,1)S(1)} %collective-permute-done.18), channel_id=1, source_target_pairs={{0,4},{4,0},{8,12},{12,8},{16,20},{20,16},{1,5},{5,1},{9,13},{13,9... | collective-permute-start | bytes 2504 | tf_op jit(solution)/shard_map/ppermute | solution.py:457
  56.1 5.0 %collective-permute-start.27 = (bf16[1,416]{1,0:T(2,128)(2,1)S(1)}, bf16[1,416]{1,0:T(2,128)(2,1)S(1)}, u32[]{:S(2)}, u32[]{:S(2)}) collective-permute-start(bf16[1,416]{1,0:T(2,128)(2,1)S(1)} %collective-permute-done.26), channel_id=1, source_target_pairs={{24,28},{28,24},{25,29},{29,25},{26,30},{30,26},{27,31},{31,27}} | collective-permute-start | bytes 2504 | tf_op jit(solution)/shard_map/ppermute | solution.py:457
  59.6 46.3 %collective-permute-start.1 = (bf16[512,768]{1,0:T(8,128)(2,1)S(1)}, bf16[512,768]{1,0:T(8,128)(2,1)}, u32[]{:S(2)}, u32[]{:S(2)}) collective-permute-start(bf16[512,768]{1,0:T(8,128)(2,1)S(1)} %bitcast.137), channel_id=1, source_target_pairs={{0,2},{1,3},{2,0},{3,1},{4,6},{5,7},{6,4},{7,5},{8,10},{9,11},{10,... | collective-permute-start | bytes 2359304 | tf_op jit(solution)/shard_map/ppermute | solution.py:405
  61.1 49.7 %collective-permute-start = (bf16[512,768]{1,0:T(8,128)(2,1)S(1)}, bf16[512,768]{1,0:T(8,128)(2,1)}, u32[]{:S(2)}, u32[]{:S(2)}) collective-permute-start(bf16[512,768]{1,0:T(8,128)(2,1)S(1)} %bitcast.138), channel_id=1, source_target_pairs={{0,1},{1,0},{2,3},{3,2},{4,5},{5,4},{6,7},{7,6},{8,9},{9,8},{10,11... | collective-permute-start | bytes 2359304 | tf_op jit(solution)/shard_map/ppermute | solution.py:405
  61.1 11.6 %collective-permute-start.6 = (bf16[96,1536]{1,0:T(8,128)(2,1)}, bf16[96,1536]{1,0:T(8,128)(2,1)}, u32[]{:S(2)}, u32[]{:S(2)}) collective-permute-start(bf16[96,1536]{1,0:T(8,128)(2,1)} %collective-permute-done.5), channel_id=1, source_target_pairs={{8,0},{12,4},{16,8},{20,12},{9,1},{13,5},{17,9},{21,13},{10,2},{14... | collective-permute-start | bytes 884744 | tf_op jit(solution)/shard_map/ppermute | solution.py:448
  63.2 42.7 %copy-start.2 = (bf16[512,1,768]{2,0,1:T(8,128)(2,1)S(1)}, bf16[512,1,768]{2,0,1:T(8,128)(2,1)}, u32[]{:S(2)}) copy-start(bf16[512,1,768]{2,0,1:T(8,128)(2,1)} %param.15) | copy-start | bytes 2359300
  63.9 22.1 %collective-permute-start.8 = (bf16[96,1536]{1,0:T(8,128)(2,1)}, bf16[96,1536]{1,0:T(8,128)(2,1)S(1)}, u32[]{:S(2)}, u32[]{:S(2)}) collective-permute-start(bf16[96,1536]{1,0:T(8,128)(2,1)} %collective-permute-done.4), channel_id=1, source_target_pairs={{8,12},{12,8},{16,20},{20,16},{24,28},{28,24},{9,13},{13,9},{17,21... | collective-permute-start | bytes 884744 | tf_op jit(solution)/shard_map/ppermute | solution.py:457
  64.6 21.6 %collective-permute-start.10 = (bf16[96,1536]{1,0:T(8,128)(2,1)}, bf16[96,1536]{1,0:T(8,128)(2,1)S(1)}, u32[]{:S(2)}, u32[]{:S(2)}) collective-permute-start(bf16[96,1536]{1,0:T(8,128)(2,1)} %collective-permute-done.4), channel_id=1, source_target_pairs={{8,16},{12,20},{16,24},{20,28},{9,17},{13,21},{17,25},{21,29},{10,... | collective-permute-start | bytes 884744 | tf_op jit(solution)/shard_map/ppermute | solution.py:445
  72.7 10.7 %collective-permute-start.7 = (bf16[96,1536]{1,0:T(8,128)(2,1)}, bf16[96,1536]{1,0:T(8,128)(2,1)S(1)}, u32[]{:S(2)}, u32[]{:S(2)}) collective-permute-start(bf16[96,1536]{1,0:T(8,128)(2,1)} %collective-permute-done.6), channel_id=1, source_target_pairs={{8,0},{12,4},{9,1},{13,5},{10,2},{14,6},{11,3},{15,7}} | collective-permute-start | bytes 884744 | tf_op jit(solution)/shard_map/ppermute | solution.py:448
  83.4 11.8 %collective-permute-start.9 = (bf16[96,1536]{1,0:T(8,128)(2,1)S(1)}, bf16[96,1536]{1,0:T(8,128)(2,1)S(1)}, u32[]{:S(2)}, u32[]{:S(2)}) collective-permute-start(bf16[96,1536]{1,0:T(8,128)(2,1)S(1)} %collective-permute-done.7), channel_id=1, source_target_pairs={{0,4},{4,0},{1,5},{5,1},{2,6},{6,2},{3,7},{7,3}} | collective-permute-start | bytes 884744 | tf_op jit(solution)/shard_map/ppermute | solution.py:457
  86.0 20.5 %collective-permute-start.30 = (bf16[512,768]{1,0:T(8,128)(2,1)}, bf16[512,768]{1,0:T(8,128)(2,1)S(1)}, u32[]{:S(2)}, u32[]{:S(2)}) collective-permute-start(bf16[512,768]{1,0:T(8,128)(2,1)} %bitcast.140), channel_id=1, source_target_pairs={{0,2},{1,3},{2,0},{3,1},{4,6},{5,7},{6,4},{7,5},{8,10},{9,11},{10,... | collective-permute-start | bytes 2359304 | tf_op jit(solution)/shard_map/ppermute | solution.py:405
  86.1 15.1 %collective-permute-start.12 = (bf16[96,1536]{1,0:T(8,128)(2,1)}, bf16[96,1536]{1,0:T(8,128)(2,1)S(1)}, u32[]{:S(2)}, u32[]{:S(2)}) collective-permute-start(bf16[96,1536]{1,0:T(8,128)(2,1)} %collective-permute-done.6), channel_id=1, source_target_pairs={{0,4},{4,0},{8,12},{12,8},{1,5},{5,1},{9,13},{13,9},{2,6},{6,2},{1... | collective-permute-start | bytes 884744 | tf_op jit(solution)/shard_map/ppermute | solution.py:457
  95.3 1.8 collective-permute-start.11
  97.1 8.8 %collective-permute-start.15 = (bf16[96,1536]{1,0:T(8,128)(2,1)}, bf16[96,1536]{1,0:T(8,128)(2,1)S(1)}, u32[]{:S(2)}, u32[]{:S(2)}) collective-permute-start(bf16[96,1536]{1,0:T(8,128)(2,1)} %collective-permute-done.5), channel_id=1, source_target_pairs={{0,4},{4,0},{8,12},{12,8},{16,20},{20,16},{1,5},{5,1},{9,13},{13,9... | collective-permute-start | bytes 884744 | tf_op jit(solution)/shard_map/ppermute | solution.py:457
  101.2 5.3 %collective-permute-start.13 = (bf16[96,1536]{1,0:T(8,128)(2,1)S(1)}, bf16[96,1536]{1,0:T(8,128)(2,1)S(1)}, u32[]{:S(2)}, u32[]{:S(2)}) collective-permute-start(bf16[96,1536]{1,0:T(8,128)(2,1)S(1)} %collective-permute-done.10), channel_id=1, source_target_pairs={{16,24},{20,28},{17,25},{21,29},{18,26},{22,30},{19,27},{23,31}} | collective-permute-start | bytes 884744 | tf_op jit(solution)/shard_map/ppermute | solution.py:445
  105.9 8.0 %collective-permute-start.29 = (bf16[512,768]{1,0:T(8,128)(2,1)S(1)}, bf16[512,768]{1,0:T(8,128)(2,1)S(1)}, u32[]{:S(2)}, u32[]{:S(2)}) collective-permute-start(bf16[512,768]{1,0:T(8,128)(2,1)S(1)} %bitcast.141), channel_id=1, source_target_pairs={{0,1},{1,0},{2,3},{3,2},{4,5},{5,4},{6,7},{7,6},{8,9},{9,8},{10,11... | collective-permute-start | bytes 2359304 | tf_op jit(solution)/shard_map/ppermute | solution.py:405
  105.9 4.9 %collective-permute-start.2 = (bf16[512,768]{1,0:T(8,128)(2,1)}, bf16[512,768]{1,0:T(8,128)(2,1)S(1)}, u32[]{:S(2)}, u32[]{:S(2)}) collective-permute-start(bf16[512,768]{1,0:T(8,128)(2,1)} %collective-permute-done.1), channel_id=1, source_target_pairs={{0,1},{1,0},{2,3},{3,2},{4,5},{5,4},{6,7},{7,6},{8,9},{9,8},{10,11... | collective-permute-start | bytes 2359304 | tf_op jit(solution)/shard_map/ppermute | solution.py:405
  106.4 7.4 %collective-permute-start.31 = (bf16[512,768]{1,0:T(8,128)(2,1)S(1)}, bf16[512,768]{1,0:T(8,128)(2,1)S(1)}, u32[]{:S(2)}, u32[]{:S(2)}) collective-permute-start(bf16[512,768]{1,0:T(8,128)(2,1)S(1)} %collective-permute-done.30), channel_id=1, source_target_pairs={{0,1},{1,0},{2,3},{3,2},{4,5},{5,4},{6,7},{7,6},{8,9},{9,8},{10,11... | collective-permute-start | bytes 2359304 | tf_op jit(solution)/shard_map/ppermute | solution.py:405
  106.5 1.9 collective-permute-start.14
  148.6 1.5 collective-permute-start.35
  150.9 4.4 %collective-permute-start.36 = (f32[8,2048]{1,0:T(8,128)S(1)}, f32[8,2048]{1,0:T(8,128)S(1)}, u32[]{:S(2)}, u32[]{:S(2)}) collective-permute-start(f32[8,2048]{1,0:T(8,128)S(1)} %add.253), channel_id=1, source_target_pairs={{0,2},{1,3},{2,0},{3,1},{4,6},{5,7},{6,4},{7,5},{8,10},{9,11},{10,... | collective-permute-start | bytes 196616 | tf_op jit(solution)/shard_map/ppermute | solution.py:405
  154.2 98.1 %collective-permute-start.33 = (bf16[512,768]{1,0:T(8,128)(2,1)}, bf16[512,768]{1,0:T(8,128)(2,1)}, u32[]{:S(2)}, u32[]{:S(2)}) collective-permute-start(bf16[512,768]{1,0:T(8,128)(2,1)} %get-tuple-element.68), channel_id=1, source_target_pairs={{0,1},{1,0},{2,3},{3,2},{4,5},{5,4},{6,7},{7,6},{8,9},{9,8},{10,11... | collective-permute-start | bytes 2359304 | tf_op jit(solution)/shard_map/ppermute | solution.py:405
  204.2 4.8 %copy-start.4 = (f32[8,1408]{1,0:T(8,128)S(1)}, f32[8,1408]{1,0:T(8,128)}, u32[]{:S(2)}) copy-start(f32[8,1408]{1,0:T(8,128)} %get-tuple-element.34) | copy-start | bytes 135172
  204.2 4.8 %collective-permute-start.49 = (f32[8,1408]{1,0:T(8,128)}, f32[8,1408]{1,0:T(8,128)S(1)}, u32[]{:S(2)}, u32[]{:S(2)}) collective-permute-start(f32[8,1408]{1,0:T(8,128)} %get-tuple-element.34), channel_id=1, source_target_pairs={{0,4},{4,0},{8,12},{12,8},{16,20},{20,16},{24,28},{28,24},{1,5},{5... | collective-permute-start | bytes 135176 | tf_op jit(solution)/shard_map/ppermute | solution.py:405
  204.8 8.8 %slice-start = ((f32[8,2048]{1,0:T(8,128)}), f32[1,2048]{1,0:T(1,128)S(1)}, s32[]{:S(2)}) async-start(f32[8,2048]{1,0:T(8,128)} %add.254.stats_ref), calls=%async_computation | async-start | bytes 16384 | tf_op jit(solution)/shard_map/slice | solution.py:650
  206.1 27.8 %collective-permute-start.40 = (bf16[4,96,1536]{2,1,0:T(8,128)(2,1)S(1)}, bf16[4,96,1536]{2,1,0:T(8,128)(2,1)}, u32[]{:S(2)}, u32[]{:S(2)}) collective-permute-start(bf16[4,96,1536]{2,1,0:T(8,128)(2,1)S(1)} %dynamic-slice_bitcast_fusion), channel_id=1, source_target_pairs={{0,4},{4,0},{8,12},{12,8},{16,20},{20,16},{24,28},{28,24},{1,5},{5... | collective-permute-start | bytes 3538952 | tf_op jit(solution)/shard_map/ppermute | solution.py:405
  209.0 4.1 %collective-permute-start.50 = (f32[8,1408]{1,0:T(8,128)S(1)}, f32[8,1408]{1,0:T(8,128)S(1)}, u32[]{:S(2)}, u32[]{:S(2)}) collective-permute-start(f32[8,1408]{1,0:T(8,128)S(1)} %add.277), channel_id=1, source_target_pairs={{0,8},{4,12},{8,0},{12,4},{16,24},{20,28},{24,16},{28,20},{1,9},{5... | collective-permute-start | bytes 135176 | tf_op jit(solution)/shard_map/ppermute | solution.py:405
  211.7 26.2 %collective-permute-start.38 = (bf16[512,768]{1,0:T(8,128)(2,1)}, bf16[512,768]{1,0:T(8,128)(2,1)}, u32[]{:S(2)}, u32[]{:S(2)}) collective-permute-start(bf16[512,768]{1,0:T(8,128)(2,1)} %get-tuple-element.66), channel_id=1, source_target_pairs={{0,1},{1,0},{2,3},{3,2},{4,5},{5,4},{6,7},{7,6},{8,9},{9,8},{10,11... | collective-permute-start | bytes 2359304 | tf_op jit(solution)/shard_map/ppermute | solution.py:405
  211.7 45.9 %collective-permute-start.37 = (bf16[512,768]{1,0:T(8,128)(2,1)}, bf16[512,768]{1,0:T(8,128)(2,1)S(1)}, u32[]{:S(2)}, u32[]{:S(2)}) collective-permute-start(bf16[512,768]{1,0:T(8,128)(2,1)} %get-tuple-element.65), channel_id=1, source_target_pairs={{0,1},{1,0},{2,3},{3,2},{4,5},{5,4},{6,7},{7,6},{8,9},{9,8},{10,11... | collective-permute-start | bytes 2359304 | tf_op jit(solution)/shard_map/ppermute | solution.py:405
  213.1 5.1 %collective-permute-start.51 = (f32[8,1408]{1,0:T(8,128)S(1)}, f32[8,1408]{1,0:T(8,128)S(1)}, u32[]{:S(2)}, u32[]{:S(2)}) collective-permute-start(f32[8,1408]{1,0:T(8,128)S(1)} %add.278), channel_id=1, source_target_pairs={{0,16},{4,20},{8,24},{12,28},{16,0},{20,4},{24,8},{28,12},{1,17},{... | collective-permute-start | bytes 135176 | tf_op jit(solution)/shard_map/ppermute | solution.py:405
  218.2 1.5 collective-permute-start.52
  219.7 4.0 %collective-permute-start.53 = (f32[8,1024]{1,0:T(8,128)S(1)}, f32[8,1024]{1,0:T(8,128)S(1)}, u32[]{:S(2)}, u32[]{:S(2)}) collective-permute-start(f32[8,1024]{1,0:T(8,128)S(1)} %slice_add_fusion), channel_id=1, source_target_pairs={{0,2},{1,3},{2,0},{3,1},{4,6},{5,7},{6,4},{7,5},{8,10},{9,11},{10,... | collective-permute-start | bytes 98312 | tf_op jit(solution)/shard_map/ppermute | solution.py:405
  236.6 6.8 %collective-permute-start.41 = (bf16[96,1536]{1,0:T(8,128)(2,1)S(1)}, bf16[96,1536]{1,0:T(8,128)(2,1)S(1)}, u32[]{:S(2)}, u32[]{:S(2)}) collective-permute-start(bf16[96,1536]{1,0:T(8,128)(2,1)S(1)} %get-tuple-element.71), channel_id=1, source_target_pairs={{0,8},{4,12},{1,9},{5,13},{2,10},{6,14},{3,11},{7,15}} | collective-permute-start | bytes 884744 | tf_op jit(solution)/shard_map/ppermute | solution.py:493
  240.3 20.2 %collective-permute-start.39 = (bf16[512,768]{1,0:T(8,128)(2,1)}, bf16[512,768]{1,0:T(8,128)(2,1)S(1)}, u32[]{:S(2)}, u32[]{:S(2)}) collective-permute-start(bf16[512,768]{1,0:T(8,128)(2,1)} %fusion.8), channel_id=1, source_target_pairs={{0,2},{1,3},{2,0},{3,1},{4,6},{5,7},{6,4},{7,5},{8,10},{9,11},{10,... | collective-permute-start | bytes 2359304 | tf_op jit(solution)/shard_map/ppermute | solution.py:405
  241.2 12.9 %collective-permute-start.44 = (bf16[96,1536]{1,0:T(8,128)(2,1)}, bf16[96,1536]{1,0:T(8,128)(2,1)}, u32[]{:S(2)}, u32[]{:S(2)}) collective-permute-start(bf16[96,1536]{1,0:T(8,128)(2,1)} %get-tuple-element.72), channel_id=1, source_target_pairs={{24,16},{28,20},{25,17},{29,21},{26,18},{30,22},{27,19},{31,23}} | collective-permute-start | bytes 884744 | tf_op jit(solution)/shard_map/ppermute | solution.py:496
  244.1 11.5 %collective-permute-start.42 = (bf16[96,1536]{1,0:T(8,128)(2,1)}, bf16[96,1536]{1,0:T(8,128)(2,1)}, u32[]{:S(2)}, u32[]{:S(2)}) collective-permute-start(bf16[96,1536]{1,0:T(8,128)(2,1)} %fusion.16), channel_id=1, source_target_pairs={{0,8},{4,12},{8,16},{12,20},{1,9},{5,13},{9,17},{13,21},{2,10},{6,... | collective-permute-start | bytes 884744 | tf_op jit(solution)/shard_map/ppermute | solution.py:493
  251.7 8.9 %copy-start.1 = (bf16[4,512,768]{2,1,0:T(8,128)(2,1)S(1)}, bf16[4,512,768]{2,1,0:T(8,128)(2,1)}, u32[]{:S(2)}) copy-start(bf16[4,512,768]{2,1,0:T(8,128)(2,1)} %get-tuple-element.32) | copy-start | bytes 9437188
  252.3 11.7 %collective-permute-start.32 = (bf16[512,768]{1,0:T(8,128)(2,1)}, bf16[512,768]{1,0:T(8,128)(2,1)S(1)}, u32[]{:S(2)}, u32[]{:S(2)}) collective-permute-start(bf16[512,768]{1,0:T(8,128)(2,1)} %get-tuple-element.67), channel_id=1, source_target_pairs={{0,1},{1,0},{2,3},{3,2},{4,5},{5,4},{6,7},{7,6},{8,9},{9,8},{10,11... | collective-permute-start | bytes 2359304 | tf_op jit(solution)/shard_map/ppermute | solution.py:405
  254.1 21.5 %collective-permute-start.34 = (bf16[512,768]{1,0:T(8,128)(2,1)S(1)}, bf16[512,768]{1,0:T(8,128)(2,1)S(1)}, u32[]{:S(2)}, u32[]{:S(2)}) collective-permute-start(bf16[512,768]{1,0:T(8,128)(2,1)S(1)} %fusion.10), channel_id=1, source_target_pairs={{0,2},{1,3},{2,0},{3,1},{4,6},{5,7},{6,4},{7,5},{8,10},{9,11},{10,... | collective-permute-start | bytes 2359304 | tf_op jit(solution)/shard_map/ppermute | solution.py:405
  256.8 18.9 %copy-start.3 = (bf16[512,1,768]{2,0,1:T(8,128)(2,1)S(1)}, bf16[512,1,768]{2,0,1:T(8,128)(2,1)}, u32[]{:S(2)}) copy-start(bf16[512,1,768]{2,0,1:T(8,128)(2,1)} %param.15) | copy-start | bytes 2359300
  256.8 5.7 %collective-permute-start.45 = (bf16[96,1536]{1,0:T(8,128)(2,1)S(1)}, bf16[96,1536]{1,0:T(8,128)(2,1)S(1)}, u32[]{:S(2)}, u32[]{:S(2)}) collective-permute-start(bf16[96,1536]{1,0:T(8,128)(2,1)S(1)} %get-tuple-element.70), channel_id=1, source_target_pairs={{16,8},{20,12},{24,16},{28,20},{17,9},{21,13},{25,17},{29,21},{18,... | collective-permute-start | bytes 884744 | tf_op jit(solution)/shard_map/ppermute | solution.py:496
  261.2 17.6 %collective-permute-start.43 = (bf16[96,1536]{1,0:T(8,128)(2,1)S(1)}, bf16[96,1536]{1,0:T(8,128)(2,1)S(1)}, u32[]{:S(2)}, u32[]{:S(2)}) collective-permute-start(bf16[96,1536]{1,0:T(8,128)(2,1)S(1)} %get-tuple-element.69), channel_id=1, source_target_pairs={{0,8},{4,12},{8,16},{12,20},{16,24},{20,28},{1,9},{5,13},{9,17},{1... | collective-permute-start | bytes 884744 | tf_op jit(solution)/shard_map/ppermute | solution.py:493
  262.6 16.2 %collective-permute-start.46 = (bf16[96,1536]{1,0:T(8,128)(2,1)S(1)}, bf16[96,1536]{1,0:T(8,128)(2,1)S(1)}, u32[]{:S(2)}, u32[]{:S(2)}) collective-permute-start(bf16[96,1536]{1,0:T(8,128)(2,1)S(1)} %fusion.15), channel_id=1, source_target_pairs={{8,0},{12,4},{16,8},{20,12},{24,16},{28,20},{9,1},{13,5},{17,9},{2... | collective-permute-start | bytes 884744 | tf_op jit(solution)/shard_map/ppermute | solution.py:496
  278.9 1.4 collective-permute-start.47
  280.4 5.3 %collective-permute-start.48 = (f32[96,256]{1,0:T(8,128)S(1)}, f32[96,256]{1,0:T(8,128)S(1)}, u32[]{:S(2)}, u32[]{:S(2)}) collective-permute-start(f32[96,256]{1,0:T(8,128)S(1)} %slice_add_fusion.1), channel_id=1, source_target_pairs={{0,2},{1,3},{2,0},{3,1},{4,6},{5,7},{6,4},{7,5},{8,10},{9,11},{10,... | collective-permute-start | bytes 294920 | tf_op jit(solution)/shard_map/ppermute | solution.py:405

commit v2 on v1

v2 whole, which is shorter than its diff:
```python
import functools

import jax
import jax.numpy as jnp
import numpy as np
from jax import lax
from jax.experimental import pallas as pl
from jax.experimental.pallas import tpu as pltpu
from jax.sharding import PartitionSpec as P

CONV = 4
SPAN = 256
LANES = 128
TAPS_AT = 8
GAIN_AT = 12
GATE_AT = 16
HEAD_AT = 64
epsilon = 1e-05
bf16 = jnp.bfloat16
f32 = jnp.float32
NN = (((1,), (0,)), ((), ()))
NT = (((1,), (1,)), ((), ()))
TN = (((0,), (0,)), ((), ()))


def mm(left, right, dims=NN):
    return lax.dot_general(left, right, dims, preferred_element_type=f32)


def split(values, parts):
    pieces = []
    for _ in range(parts):
        piece = values.astype(bf16)
        pieces.append(piece)
        values = values - piece.astype(f32)
    return pieces


def mm_left_exact(left, right, parts):
    return sum(mm(left, piece) for piece in split(right, parts))


def mm_right_exact(left, right, parts):
    return sum(mm(piece, right) for piece in split(left, parts))


def sigmoid(values):
    return 1.0 / (1.0 + jnp.exp(-values))


def softplus(values):
    return jnp.maximum(values, 0.0) + jnp.log1p(jnp.exp(-jnp.abs(values)))


def doc_start(position, ends):
    start = jnp.zeros_like(position)
    for end in ends:
        start = jnp.where(position >= end, end, start)
    return start


def scalar_start(position, ends):
    start = jnp.int32(0)
    for end in ends:
        start = jnp.where(position >= end, end, start)
    return start


def iota(shape, dim):
    return lax.broadcasted_iota(jnp.int32, shape, dim)


def tap_row(rows_ref, back, cols):
    at = TAPS_AT + CONV - 1 - back
    return rows_ref[at : at + 1, cols]


def conv_block(ext_ref, rows_ref, position, start, width):
    masks = [None] + [(position - k >= start).astype(f32) for k in range(1, CONV)]
    groups = []
    for at in range(0, width, LANES):
        cols = slice(at, at + LANES)
        total = ext_ref[8 : 8 + SPAN, cols] * tap_row(rows_ref, 0, cols)
        for k in range(1, CONV):
            total = total + ext_ref[8 - k : 8 - k + SPAN, cols] * masks[k] * (
                tap_row(rows_ref, k, cols)
            )
        groups.append(total)
    return jnp.concatenate(groups, axis=1)


def wide(mask, width):
    return jnp.concatenate([mask] * (width // LANES), axis=1)


def pick_piece(block, per_piece, mine, refs, chosen_ref):
    relative = (block // per_piece) ^ mine
    for k, ref in enumerate(refs):

        @pl.when(relative == k)
        def _(ref=ref):
            chosen_ref[...] = ref[...]


def forward_kernel(
    inner,
    state_count,
    heads,
    per_piece,
    pieces,
    info_ref,
    *refs,
):
    hidden_refs, refs = refs[:pieces], refs[pieces:]
    (
        weight_ref,
        choose_ref,
        chan_ref,
        head_ref,
        expand_ref,
        normed_ref,
        pre_ref,
        y_ref,
        cum_ref,
        entering_ref,
        rows_ref,
        ext_ref,
        state_ref,
        hidden_ref,
    ) = refs
    block = pl.program_id(0)
    conv_width = inner + 2 * state_count
    ends = [info_ref[k] for k in range(3)]
    base = block * SPAN

    @pl.when(block == 0)
    def _():
        ext_ref[...] = jnp.zeros_like(ext_ref)
        state_ref[...] = jnp.zeros_like(state_ref)
        rows_ref[...] = mm(weight_ref[:, conv_width:], choose_ref[...], TN)[0:16, :]

    pick_piece(block, per_piece, info_ref[3], hidden_refs, hidden_ref)
    residual = hidden_ref[...].astype(f32)
    row_scale = lax.rsqrt(jnp.mean(residual * residual, axis=1, keepdims=True) + epsilon)
    normed = (residual * row_scale * rows_ref[GAIN_AT : GAIN_AT + 1, conv_width:]).astype(bf16)
    normed_ref[...] = normed
    pre = mm(normed, weight_ref[...])
    pre_ref[...] = pre

    ext_ref[0:8, :] = ext_ref[SPAN : SPAN + 8, :]
    ext_ref[8 : 8 + SPAN, :] = pre[:, :conv_width]
    position = base + iota((SPAN, LANES), 0)
    start = doc_start(position, ends)
    conv = conv_block(ext_ref, rows_ref, position, start, conv_width)
    active = conv * sigmoid(conv)
    x_val = active[:, :inner].astype(bf16).astype(f32)
    in_map = active[:, inner : inner + state_count].astype(bf16)
    out_map = active[:, inner + state_count :].astype(bf16)

    step_size = softplus(pre[:, conv_width:] + head_ref[1:2, :])
    log_decay = step_size * head_ref[0:1, :]
    row_at = iota((SPAN, SPAN), 0)
    col_at = iota((SPAN, SPAN), 1)
    lower = (col_at <= row_at).astype(f32).astype(bf16)
    cum = mm_left_exact(lower, log_decay, 3)
    cum_ref[...] = cum
    cum_rows = cum.T

    start_last = scalar_start(base + SPAN - 1, ends)
    keep = (start < base).astype(f32)
    tail = (position >= start_last).astype(f32)
    survives = (start_last < base).astype(f32)
    expand = expand_ref[...]
    step_wide = mm_right_exact(step_size, expand, 2)
    decay_wide = mm_right_exact(jnp.exp(cum), expand, 2)
    into_wide = mm_right_exact(jnp.exp(cum[SPAN - 1 :, :] - cum) * tail, expand, 2)

    x_step = x_val * step_wide
    x_step_low = x_step.astype(bf16)
    state = state_ref[...]
    entering_ref[...] = state
    outside = mm(out_map, state.astype(bf16)) * (decay_wide * wide(keep, inner))
    visible = (col_at <= row_at) & (base + col_at >= wide(start, SPAN))
    scores = jnp.where(visible, mm(out_map, in_map, NT), 0.0)
    upper_half = iota((SPAN, LANES), 1) >= LANES // 2
    inside = []
    for pair in range(heads // 2):
        x_pair = x_step_low[:, pair * LANES : (pair + 1) * LANES]
        total = None
        for which in range(2):
            head = 2 * pair + which
            gap = cum[:, head : head + 1] - cum_rows[head : head + 1, :]
            mixing = (scores * jnp.exp(jnp.minimum(gap, 0.0))).astype(bf16)
            chosen = upper_half if which else jnp.logical_not(upper_half)
            part = mm(mixing, jnp.where(chosen, x_pair, jnp.zeros_like(x_pair)))
            total = part if total is None else total + part
        inside.append(total)
    y_val = jnp.concatenate(inside, axis=1) + outside + chan_ref[0:1, :] * x_val
    y_ref[...] = y_val

    scaled = (x_step * into_wide).astype(bf16)
    state_ref[...] = (decay_wide[SPAN - 1 :, :] * survives) * state + mm(in_map, scaled, TN)


def branch_kernel(per_piece, pieces, info_ref, *refs):
    grad_refs, refs = refs[:pieces], refs[pieces:]
    normed_ref, y_ref, gate_w_ref, out_ref, chan_ref = refs[:5]
    gate_ref, branch_ref, stats_ref, grad_ref = refs[5:]
    block = pl.program_id(0)
    pick_piece(block, per_piece, info_ref[3], grad_refs, grad_ref)
    gate = mm(normed_ref[...], gate_w_ref[...])
    gate_ref[...] = gate
    mixed = y_ref[...] * (gate * sigmoid(gate))
    out_w = out_ref[...]
    gain = chan_ref[1:2, :]
    branch_ref[...] = mm((mixed * gain).astype(bf16), out_w, NT).astype(bf16)
    weighted = mm(grad_ref[...], out_w) * gain
    squares = jnp.sum(mixed * mixed, axis=1, keepdims=True)
    crossed = jnp.sum(weighted * mixed, axis=1, keepdims=True)
    lane = iota((mixed.shape[0], LANES), 1)
    both = jnp.where(lane == 0, squares, jnp.where(lane == 1, crossed, 0.0))
    stats_ref[...] = both.T[0:8, :]


def product_sums(left, right):
    ones = jnp.ones((8, left.shape[1]), bf16)
    return sum(mm(ones, piece, NT) for piece in split(left * right.astype(f32), 3))


def gate_kernel(inner, inner_total, per_piece, pieces, info_ref, *refs):
    grad_refs, refs = refs[:pieces], refs[pieces:]
    (
        stats_ref,
        normed_ref,
        gate_w_ref,
        out_ref,
        gate_ref,
        y_ref,
        chan_ref,
        gate_grad_ref,
        y_grad_ref,
        early_ref,
        gain_grad_ref,
        product_ref,
        gate_acc,
        out_acc,
        grad_ref,
    ) = refs
    block = pl.program_id(0)

    @pl.when(block == 0)
    def _():
        gate_acc[...] = jnp.zeros_like(gate_acc)
        out_acc[...] = jnp.zeros_like(out_acc)
        gain_grad_ref[...] = jnp.zeros_like(gain_grad_ref)

    pick_piece(block, per_piece, info_ref[3], grad_refs, grad_ref)
    stats = stats_ref[...].T
    gate_scale = lax.rsqrt(stats[:, 0:1] / inner_total + epsilon)
    crossed = stats[:, 1:2] / inner_total
    gate = gate_ref[...]
    gate_sig = sigmoid(gate)
    gate_act = gate * gate_sig
    y_val = y_ref[...]
    mixed = y_val * gate_act
    grad = grad_ref[...]
    gain = chan_ref[1:2, :]
    gated_grad = mm(grad, out_ref[...])
    scaled_mixed = mixed * gate_scale
    out_acc[...] += mm(grad, (scaled_mixed * gain).astype(bf16), TN)
    gain_grad_ref[0:1, :] += jnp.sum(gated_grad * scaled_mixed, axis=0, keepdims=True)
    mixed_grad = gate_scale * (gated_grad * gain) - scaled_mixed * (
        gate_scale * gate_scale * crossed
    )
    gate_grad = mixed_grad * y_val * (gate_sig * (1.0 + gate * (1.0 - gate_sig)))
    gate_grad = gate_grad.astype(bf16)
    gate_grad_ref[...] = gate_grad
    y_grad_ref[...] = mixed_grad * gate_act
    gate_acc[...] += mm(normed_ref[...], gate_grad, TN)

    @pl.when(block == pl.num_programs(0) - 1)
    def _():
        early_ref[:, :inner] = gate_acc[...].astype(bf16)
        early_ref[:, inner:] = out_acc[...].astype(bf16)
        product_ref[...] = product_sums(gate_acc[...], gate_w_ref[...])


def backward_kernel(inner, state_count, heads, blocks, at, final, info_ref, *refs):
    (
        normed_ref,
        weight_ref,
        gate_w_ref,
        pre_ref,
        halo_ref,
        y_ref,
        y_grad_ref,
        gate_grad_ref,
        cum_ref,
        entering_ref,
        rows_ref,
        chan_ref,
        head_ref,
        expand_ref,
        gather_ref,
    ) = refs[:15]
    refs = refs[15:]
    if at:
        next_in, state_in, late_in, small_in, head_in, product_ref, choose_ref, extra_ref, _ = refs[:9]
        refs = refs[9:]
    total_ref = refs[0]
    if final:
        late_ref = refs[1]
        ext_ref, next_ref, pre_grad_ref, state_grad_ref, late_acc, small_ref, heads_ref = refs[2:]
    else:
        next_out, state_grad_ref, late_acc, small_ref, heads_ref = refs[1:6]
        ext_ref, next_ref, pre_grad_ref = refs[6:]
    step = pl.program_id(0)
    block = blocks - 1 - at - step
    base = block * SPAN
    conv_width = inner + 2 * state_count
    ends = [info_ref[k] for k in range(3)]

    @pl.when(step == 0)
    def _():
        if at:
            next_ref[0:8, :] = next_in[...]
            state_grad_ref[...] = state_in[...]
            late_acc[...] = late_in[...]
            small_ref[...] = small_in[...]
            heads_ref[...] = head_in[...]
        else:
            next_ref[...] = jnp.zeros_like(next_ref)
            state_grad_ref[...] = jnp.zeros_like(state_grad_ref)
            late_acc[...] = jnp.zeros_like(late_acc)
            small_ref[...] = jnp.zeros_like(small_ref)
            heads_ref[...] = jnp.zeros_like(heads_ref)

    skip = chan_ref[0:1, :]
    y_val = y_ref[...]
    y_grad = y_grad_ref[...]

    ext_ref[0:8, :] = halo_ref[:, :conv_width]
    ext_ref[8 : 8 + SPAN, :] = pre_ref[:, :conv_width]
    position = base + iota((SPAN, LANES), 0)
    start = doc_start(position, ends)
    conv = conv_block(ext_ref, rows_ref, position, start, conv_width)
    conv_sig = sigmoid(conv)
    active = conv * conv_sig
    act_slope = conv_sig * (1.0 + conv * (1.0 - conv_sig))
    x_val = active[:, :inner].astype(bf16).astype(f32)
    in_map = active[:, inner : inner + state_count].astype(bf16)
    out_map = active[:, inner + state_count :].astype(bf16)

    step_pre = pre_ref[:, conv_width:] + head_ref[1:2, :]
    step_size = softplus(step_pre)
    rates = head_ref[0:1, :]
    cum = cum_ref[...]
    cum_rows = cum.T
    start_last = scalar_start(base + SPAN - 1, ends)
    keep = (start < base).astype(f32)
    tail = (position >= start_last).astype(f32)
    survives = (start_last < base).astype(f32)
    expand = expand_ref[...]
    step_wide = mm_right_exact(step_size, expand, 2)
    decay_wide = mm_right_exact(jnp.exp(cum), expand, 2)
    into_wide = mm_right_exact(jnp.exp(cum[SPAN - 1 :, :] - cum) * tail, expand, 2)
    keep_decay = decay_wide * wide(keep, inner)
    last_decay = decay_wide[SPAN - 1 :, :] * survives

    x_step = x_val * step_wide
    x_step_low = x_step.astype(bf16)
    scaled = (x_step * into_wide).astype(bf16)
    entering = entering_ref[...]
    entering_low = entering.astype(bf16)
    y_grad_low = y_grad.astype(bf16)
    state_grad = state_grad_ref[...]
    state_grad_low = state_grad.astype(bf16)

    outside = mm(out_map, entering_low)
    outside_grad = (y_grad * keep_decay).astype(bf16)
    scaled_grad = mm(in_map, state_grad_low)
    out_map_grad = mm(outside_grad, entering_low, NT)
    in_map_grad = mm(scaled, state_grad_low, NT)
    state_grad_ref[...] = last_decay * state_grad + mm(out_map, outside_grad, TN)

    row_at = iota((SPAN, SPAN), 0)
    col_at = iota((SPAN, SPAN), 1)
    col_start = doc_start(base + col_at, ends)
    visible = (row_at <= col_at) & (base + row_at >= col_start)
    scores = jnp.where(visible, mm(in_map, out_map, NT), 0.0)
    upper_half = iota((SPAN, LANES), 1) >= LANES // 2
    score_grad = jnp.zeros((SPAN, SPAN), f32)
    x_step_grads = []
    for pair in range(heads // 2):
        x_pair = x_step_low[:, pair * LANES : (pair + 1) * LANES]
        grad_pair = y_grad_low[:, pair * LANES : (pair + 1) * LANES]
        total = None
        for which in range(2):
            head = 2 * pair + which
            chosen = upper_half if which else jnp.logical_not(upper_half)
            grad_head = jnp.where(chosen, grad_pair, jnp.zeros_like(grad_pair))
            gap = cum_rows[head : head + 1, :] - cum[:, head : head + 1]
            decays = jnp.exp(jnp.minimum(gap, 0.0))
            score_grad = score_grad + mm(x_pair, grad_head, NT) * decays
            part = mm((scores * decays).astype(bf16), grad_head)
            total = part if total is None else total + part
        x_step_grads.append(total)
    x_step_grad = jnp.concatenate(x_step_grads, axis=1)
    score_grad = jnp.where(visible, score_grad, 0.0).astype(bf16)
    in_map_grad = in_map_grad + mm(score_grad, out_map)
    out_map_grad = out_map_grad + mm(score_grad, in_map, TN)

    inside = y_val - skip * x_val - keep_decay * outside
    into_terms = scaled.astype(f32) * scaled_grad
    cum_terms = (
        y_grad_low.astype(f32) * inside
        + outside_grad.astype(f32) * outside
        - x_step_low.astype(f32) * x_step_grad
        - into_terms
    )
    last_terms = jnp.sum(into_terms, axis=0, keepdims=True) + last_decay * jnp.sum(
        state_grad * entering, axis=0, keepdims=True
    )
    last_row = iota((SPAN, inner), 0) == SPAN - 1
    cum_terms = cum_terms + jnp.where(last_row, last_terms, 0.0)
    x_step_grad = x_step_grad + into_wide * scaled_grad
    gather = gather_ref[...]
    cum_grad = mm_right_exact(cum_terms, gather, 2)
    step_grad = mm_right_exact(x_val * x_step_grad, gather, 2)
    upper = (row_at <= col_at).astype(f32).astype(bf16)
    log_grad = mm_left_exact(upper, cum_grad, 3)
    step_grad = (step_grad + log_grad * rates) * sigmoid(step_pre)
    pre_grad_ref[:, conv_width:] = step_grad.astype(bf16)
    x_grad = skip * y_grad + step_wide * x_step_grad

    heads_ref[0:1, :] += jnp.sum(y_grad * x_val, axis=0, keepdims=True)
    heads_ref[1:2, :LANES] += jnp.sum(step_size * rates * log_grad, axis=0, keepdims=True)
    heads_ref[2:3, :LANES] += jnp.sum(step_grad, axis=0, keepdims=True)

    conv_grad = jnp.concatenate([x_grad, in_map_grad, out_map_grad], axis=1) * act_slope
    next_ref[SPAN : SPAN + 8, :] = next_ref[0:8, :]
    next_ref[0:SPAN, :] = conv_grad
    back = [None] + [(position - k >= start).astype(f32) for k in range(1, CONV)]
    ahead = [None] + [
        (position >= doc_start(position + k, ends)).astype(f32) for k in range(1, CONV)
    ]
    for col in range(0, conv_width, LANES):
        cols = slice(col, col + LANES)
        grad_here = next_ref[0:SPAN, cols]
        total = grad_here * tap_row(rows_ref, 0, cols)
        small_ref[TAPS_AT + CONV - 1 : TAPS_AT + CONV, cols] += jnp.sum(
            grad_here * ext_ref[8 : 8 + SPAN, cols], axis=0, keepdims=True
        )
        for k in range(1, CONV):
            total = total + next_ref[k : k + SPAN, cols] * ahead[k] * (
                tap_row(rows_ref, k, cols)
            )
            small_ref[TAPS_AT + CONV - 1 - k : TAPS_AT + CONV - k, cols] += jnp.sum(
                grad_here * back[k] * ext_ref[8 - k : 8 - k + SPAN, cols], axis=0, keepdims=True
            )
        pre_grad_ref[:, cols] = total.astype(bf16)

    pre_grads = pre_grad_ref[...]
    total = mm(pre_grads, weight_ref[...], NT) + mm(gate_grad_ref[...], gate_w_ref[...], NT)
    total_ref[...] = total.astype(bf16)
    late_acc[...] += mm(normed_ref[...], pre_grads, TN)

    @pl.when(step == pl.num_programs(0) - 1)
    def _():
        if final:
            late = late_acc[...]
            sums = product_sums(late, weight_ref[...]) + product_ref[...]
            gain = rows_ref[GAIN_AT : GAIN_AT + 1, conv_width:]
            small_ref[GAIN_AT : GAIN_AT + 1, conv_width:] = sums[0:1, :] / gain
            chosen = small_ref[...].astype(bf16)
            filler = jnp.zeros((LANES - chosen.shape[0], chosen.shape[1]), bf16)
            misc = mm(choose_ref[...], jnp.concatenate([chosen, filler], axis=0), NT)
            totals = heads_ref[...]
            skips = mm_right_exact(totals, gather_ref[...], 2)
            per_head = [totals[1:2, :LANES], totals[2:3, :LANES], skips[0:1, :]]
            for at_head, value in enumerate(per_head):
                value = jnp.broadcast_to(value, (8, LANES))
                misc = misc + pltpu.roll(value, HEAD_AT + at_head * heads, 1)[0:1, :]
            late_ref[:, :conv_width] = late[:, :conv_width].astype(bf16)
            late_ref[:, conv_width:] = (late[:, conv_width:] + misc + extra_ref[...]).astype(bf16)
        else:
            next_out[...] = next_ref[0:8, :]


def swap(values, axis, bits):
    size = lax.axis_size(axis)
    return lax.ppermute(values, axis, [(i, i ^ bits) for i in range(size)])


def bits_of(size):
    return [1 << k for k in range(size.bit_length() - 1)]


def after(values, *others):
    return lax.optimization_barrier((values,) + others)[0]


def sum_over(values, axis):
    size = lax.axis_size(axis)
    if size > 8:
        for bit in bits_of(size):
            values = values + swap(values, axis, bit)
        return values
    return tree_sum([values] + [swap(values, axis, k) for k in range(1, size)])


def tree_sum(pieces):
    while len(pieces) > 1:
        pieces = [pieces[k] + pieces[k + 1] for k in range(0, len(pieces), 2)]
    return pieces[0]


def gather_far(values, axis):
    pieces = {0: values}
    bits = bits_of(lax.axis_size(axis))
    for bit in reversed(bits[1:]):
        pieces.update({k | bit: swap(piece, axis, bit) for k, piece in list(pieces.items())})
    pieces[1] = swap(values, axis, 1)
    return pieces


def gather_near(pieces, axis, *others):
    pieces = dict(pieces)
    for k in list(pieces):
        if k > 1:
            pieces[k | 1] = swap(after(pieces[k], *others) if others else pieces[k], axis, 1)
    return [pieces[k] for k in range(len(pieces))]


def scatter_near(pieces, axis):
    far = {}
    for k in range(len(pieces) - 2, 0, -2):
        both = pieces[k].astype(f32) + swap(pieces[k + 1], axis, 1).astype(f32)
        far[k] = both.astype(bf16)
    return far


def scatter_far(pieces, far, axis, parts=1):
    near = swap(after(pieces[1], *far.values()), axis, 1)
    received = None
    for bit in bits_of(lax.axis_size(axis))[1:]:
        if received is not None:
            far = {
                k: (v.astype(f32) + received[k].astype(f32)).astype(bf16) for k, v in far.items()
            }
        if parts > 1 and len(far) == 1:
            (last,) = far.values()
            size = last.shape[0] // parts
            cuts = [last[at : at + size] for at in range(0, last.shape[0], size)]
            return near, [swap(cut, axis, bit) for cut in cuts]
        received = {
            k ^ bit: swap(v, axis, bit) for k, v in far.items() if k & bit
        }
        far = {k: v for k, v in far.items() if not k & bit}
    return near, received[0] if parts == 1 else received


def gather_direct(values, axis, other):
    size = lax.axis_size(axis)
    place = lax.axis_index(axis)
    near = swap(values, axis, 1)
    far = [swap(values, axis, k) for k in range(size - 2, 0, -2)]
    far, other = lax.optimization_barrier((jnp.stack(far), other))
    beside = swap(far, axis, 1)
    result = jnp.zeros((size,) + values.shape, values.dtype)
    pieces = {0: values, 1: near}
    for at, k in enumerate(range(size - 2, 0, -2)):
        pieces.update({k: far[at], k + 1: beside[at]})
    for k in range(size):
        result = lax.dynamic_update_slice(
            result, pieces[k][None], (place ^ k,) + (0,) * values.ndim
        )
    return result.reshape((-1,) + values.shape[1:])


def gather_pairs(values, axis):
    size = lax.axis_size(axis)
    place = lax.axis_index(axis)
    other = swap(values, axis, 1)
    first = place % 2 == 0
    pair = jnp.stack([jnp.where(first, values, other), jnp.where(first, other, values)])
    result = jnp.zeros((size // 2,) + pair.shape, values.dtype)
    for k in range(0, size, 2):
        piece = swap(pair, axis, k) if k else pair
        result = lax.dynamic_update_slice(
            result, piece[None], ((place ^ k) // 2,) + (0,) * pair.ndim
        )
    return result.reshape((-1,) + values.shape[1:])


def block_of(values, place, share):
    return lax.dynamic_slice_in_dim(values, place * share, share, 0)


def fold_pairs(values, axis, steps):
    size = lax.axis_size(axis)
    place = lax.axis_index(axis)
    share = values.shape[0] // size
    theirs = jnp.stack([block_of(values, place ^ k ^ 1, share) for k in steps])
    return swap(theirs, axis, 1)


def fold_sums(values, theirs, axis, steps):
    place = lax.axis_index(axis)
    share = values.shape[0] // lax.axis_size(axis)
    sums = [
        block_of(values, place ^ k, share).astype(f32) + theirs[at].astype(f32)
        for at, k in enumerate(steps)
    ]
    return [both.astype(bf16) if k else both for k, both in zip(steps, sums)]


def send_sums(folded, axis, steps):
    return [
        swap(both, axis, k) if k else both for k, both in zip(steps, folded)
    ]


def per_device(
    hidden_rows,
    out_grad,
    doc_lengths,
    zx_weight,
    step_weight,
    bc_weight,
    conv_inner,
    conv_shared,
    out_weight,
    decay_log,
    step_bias,
    skip_gain,
    norm_gain,
    gate_gain,
):
    piece_len, _, width = hidden_rows.shape
    tensor = lax.axis_size("tensor")
    data = lax.axis_size("dp")
    full_len = piece_len * tensor
    blocks = full_len // SPAN
    per_piece = piece_len // SPAN
    share = zx_weight.shape[1]
    inner = zx_weight.shape[2]
    heads = step_weight.shape[1]
    head_dim = inner // heads
    state_count = bc_weight.shape[1] // 2
    conv_width = inner + 2 * state_count
    span = conv_width + LANES
    inner_total = float(inner * tensor)
    mine = lax.axis_index("tensor")
    place = lax.axis_index("dp")

    hidden = hidden_rows[:, 0, :]
    hidden_all = gather_far(hidden, "tensor")
    hidden_far = hidden_all[tensor // 2]
    hidden_all = gather_near(hidden_all, "tensor")

    inner_share = conv_inner.size // CONV
    shared_share = conv_shared.size // CONV
    taps = jnp.concatenate([conv_inner.reshape(-1, CONV), conv_shared.reshape(-1, CONV)])
    taps = jnp.pad(taps, ((0, share - inner_share - shared_share), (0, 0)))
    misc = jnp.concatenate(
        [
            jnp.pad(step_weight, ((0, 0), (0, TAPS_AT - heads))),
            taps,
            norm_gain[:, None],
            jnp.zeros((share, LANES - GAIN_AT - 1), bf16),
        ],
        axis=1,
    )
    shard = jnp.concatenate([zx_weight[1], bc_weight, misc], axis=1)
    weights = gather_direct(shard, "dp", hidden_far)
    shard = jnp.concatenate([zx_weight[0], out_weight.T], axis=1)
    weights_late = gather_pairs(shard, "dp")
    grad_all = gather_far(after(out_grad, hidden_far)[:, 0, :], "tensor")

    channel = np.arange(inner)
    per_dev = head_dim // data
    sources = [
        (channel % head_dim) // per_dev * share
        + channel // head_dim * per_dev
        + channel % per_dev,
        np.arange(2 * state_count) // shared_share * share
        + inner_share
        + np.arange(2 * state_count) % shared_share,
        np.arange(width),
    ]
    sources = jnp.asarray(np.concatenate(sources), jnp.int32)
    choose = (jnp.arange(width, dtype=jnp.int32)[:, None] == sources[None, :]).astype(bf16)
    chan = jnp.pad(jnp.stack([jnp.repeat(skip_gain, head_dim), gate_gain]), ((0, 6), (0, 0)))
    head_rows = jnp.pad(
        jnp.stack([-jnp.exp(decay_log), step_bias]), ((0, 6), (0, LANES - heads))
    )
    expand = (jnp.arange(LANES)[:, None] == jnp.arange(inner)[None, :] // head_dim).astype(bf16)
    gather = expand.T
    lengths = doc_lengths[0].astype(jnp.int32)
    info = jnp.stack(
        [lengths[0], lengths[0] + lengths[1], lengths[0] + lengths[1] + lengths[2], mine]
    ).astype(jnp.int32)

    limits = pltpu.CompilerParams(
        dimension_semantics=("arbitrary",), vmem_limit_bytes=56 * 1024 * 1024
    )
    shaped = jax.ShapeDtypeStruct

    def fixed(shape, at=0):
        return pl.BlockSpec(shape, lambda i, info: (0,) * (len(shape) - 1) + (at,))

    def rows(cols, at=0, order=lambda i: i):
        return pl.BlockSpec((SPAN, cols), lambda i, info: (order(i), at))

    def piece_specs(order=lambda i: i):
        return [
            pl.BlockSpec(
                (SPAN, width),
                lambda i, info, k=k: (
                    jnp.clip(order(i) - (info[3] ^ k) * per_piece, 0, per_piece - 1),
                    0,
                ),
            )
            for k in range(tensor)
        ]

    def call(
        kernel, name, micros, steps, in_specs, out_specs, out_shape, scratch, args, aliases={}
    ):
        return pl.pallas_call(
            kernel,
            grid_spec=pltpu.PrefetchScalarGridSpec(
                num_scalar_prefetch=1,
                grid=(steps,),
                in_specs=in_specs,
                out_specs=out_specs,
                scratch_shapes=scratch,
            ),
            out_shape=out_shape,
            compiler_params=limits,
            input_output_aliases=aliases,
            cost_estimate=pl.CostEstimate(
                flops=int(micros * 1.0e9), bytes_accessed=int(micros * 3.0e6), transcendentals=0
            ),
            name=name,
        )(info, *args)

    def relative(order):
        return pl.BlockSpec(
            (SPAN, width),
            lambda i, info: (
                ((order(i) // per_piece) ^ info[3]) * per_piece + order(i) % per_piece,
                0,
            ),
        )

    natural = lambda i: i
    state_spec = lambda order: pl.BlockSpec(
        (state_count, inner), lambda i, info: (order(i), 0)
    )
    normed, pre, y_val, cum, entering, rows_all = call(
        functools.partial(forward_kernel, inner, state_count, heads, per_piece, tensor),
        "forward",
        22,
        blocks,
        piece_specs()
        + [
            fixed((width, span)),
            fixed(choose.shape),
            fixed(chan.shape),
            fixed(head_rows.shape),
            fixed(expand.shape),
        ],
        [
            rows(width),
            rows(span),
            rows(inner),
            rows(LANES),
            state_spec(natural),
            fixed((16, conv_width + width)),
        ],
        [
            shaped((full_len, width), bf16),
            shaped((full_len, span), f32),
            shaped((full_len, inner), f32),
            shaped((full_len, LANES), f32),
            shaped((blocks * state_count, inner), f32),
            shaped((16, conv_width + width), f32),
        ],
        [
            pltpu.VMEM((SPAN + 8, conv_width), f32),
            pltpu.VMEM((state_count, inner), f32),
            pltpu.VMEM((SPAN, width), bf16),
        ],
        (*hidden_all, weights, choose, chan, head_rows, expand),
    )

    tall = lambda cols: pl.BlockSpec((piece_len, cols), lambda i, info: (i, 0))
    whole_pieces = [fixed((piece_len, width))] * tensor
    grad_all = gather_near(grad_all, "tensor", rows_all)
    gate_spec, out_spec = fixed((width, inner)), fixed((width, inner), 1)
    gate, branch, stats = call(
        functools.partial(branch_kernel, 1, tensor),
        "branch",
        11,
        tensor,
        whole_pieces + [tall(width), tall(inner), gate_spec, out_spec, fixed(chan.shape)],
        [tall(inner), pl.BlockSpec((piece_len, width), lambda i, info: (i ^ info[3], 0)), pl.BlockSpec((8, piece_len), lambda i, info: (0, i))],
        [
            shaped((full_len, inner), f32),
            shaped((full_len, width), bf16),
            shaped((8, full_len), f32),
        ],
        [pltpu.VMEM((piece_len, width), bf16)],
        (*grad_all, normed, y_val, weights_late, weights_late, chan),
    )

    cut = lambda values: [
        values[k * piece_len : (k + 1) * piece_len] for k in range(tensor)
    ]
    branch = cut(branch)
    branch_sums = scatter_near(branch, "tensor")
    stats = sum_over(stats, "tensor")

    gate_grad, y_grad, early, gain_grad, product = call(
        functools.partial(gate_kernel, inner, inner_total, 1, tensor),
        "gate_back",
        13,
        tensor,
        whole_pieces
        + [
            pl.BlockSpec((8, piece_len), lambda i, info: (0, i)),
            tall(width),
            gate_spec,
            out_spec,
            tall(inner),
            tall(inner),
            fixed(chan.shape),
        ],
        [
            tall(inner),
            tall(inner),
            fixed((width, 2 * inner)),
            fixed((8, inner)),
            fixed((8, width)),
        ],
        [
            shaped((full_len, inner), bf16),
            shaped((full_len, inner), f32),
            shaped((width, 2 * inner), bf16),
            shaped((8, inner), f32),
            shaped((8, width), f32),
        ],
        [
            pltpu.VMEM((width, inner), f32),
            pltpu.VMEM((width, inner), f32),
            pltpu.VMEM((piece_len, width), bf16),
        ],
        (*grad_all, stats, normed, weights_late, weights_late, gate, y_val, chan),
    )
    far_first = list(range(data - 2, -1, -2))
    early_theirs = fold_pairs(early, "dp", far_first)
    gate_grad, *held = lax.optimization_barrier(
        (gate_grad, *branch_sums.values())
    )
    branch_sums = dict(zip(branch_sums, held))
    branch_near, branch_far = scatter_far(branch, branch_sums, "tensor")

    small_width = conv_width + width
    half = blocks // 2
    carried = [
        shaped((8, conv_width), f32),
        shaped((state_count, inner), f32),
        shaped((width, span), f32),
        shaped((16, small_width), f32),
        shaped((8, inner), f32),
    ]

    def backward(at, steps, final, extra):
        back = lambda i: blocks - 1 - at - i
        back_rows = lambda cols: rows(cols, 0, back)
        extra_specs = [fixed(value.shape) for value in extra[:-1]]
        extra_specs += [pl.BlockSpec(memory_space=pl.ANY)] * len(extra[-1:])
        outs = [shaped((width, span), bf16)] if final else carried
        scratch = [
            pltpu.VMEM((SPAN + 8, conv_width), f32),
            pltpu.VMEM((SPAN + 8, conv_width), f32),
            pltpu.VMEM((SPAN, span), bf16),
        ]
        if final:
            scratch += [pltpu.VMEM(value.shape, f32) for value in carried[1:]]
        return call(
            functools.partial(backward_kernel, inner, state_count, heads, blocks, at, final),
            "backward",
            23,
            steps,
            [
                back_rows(width),
                fixed((width, span)),
                gate_spec,
                back_rows(span),
                pl.BlockSpec(
                    (8, span), lambda i, info: (jnp.maximum(back(i) * (SPAN // 8) - 1, 0), 0)
                ),
                back_rows(inner),
                back_rows(inner),
                back_rows(inner),
                back_rows(LANES),
                state_spec(back),
                fixed((16, small_width)),
                fixed(chan.shape),
                fixed(head_rows.shape),
                fixed(expand.shape),
                fixed(gather.shape),
            ]
            + extra_specs,
            [relative(back)] + [fixed(out.shape) for out in outs],
            [shaped((full_len, width), bf16)] + outs,
            scratch,
            (
                normed,
                weights,
                weights_late,
                pre,
                pre,
                y_val,
                y_grad,
                gate_grad,
                cum,
                entering,
                rows_all,
                chan,
                head_rows,
                expand,
                gather,
                *extra,
            ),
            {24: 0} if extra else {},
        )

    total, next_rows, *rest = backward(0, half, False, ())
    next_rows, early_theirs, branch_near, branch_far = lax.optimization_barrier(
        (next_rows, early_theirs, branch_near, branch_far)
    )
    early_pieces = send_sums(
        fold_sums(early, early_theirs, "dp", far_first), "dp", far_first
    )
    gate_lanes = inner // share
    extra = jnp.tile(gain_grad[0].reshape(gate_lanes, share).T, (data, 1))
    extra = jnp.pad(extra, ((0, 0), (GATE_AT, LANES - GATE_AT - gate_lanes)))
    total, late = backward(
        half, blocks - half, True, (next_rows, *rest, product, choose, extra, total)
    )

    total, late, *early_pieces = lax.optimization_barrier((total, late, *early_pieces))
    total = cut(total)
    total_sums = scatter_near(total, "tensor")
    groups = far_first[: len(far_first) // 2], far_first[len(far_first) // 2 :]
    theirs = [fold_pairs(late, "dp", steps) for steps in groups]
    total_near, total_far = scatter_far(total, total_sums, "tensor")
    theirs[0] = after(theirs[0], *total_sums.values())
    folded = fold_sums(late, theirs[0], "dp", groups[0])
    theirs[1] = after(theirs[1], total_far, *folded)
    folded += fold_sums(late, theirs[1], "dp", groups[1])
    branch_far, *held = lax.optimization_barrier((branch_far, *early_pieces, folded[0]))
    early_pieces = held[: len(early_pieces)]
    late_part = tree_sum([piece.astype(f32) for piece in send_sums(folded, "dp", far_first)])
    late_part, total_far = lax.optimization_barrier((late_part, total_far))
    normed_grad = (
        total[0].astype(f32) + total_near.astype(f32) + total_far.astype(f32)
    )
    early_part = tree_sum([piece.astype(f32) for piece in early_pieces])
    misc_part = late_part[:, conv_width:]
    shared_part = sum_over(late_part[:, inner:], "tensor")
    bc_part, misc_shared = shared_part[:, : 2 * state_count], shared_part[:, 2 * state_count :]

    residual = hidden.astype(f32)
    gate_scale = lax.rsqrt(
        lax.dynamic_slice_in_dim(stats[0], mine * piece_len, piece_len) / inner_total + epsilon
    )
    branch_local = (
        branch[0].astype(f32) + branch_near.astype(f32) + branch_far.astype(f32)
    )
    block_out = (residual + branch_local * gate_scale[:, None]).astype(bf16)
    row_scale = lax.rsqrt(jnp.mean(residual * residual, axis=1, keepdims=True) + epsilon)
    scaled_grad = normed_grad * rows_all[GAIN_AT : GAIN_AT + 1, conv_width:]
    hidden_grad = row_scale * scaled_grad - residual * row_scale**3 * jnp.mean(
        scaled_grad * residual, axis=1, keepdims=True
    )
    hidden_grad = (hidden_grad + grad_all[0].astype(f32)).astype(bf16)

    taps_at = slice(TAPS_AT, TAPS_AT + CONV)
    head_values = misc_part[0, HEAD_AT : HEAD_AT + 3 * heads]
    return (
        block_out[:, None, :],
        hidden_grad[:, None, :],
        jnp.stack([early_part[:, :inner], late_part[:, :inner]]),
        misc_part[:, :heads],
        bc_part,
        misc_part[:inner_share, taps_at].reshape(conv_inner.shape),
        misc_shared[inner_share : inner_share + shared_share, taps_at].reshape(-1),
        early_part[:, inner:].T,
        head_values[:heads],
        head_values[heads : 2 * heads],
        head_values[2 * heads :],
        misc_shared[:, GAIN_AT],
        misc_part[:, GATE_AT : GATE_AT + gate_lanes].T.reshape(-1),
    )


def solution(mesh):
    in_specs = (
        P("tensor", "dp", None),
        P("tensor", "dp", None),
        P("dp", None),
        P(None, "dp", "tensor"),
        P("dp", "tensor"),
        P("dp", None),
        P("tensor", "dp"),
        P("dp"),
        P("tensor", "dp"),
        P("tensor"),
        P("tensor"),
        P("tensor"),
        P("dp"),
        P("tensor"),
    )
    out_specs = (
        P("tensor", "dp", None),
        P("tensor", "dp", None),
        P(None, "dp", "tensor"),
        P("dp", "tensor"),
        P("dp", None),
        P("tensor", "dp"),
        P("dp"),
        P("tensor", "dp"),
        P("tensor"),
        P("tensor"),
        P("tensor"),
        P("dp"),
        P("tensor"),
    )
    return jax.shard_map(
        per_device, mesh=mesh, in_specs=in_specs, out_specs=out_specs, check_vma=False
    )
```

time: 288 us -> 215 us (0.75)
  waiting for transfers between devices: 73.3 us -> 32.9 us
  starting transfers between devices: 71.5 us -> 36.6 us
  Pallas kernels: 80.4 us -> 93.9 us
  other arithmetic: 29.2 us -> 20.9 us
  local copies, waits for them, and re-layouts: 30.4 us -> 26.2 us
    ppermute x54 -> x36, waiting for transfers between devices: 73.3 us -> 32.9 us  [swap(): return lax.ppermute(values, axis, [(i, i ^ bits) for i in range(size)])]
    ppermute x54 -> x36, starting transfers between devices: 71.5 us -> 36.6 us  [swap(): return lax.ppermute(values, axis, [(i, i ^ bits) for i in range(size)])]
    pallas_call x3 -> x5, Pallas kernels: 80.4 us -> 93.9 us  [call(): pl.pallas_call(kernel, grid_spec=pltpu.PrefetchScalarGridSpec(num_scalar_...]
    squeeze x5 -> x1, local copies, waits for them, and re-layouts: 7.89 us -> 0.94 us  [per_device(): shard = jnp.concatenate([zx_weight[0], out_weight.T], axis=1)]
    slice x11 -> x12, local copies, waits for them, and re-layouts: 3.09 us -> 9.85 us  [the longest x2 4.26 us: per_device(): values[k * piece_len:(k + 1) * piece_len]]
    another operation x4 -> x8, other arithmetic: 6.49 us -> 3.14 us  [the longest x1 1.64 us: per_device(): jnp.stack([early_part[:, :inner], late_part[:, :inner]])]
    convert_element_type x8 -> x7, other arithmetic: 9.67 us -> 7.08 us  [the longest x1 2.9 us: per_device(): (jnp.arange(width, dtype=jnp.int32)[:, None] == sources[None, :]).astype(...]
    unnamed x16 -> x61, local copies, waits for them, and re-layouts: 6.65 us -> 5.16 us
  transfers between devices with their start and end apart: 54 -> 36, of which waited for: 19 -> 9; matrix products, arithmetic and copies ran while one was open for 17% -> 14% of each run, Pallas kernels for 17% -> 39%
where the time goes in v2:
time: 215 us; the launch traced here: 214 us
  Pallas kernels  93.9 us (44%)
  starting transfers between devices  36.6 us (17%)
  waiting for transfers between devices  32.9 us (15%)
  local copies, waits for them, and re-layouts  26.2 us (12%)
  other arithmetic  20.9 us (10%)
  between operations  3.33 us (2%)
    pallas_call x5, Pallas kernels, call(): pl.pallas_call(kernel, grid_spec=pltpu.PrefetchScalarGridSpec(num_scalar_...  93.9 us
    ppermute x36, starting transfers between devices, swap(): return lax.ppermute(values, axis, [(i, i ^ bits) for i in range(size)])  36.6 us
    ppermute x36, waiting for transfers between devices, swap(): return lax.ppermute(values, axis, [(i, i ^ bits) for i in range(size)])  32.9 us
    unnamed x61, local copies, waits for them, and re-layouts  5.16 us
  transfers between devices with their start and end apart: 36, of which 9 were waited for; matrix products, arithmetic and copies ran while one was open for 14% of the time, Pallas kernels for 39%

profile of v2, /device:TPU:0, one launch (start us, length us, event | category | flops | bytes accessed | tf_op | source)
XLA Modules:
  0.0 213.8 jit_solution(3108935084521582709)
XLA Ops:
  0.6 0.8 reshape.150
  1.5 0.8 reshape.149
  2.6 0.8 copy.46
  3.4 0.8 copy.42
  4.2 0.9 slice_bitcast_fusion.3
  5.1 0.9 concatenate.10
  6.1 3.1 %collective-permute-start.8 = (bf16[96,768]{1,0:T(8,128)(2,1)S(1)}, bf16[96,768]{1,0:T(8,128)(2,1)S(1)}, u32[]{:S(2)}, u32[]{:S(2)}) collective-permute-start(bf16[96,768]{1,0:T(8,128)(2,1)S(1)} %concatenate.10), channel_id=1, source_target_pairs={{0,8},{4,12},{8,0},{12,4},{16,24},{20,28},{24,16},{28,20},{1,9},{5... | collective-permute-start | bytes 442376 | tf_op jit(solution)/shard_map/ppermute | solution.py:492
  9.1 2.6 %collective-permute-start.7 = (bf16[96,768]{1,0:T(8,128)(2,1)S(1)}, bf16[96,768]{1,0:T(8,128)(2,1)S(1)}, u32[]{:S(2)}, u32[]{:S(2)}) collective-permute-start(bf16[96,768]{1,0:T(8,128)(2,1)S(1)} %concatenate.10), channel_id=1, source_target_pairs={{0,16},{4,20},{8,24},{12,28},{16,0},{20,4},{24,8},{28,12},{1,17},{... | collective-permute-start | bytes 442376 | tf_op jit(solution)/shard_map/ppermute | solution.py:492
  11.7 0.9 pad_maximum_fusion.6
  12.6 1.8 collective-permute-start.11
  14.4 1.5 collective-permute-start
  15.9 0.7 fusion.18.refs_8_.refs_13_
  16.6 0.8 fusion.19.refs_14_
  18.0 1.4 fusion.28
  19.4 2.9 %fusion.refs_5_.refs_21_ = bf16[768,1408]{1,0:T(8,128)(2,1)} fusion(s32[1408]{0:T(1024)} %constant.111.clone), kind=kLoop, calls=%fused_computation.1 | loop fusion | flops 2162688 | bytes 2168320 | tf_op jit(solution)/shard_map/convert_element_type | solution.py:693
  25.0 1.2 pad_add_fusion.info_ref
  27.8 1.8 collective-permute-start.13
  29.5 2.5 %collective-permute-start.12 = (bf16[2,96,768]{2,1,0:T(8,128)(2,1)S(1)}, bf16[2,96,768]{2,1,0:T(8,128)(2,1)S(1)}, u32[]{:S(2)}, u32[]{:S(2)}) collective-permute-start(bf16[2,96,768]{2,1,0:T(8,128)(2,1)S(1)} %pad_maximum_fusion.2), channel_id=1, source_target_pairs={{0,8},{4,12},{8,0},{12,4},{16,24},{20,28},{24,16},{28,20},{1,9},{5... | collective-permute-start | bytes 884744 | tf_op jit(solution)/shard_map/ppermute | solution.py:492
  32.1 0.9 collective-permute-done.refs_2_
  33.0 3.5 %collective-permute-start.14 = (bf16[2,96,768]{2,1,0:T(8,128)(2,1)S(1)}, bf16[2,96,768]{2,1,0:T(8,128)(2,1)S(1)}, u32[]{:S(2)}, u32[]{:S(2)}) collective-permute-start(bf16[2,96,768]{2,1,0:T(8,128)(2,1)S(1)} %pad_maximum_fusion.2), channel_id=1, source_target_pairs={{0,24},{4,28},{8,16},{12,20},{16,8},{20,12},{24,0},{28,4},{1,25},{... | collective-permute-start | bytes 884744 | tf_op jit(solution)/shard_map/ppermute | solution.py:492
  37.1 9.0 %collective-permute-done.9 = bf16[3,96,768]{2,1,0:T(8,128)(2,1)S(1)} collective-permute-done((bf16[3,96,768]{2,1,0:T(8,128)(2,1)S(1)}, bf16[3,96,768]{2,1,0:T(8,128)(2,1)S(1)}, u32[]{:S(2)}, u32[]{:S(2)}) %collective-permute-start.9) | collective-permute-done | bytes 442400 | tf_op jit(solution)/shard_map/ppermute | solution.py:492
  46.3 0.9 copy-done.26
  47.2 1.5 collective-permute-start.2
  49.6 22.5 %forward.1 = (bf16[2048,768]{1,0:T(8,128)(2,1)}, f32[2048,768]{1,0:T(8,128)}, f32[2048,384]{1,0:T(8,128)}, f32[2048,128]{1,0:T(8,128)}, f32[1024,384]{1,0:T(8,128)}, /*index=5*/f32[16,1408]{1,0:T(8,128)}) custom-call(s32[4]{0:T(128)} %pad_add_fusion.info_ref, bf16[512,768]{1,0:T(8,128)(2,1)} %bitcast.103, bf16[512,768]{1,0:T(8,128)(2,1)} %copy-done.26, ...), custom_call_target="tpu_custom_call" | custom-call | flops 22000001024 | bytes 66000000 | tf_op jit(solution)/shard_map/forward/pallas_call | solution.py:731
  73.0 1.5 collective-permute-done.10.refs_3_
  74.5 0.9 copy-done.27
  75.4 11.2 %branch.1 = (f32[2048,384]{1,0:T(8,128)}, bf16[2048,768]{1,0:T(8,128)(2,1)}, f32[8,2048]{1,0:T(8,128)}) custom-call(s32[4]{0:T(128)} %pad_add_fusion.info_ref, bf16[512,768]{1,0:T(8,128)(2,1)} %bitcast.115, bf16[512,768]{1,0:T(8,128)(2,1)} %copy-done.25, bf16[512,768]{1,0:T(8,128)(2,1)} %copy-done.24, bf16[512,768]{1,0:T(8,128)(2,1)} %copy-done.27, ...), custom_call_target="tpu_custom_call" | custom-call | flops 11000000512 | bytes 33000000 | tf_op jit(solution)/shard_map/branch/pallas_call | solution.py:731
  86.6 1.1 collective-permute-start.17
  87.7 0.8 collective-permute-start.16
  88.5 1.5 fusion.27
  90.7 1.9 collective-permute-done.16
  93.2 13.5 %gate_back.1 = (bf16[2048,384]{1,0:T(8,128)(2,1)}, f32[2048,384]{1,0:T(8,128)}, bf16[768,768]{1,0:T(8,128)(2,1)}, f32[8,384]{1,0:T(8,128)}, f32[8,768]{1,0:T(8,128)}) custom-call(s32[4]{0:T(128)} %pad_add_fusion.info_ref, bf16[512,768]{1,0:T(8,128)(2,1)} %bitcast.116, bf16[512,768]{1,0:T(8,128)(2,1)} %copy-done.25, bf16[512,768]{1,0:T(8,128)(2,1)} %copy-done.24, ...), custom_call_target="tpu_custom_call" | custom-call | flops 12999999488 | bytes 39000000 | tf_op jit(solution)/shard_map/gate_back/pallas_call | solution.py:731
  106.7 0.7 slice_reduce_fusion.2
  107.6 1.2 dynamic-slice_bitcast_fusion.7
  109.5 0.9 pad.24.refs_22_
  110.4 1.3 add_convert_fusion.1
  111.7 1.5 collective-permute-start.21
  113.2 22.1 %backward.2 = (bf16[2048,768]{1,0:T(8,128)(2,1)}, f32[8,640]{1,0:T(8,128)}, f32[128,384]{1,0:T(8,128)}, f32[768,768]{1,0:T(8,128)}, f32[16,1408]{1,0:T(8,128)}, /*index=5*/f32[8,384]{1,0:T(8,128)}) custom-call(s32[4]{0:T(128)} %pad_add_fusion.info_ref, bf16[2048,768]{1,0:T(8,128)(2,1)} %get-tuple-element.65.refs_4_.refs_5_.refs_0_, ...), custom_call_target="tpu_custom_call" | custom-call | flops 23000000512 | bytes 69000000 | tf_op jit(solution)/shard_map/backward/pallas_call | solution.py:731
  135.6 2.2 %collective-permute-start.23 = (bf16[96,768]{1,0:T(8,128)(2,1)S(1)}, bf16[96,768]{1,0:T(8,128)(2,1)S(1)}, u32[]{:S(2)}, u32[]{:S(2)}) collective-permute-start(bf16[96,768]{1,0:T(8,128)(2,1)S(1)} %get-tuple-element.156), channel_id=1, source_target_pairs={{0,16},{4,20},{8,24},{12,28},{16,0},{20,4},{24,8},{28,12},{1,17},{... | collective-permute-start | bytes 442376 | tf_op jit(solution)/shard_map/ppermute | solution.py:492
  137.8 2.1 %collective-permute-start.22 = (bf16[96,768]{1,0:T(8,128)(2,1)S(1)}, bf16[96,768]{1,0:T(8,128)(2,1)S(1)}, u32[]{:S(2)}, u32[]{:S(2)}) collective-permute-start(bf16[96,768]{1,0:T(8,128)(2,1)S(1)} %get-tuple-element.157), channel_id=1, source_target_pairs={{0,24},{4,28},{8,16},{12,20},{16,8},{20,12},{24,0},{28,4},{1,25},{... | collective-permute-start | bytes 442376 | tf_op jit(solution)/shard_map/ppermute | solution.py:492
  139.9 24.6 %backward.3 = (bf16[2048,768]{1,0:T(8,128)(2,1)}, bf16[768,768]{1,0:T(8,128)(2,1)}) custom-call(s32[4]{0:T(128)} %pad_add_fusion.info_ref, bf16[2048,768]{1,0:T(8,128)(2,1)} %get-tuple-element.65.refs_4_.refs_5_.refs_0_, bf16[768,768]{1,0:T(8,128)(2,1)} %bitcast.114, bf16[768,768]{1,0:T(8,128)(2,1)} %bitcast.111, ...), custom_call_target="tpu_custom_call", output_to_operand_aliasing={{0}: (24, {})} | custom-call | flops 23000000512 | bytes 69000000 | tf_op jit(solution)/shard_map/backward/pallas_call | solution.py:731
  165.4 2.8 %fusion.26 = (bf16[512,768]{1,0:T(8,128)(2,1)}, bf16[512,768]{1,0:T(8,128)(2,1)}) fusion(bf16[2048,768]{1,0:T(8,128)(2,1)} %get-tuple-element.98), kind=kLoop, calls=%fused_computation.104 | loop fusion | bytes 3145728 | tf_op jit(solution)/shard_map/slice | solution.py:820
  168.1 1.2 dynamic-slice_bitcast_fusion.1
  169.4 1.6 collective-permute-start.25
  171.0 1.3 add_convert_fusion
  172.3 0.7 collective-permute-start.31
  173.0 0.8 slice_reduce_fusion.1
  173.8 1.4 collective-permute-start.30
  175.2 4.1 %collective-permute-done.25 = bf16[2,96,768]{2,1,0:T(8,128)(2,1)S(1)} collective-permute-done((bf16[2,96,768]{2,1,0:T(8,128)(2,1)S(1)}, bf16[2,96,768]{2,1,0:T(8,128)(2,1)S(1)}, u32[]{:S(2)}, u32[]{:S(2)}) %collective-permute-start.25) | collective-permute-done | bytes 294944 | tf_op jit(solution)/shard_map/ppermute | solution.py:492
  179.3 1.8 collective-permute-start.28
  181.2 4.0 %collective-permute-done.30 = bf16[2,96,768]{2,1,0:T(8,128)(2,1)S(1)} collective-permute-done((bf16[2,96,768]{2,1,0:T(8,128)(2,1)S(1)}, bf16[2,96,768]{2,1,0:T(8,128)(2,1)S(1)}, u32[]{:S(2)}, u32[]{:S(2)}) %collective-permute-start.30) | collective-permute-done | bytes 294944 | tf_op jit(solution)/shard_map/ppermute | solution.py:492
  185.2 6.9 %collective-permute-done.31 = bf16[512,768]{1,0:T(8,128)(2,1)} collective-permute-done((bf16[512,768]{1,0:T(8,128)(2,1)S(1)}, bf16[512,768]{1,0:T(8,128)(2,1)}, u32[]{:S(2)}, u32[]{:S(2)}) %collective-permute-start.31) | collective-permute-done | bytes 786464 | tf_op jit(solution)/shard_map/ppermute | solution.py:492
  192.2 0.7 slice_bitcast_fusion
  193.0 4.4 %collective-permute-done.32 = bf16[96,768]{1,0:T(8,128)(2,1)S(1)} collective-permute-done((bf16[96,768]{1,0:T(8,128)(2,1)S(1)}, bf16[96,768]{1,0:T(8,128)(2,1)S(1)}, u32[]{:S(2)}, u32[]{:S(2)}) %collective-permute-start.32) | collective-permute-done | bytes 147488 | tf_op jit(solution)/shard_map/ppermute | solution.py:492
  197.6 0.7 slice.192
  198.9 1.5 collective-permute-start.33
  200.4 0.7 reshape.153
  201.2 0.7 reshape.155
  201.9 0.7 copy.45
  202.6 2.4 %fusion.2 = (f32[512]{0:T(512)S(1)}, f32[512]{0:T(512)S(1)}) fusion(bf16[512,1,768]{2,0,1:T(8,128)(2,1)} %param.15, f32[768]{0:T(1024)S(1)} %slice_reduce_fusion.1, bf16[512,768]{1,0:T(8,128)(2,1)} %collective-permute-done.31, bf16[512,768]{1,0:T(8,128)(2,1)} %collective-permute-done.27, bf16[2048,768]{1,0:T(8,128)(2,1)S(1)} %copy-done), kind=kLoop, calls=%fused_computation.7 | loop fusion | flops 4324352 | bytes 3152896 | tf_op jit(solution)/shard_map/reduce_sum | solution.py:986
  205.1 3.4 %fusion.8 = (bf16[512,1,768]{2,0,1:T(8,128)(2,1)}, bf16[512,1,768]{2,0,1:T(8,128)(2,1)}) fusion(bf16[512,768]{1,0:T(8,128)(2,1)} %collective-permute-done.31, bf16[512,768]{1,0:T(8,128)(2,1)} %collective-permute-done.27, f32[512]{0:T(512)S(1)} %get-tuple-element.186, f32[512]{0:T(512)S(1)} %get-tuple-element.182, f32[768]{0:T(1024)S(1)} %slice_reduce_fusion.1, ...), kind=kLoop, calls=%fused_computation.16 | loop fusion | flops 8650752 | bytes 7875584 | tf_op jit(solution)/shard_map/broadcast_in_dim | solution.py:997
  209.1 1.1 add_add_fusion.1
  210.2 0.7 slice_reduce_fusion
  212.2 1.6 pad_maximum_fusion.5
  (157 shorter events, 12.1 us)
Async XLA Ops:
  6.1 21.6 %collective-permute-start.8 = (bf16[96,768]{1,0:T(8,128)(2,1)S(1)}, bf16[96,768]{1,0:T(8,128)(2,1)S(1)}, u32[]{:S(2)}, u32[]{:S(2)}) collective-permute-start(bf16[96,768]{1,0:T(8,128)(2,1)S(1)} %concatenate.10), channel_id=1, source_target_pairs={{0,8},{4,12},{8,0},{12,4},{16,24},{20,28},{24,16},{28,20},{1,9},{5... | collective-permute-start | bytes 442376 | tf_op jit(solution)/shard_map/ppermute | solution.py:492
  9.1 18.6 %collective-permute-start.7 = (bf16[96,768]{1,0:T(8,128)(2,1)S(1)}, bf16[96,768]{1,0:T(8,128)(2,1)S(1)}, u32[]{:S(2)}, u32[]{:S(2)}) collective-permute-start(bf16[96,768]{1,0:T(8,128)(2,1)S(1)} %concatenate.10), channel_id=1, source_target_pairs={{0,16},{4,20},{8,24},{12,28},{16,0},{20,4},{24,8},{28,12},{1,17},{... | collective-permute-start | bytes 442376 | tf_op jit(solution)/shard_map/ppermute | solution.py:492
  11.7 17.8 %collective-permute-start.6 = (bf16[96,768]{1,0:T(8,128)(2,1)S(1)}, bf16[96,768]{1,0:T(8,128)(2,1)S(1)}, u32[]{:S(2)}, u32[]{:S(2)}) collective-permute-start(bf16[96,768]{1,0:T(8,128)(2,1)S(1)} %concatenate.10), channel_id=1, source_target_pairs={{0,24},{4,28},{8,16},{12,20},{16,8},{20,12},{24,0},{28,4},{1,25},{... | collective-permute-start | bytes 442376 | tf_op jit(solution)/shard_map/ppermute | solution.py:492
  12.6 14.4 %collective-permute-start.11 = (bf16[96,768]{1,0:T(8,128)(2,1)S(1)}, bf16[96,768]{1,0:T(8,128)(2,1)S(1)}, u32[]{:S(2)}, u32[]{:S(2)}) collective-permute-start(bf16[96,768]{1,0:T(8,128)(2,1)S(1)} %pad_maximum_fusion.6), channel_id=1, source_target_pairs={{0,4},{4,0},{8,12},{12,8},{16,20},{20,16},{24,28},{28,24},{1,5},{5... | collective-permute-start | bytes 442376 | tf_op jit(solution)/shard_map/ppermute | solution.py:492
  14.4 18.5 %collective-permute-start = (bf16[512,768]{1,0:T(8,128)(2,1)}, bf16[512,768]{1,0:T(8,128)(2,1)}, u32[]{:S(2)}, u32[]{:S(2)}) collective-permute-start(bf16[512,768]{1,0:T(8,128)(2,1)} %bitcast.102), channel_id=1, source_target_pairs={{0,2},{1,3},{2,0},{3,1},{4,6},{5,7},{6,4},{7,5},{8,10},{9,11},{10,... | collective-permute-start | bytes 2359304 | tf_op jit(solution)/shard_map/ppermute | solution.py:492
  19.4 5.1 %copy-start.22 = (f32[6]{0:T(128)S(1)}, f32[6]{0:T(128)}, u32[]{:S(2)}) copy-start(f32[6]{0:T(128)} %param.25) | copy-start | bytes 76
  19.4 6.9 %copy-start.21 = (f32[384]{0:T(512)S(1)}, f32[384]{0:T(512)}, u32[]{:S(2)}) copy-start(f32[384]{0:T(512)} %param.28) | copy-start | bytes 4612
  19.4 6.9 %copy-start.23 = (f32[6]{0:T(128)S(1)}, f32[6]{0:T(128)}, u32[]{:S(2)}) copy-start(f32[6]{0:T(128)} %param.26) | copy-start | bytes 76
  19.4 8.2 %copy-start.13 = (bf16[384,96]{0,1:T(8,128)(2,1)S(1)}, bf16[384,96]{0,1:T(8,128)(2,1)}, u32[]{:S(2)}) copy-start(bf16[384,96]{0,1:T(8,128)(2,1)} %param.23) | copy-start | bytes 221188
  22.3 5.4 %copy-start.1 = (bf16[512,1,768]{2,0,1:T(8,128)(2,1)S(1)}, bf16[512,1,768]{2,0,1:T(8,128)(2,1)}, u32[]{:S(2)}) copy-start(bf16[512,1,768]{2,0,1:T(8,128)(2,1)} %param.15) | copy-start | bytes 2359300
  27.0 9.5 %collective-permute-start.5 = (bf16[96,768]{1,0:T(8,128)(2,1)S(1)}, bf16[96,768]{1,0:T(8,128)(2,1)S(1)}, u32[]{:S(2)}, u32[]{:S(2)}) collective-permute-start(bf16[96,768]{1,0:T(8,128)(2,1)S(1)} %concatenate.10), channel_id=1, source_target_pairs={{0,4},{4,0},{8,12},{12,8},{16,20},{20,16},{24,28},{28,24},{1,5},{5... | collective-permute-start | bytes 442376 | tf_op jit(solution)/shard_map/ppermute | solution.py:492
  27.7 19.5 %copy-start.7 = (bf16[512,1,768]{2,0,1:T(8,128)(2,1)S(1)}, bf16[512,1,768]{2,0,1:T(8,128)(2,1)}, u32[]{:S(2)}) copy-start(bf16[512,1,768]{2,0,1:T(8,128)(2,1)} %param.16) | copy-start | bytes 2359300
  27.7 18.6 %collective-permute-start.3 = (bf16[512,768]{1,0:T(8,128)(2,1)S(1)}, bf16[512,768]{1,0:T(8,128)(2,1)S(1)}, u32[]{:S(2)}, u32[]{:S(2)}) collective-permute-start(bf16[512,768]{1,0:T(8,128)(2,1)S(1)} %bitcast.104), channel_id=1, source_target_pairs={{0,1},{1,0},{2,3},{3,2},{4,5},{5,4},{6,7},{7,6},{8,9},{9,8},{10,11... | collective-permute-start | bytes 2359304 | tf_op jit(solution)/shard_map/ppermute | solution.py:492
  27.8 45.0 %collective-permute-start.13 = (bf16[2,96,768]{2,1,0:T(8,128)(2,1)S(1)}, bf16[2,96,768]{2,1,0:T(8,128)(2,1)S(1)}, u32[]{:S(2)}, u32[]{:S(2)}) collective-permute-start(bf16[2,96,768]{2,1,0:T(8,128)(2,1)S(1)} %pad_maximum_fusion.2), channel_id=1, source_target_pairs={{0,16},{4,20},{8,24},{12,28},{16,0},{20,4},{24,8},{28,12},{1,17},{... | collective-permute-start | bytes 884744 | tf_op jit(solution)/shard_map/ppermute | solution.py:492
  29.5 43.1 %collective-permute-start.12 = (bf16[2,96,768]{2,1,0:T(8,128)(2,1)S(1)}, bf16[2,96,768]{2,1,0:T(8,128)(2,1)S(1)}, u32[]{:S(2)}, u32[]{:S(2)}) collective-permute-start(bf16[2,96,768]{2,1,0:T(8,128)(2,1)S(1)} %pad_maximum_fusion.2), channel_id=1, source_target_pairs={{0,8},{4,12},{8,0},{12,4},{16,24},{20,28},{24,16},{28,20},{1,9},{5... | collective-permute-start | bytes 884744 | tf_op jit(solution)/shard_map/ppermute | solution.py:492
  33.0 39.8 %collective-permute-start.14 = (bf16[2,96,768]{2,1,0:T(8,128)(2,1)S(1)}, bf16[2,96,768]{2,1,0:T(8,128)(2,1)S(1)}, u32[]{:S(2)}, u32[]{:S(2)}) collective-permute-start(bf16[2,96,768]{2,1,0:T(8,128)(2,1)S(1)} %pad_maximum_fusion.2), channel_id=1, source_target_pairs={{0,24},{4,28},{8,16},{12,20},{16,8},{20,12},{24,0},{28,4},{1,25},{... | collective-permute-start | bytes 884744 | tf_op jit(solution)/shard_map/ppermute | solution.py:492
  36.5 9.6 %collective-permute-start.9 = (bf16[3,96,768]{2,1,0:T(8,128)(2,1)S(1)}, bf16[3,96,768]{2,1,0:T(8,128)(2,1)S(1)}, u32[]{:S(2)}, u32[]{:S(2)}) collective-permute-start(bf16[3,96,768]{2,1,0:T(8,128)(2,1)S(1)} %pad_maximum_fusion.1), channel_id=1, source_target_pairs={{0,4},{4,0},{8,12},{12,8},{16,20},{20,16},{24,28},{28,24},{1,5},{5... | collective-permute-start | bytes 1327112 | tf_op jit(solution)/shard_map/ppermute | solution.py:492
  46.1 2.6 %collective-permute-start.4 = (bf16[512,768]{1,0:T(8,128)(2,1)}, bf16[512,768]{1,0:T(8,128)(2,1)S(1)}, u32[]{:S(2)}, u32[]{:S(2)}) collective-permute-start(bf16[512,768]{1,0:T(8,128)(2,1)} %collective-permute-done.refs_2_), channel_id=1, source_target_pairs={{0,1},{1,0},{2,3},{3,2},{4,5},{5,4},{6,7},{7,6},{8,9},{9,8},{10,11... | collective-permute-start | bytes 2359304 | tf_op jit(solution)/shard_map/ppermute | solution.py:492
  46.2 3.3 %copy-start.6 = (bf16[8,96,768]{2,1,0:T(8,128)(2,1)}, bf16[8,96,768]{2,1,0:T(8,128)(2,1)S(1)}, u32[]{:S(2)}) copy-start(bf16[8,96,768]{2,1,0:T(8,128)(2,1)S(1)} %slice_dynamic-update-slice_fusion) | copy-start | bytes 3538948
  46.2 0.9 copy-start.26
  47.2 24.9 %collective-permute-start.2 = (bf16[512,768]{1,0:T(8,128)(2,1)S(1)}, bf16[512,768]{1,0:T(8,128)(2,1)S(1)}, u32[]{:S(2)}, u32[]{:S(2)}) collective-permute-start(bf16[512,768]{1,0:T(8,128)(2,1)S(1)} %bitcast.117), channel_id=1, source_target_pairs={{0,2},{1,3},{2,0},{3,1},{4,6},{5,7},{6,4},{7,5},{8,10},{9,11},{10,... | collective-permute-start | bytes 2359304 | tf_op jit(solution)/shard_map/ppermute | solution.py:492
  48.7 0.9 copy-start.28
  48.7 24.3 %collective-permute-start.1 = (bf16[512,768]{1,0:T(8,128)(2,1)S(1)}, bf16[512,768]{1,0:T(8,128)(2,1)S(1)}, u32[]{:S(2)}, u32[]{:S(2)}) collective-permute-start(bf16[512,768]{1,0:T(8,128)(2,1)S(1)} %bitcast.118), channel_id=1, source_target_pairs={{0,1},{1,0},{2,3},{3,2},{4,5},{5,4},{6,7},{7,6},{8,9},{9,8},{10,11... | collective-permute-start | bytes 2359304 | tf_op jit(solution)/shard_map/ppermute | solution.py:492
  72.1 0.9 copy-start.24
  72.1 2.4 %collective-permute-start.10 = (bf16[512,768]{1,0:T(8,128)(2,1)S(1)}, bf16[512,768]{1,0:T(8,128)(2,1)S(1)}, u32[]{:S(2)}, u32[]{:S(2)}) collective-permute-start(bf16[512,768]{1,0:T(8,128)(2,1)S(1)} %collective-permute-done.2.refs_2_), channel_id=1, source_target_pairs={{0,1},{1,0},{2,3},{3,2},{4,5},{5,4},{6,7},{7,6},{8,9},{9,8},{10,11... | collective-permute-start | bytes 2359304 | tf_op jit(solution)/shard_map/ppermute | solution.py:492
  73.0 1.5 copy-start.5
  73.0 1.5 copy-start.25
  74.5 0.9 copy-start.27
  86.6 4.1 %collective-permute-start.17 = (f32[8,2048]{1,0:T(8,128)}, f32[8,2048]{1,0:T(8,128)S(1)}, u32[]{:S(2)}, u32[]{:S(2)}) collective-permute-start(f32[8,2048]{1,0:T(8,128)} %get-tuple-element.69), channel_id=1, source_target_pairs={{0,3},{1,2},{2,1},{3,0},{4,7},{5,6},{6,5},{7,4},{8,11},{9,10},{10,... | collective-permute-start | bytes 196616 | tf_op jit(solution)/shard_map/ppermute | solution.py:492
  87.7 4.9 %collective-permute-start.16 = (f32[8,2048]{1,0:T(8,128)}, f32[8,2048]{1,0:T(8,128)S(1)}, u32[]{:S(2)}, u32[]{:S(2)}) collective-permute-start(f32[8,2048]{1,0:T(8,128)} %get-tuple-element.69), channel_id=1, source_target_pairs={{0,2},{1,3},{2,0},{3,1},{4,6},{5,7},{6,4},{7,5},{8,10},{9,11},{10,... | collective-permute-start | bytes 196616 | tf_op jit(solution)/shard_map/ppermute | solution.py:492
  88.5 4.0 %collective-permute-start.15 = (f32[8,2048]{1,0:T(8,128)}, f32[8,2048]{1,0:T(8,128)S(1)}, u32[]{:S(2)}, u32[]{:S(2)}) collective-permute-start(f32[8,2048]{1,0:T(8,128)} %get-tuple-element.69), channel_id=1, source_target_pairs={{0,1},{1,0},{2,3},{3,2},{4,5},{5,4},{6,7},{7,6},{8,9},{9,8},{10,11... | collective-permute-start | bytes 196616 | tf_op jit(solution)/shard_map/ppermute | solution.py:492
  88.5 4.0 %copy-start.20 = (f32[8,2048]{1,0:T(8,128)S(1)}, f32[8,2048]{1,0:T(8,128)}, u32[]{:S(2)}) copy-start(f32[8,2048]{1,0:T(8,128)} %get-tuple-element.69) | copy-start | bytes 196612
  90.0 20.4 %collective-permute-start.18 = (bf16[512,768]{1,0:T(8,128)(2,1)S(1)}, bf16[512,768]{1,0:T(8,128)(2,1)S(1)}, u32[]{:S(2)}, u32[]{:S(2)}) collective-permute-start(bf16[512,768]{1,0:T(8,128)(2,1)S(1)} %get-tuple-element.153), channel_id=1, source_target_pairs={{0,1},{1,0},{2,3},{3,2},{4,5},{5,4},{6,7},{7,6},{8,9},{9,8},{10,11... | collective-permute-start | bytes 2359304 | tf_op jit(solution)/shard_map/ppermute | solution.py:492
  108.9 26.4 %collective-permute-start.19 = (bf16[4,96,768]{2,1,0:T(8,128)(2,1)S(1)}, bf16[4,96,768]{2,1,0:T(8,128)(2,1)S(1)}, u32[]{:S(2)}, u32[]{:S(2)}) collective-permute-start(bf16[4,96,768]{2,1,0:T(8,128)(2,1)S(1)} %pad_maximum_fusion), channel_id=1, source_target_pairs={{0,4},{4,0},{8,12},{12,8},{16,20},{20,16},{24,28},{28,24},{1,5},{5... | collective-permute-start | bytes 1769480 | tf_op jit(solution)/shard_map/ppermute | solution.py:492
  111.7 23.6 %collective-permute-start.21 = (bf16[512,768]{1,0:T(8,128)(2,1)S(1)}, bf16[512,768]{1,0:T(8,128)(2,1)S(1)}, u32[]{:S(2)}, u32[]{:S(2)}) collective-permute-start(bf16[512,768]{1,0:T(8,128)(2,1)S(1)} %add_convert_fusion.1), channel_id=1, source_target_pairs={{0,2},{1,3},{2,0},{3,1},{4,6},{5,7},{6,4},{7,5},{8,10},{9,11},{10,... | collective-permute-start | bytes 2359304 | tf_op jit(solution)/shard_map/ppermute | solution.py:492
  113.2 22.1 %collective-permute-start.20 = (bf16[512,768]{1,0:T(8,128)(2,1)S(1)}, bf16[512,768]{1,0:T(8,128)(2,1)S(1)}, u32[]{:S(2)}, u32[]{:S(2)}) collective-permute-start(bf16[512,768]{1,0:T(8,128)(2,1)S(1)} %get-tuple-element.79), channel_id=1, source_target_pairs={{0,1},{1,0},{2,3},{3,2},{4,5},{5,4},{6,7},{7,6},{8,9},{9,8},{10,11... | collective-permute-start | bytes 2359304 | tf_op jit(solution)/shard_map/ppermute | solution.py:492
  113.2 22.1 %copy-start.3 = (bf16[768,768]{1,0:T(8,128)(2,1)S(1)}, bf16[768,768]{1,0:T(8,128)(2,1)}, u32[]{:S(2)}) copy-start(bf16[768,768]{1,0:T(8,128)(2,1)} %get-tuple-element.77) | copy-start | bytes 3538948
  135.3 29.3 %copy-start.11 = (bf16[512,768]{1,0:T(8,128)(2,1)}, bf16[512,768]{1,0:T(8,128)(2,1)S(1)}, u32[]{:S(2)}) copy-start(bf16[512,768]{1,0:T(8,128)(2,1)S(1)} %collective-permute-done.20) | copy-start | bytes 2359300
  135.3 29.3 %copy-start.9 = (bf16[512,768]{1,0:T(8,128)(2,1)}, bf16[512,768]{1,0:T(8,128)(2,1)S(1)}, u32[]{:S(2)}) copy-start(bf16[512,768]{1,0:T(8,128)(2,1)S(1)} %collective-permute-done.21) | copy-start | bytes 2359300
  135.5 29.1 %collective-permute-start.24 = (bf16[96,768]{1,0:T(8,128)(2,1)S(1)}, bf16[96,768]{1,0:T(8,128)(2,1)S(1)}, u32[]{:S(2)}, u32[]{:S(2)}) collective-permute-start(bf16[96,768]{1,0:T(8,128)(2,1)S(1)} %get-tuple-element.155), channel_id=1, source_target_pairs={{0,8},{4,12},{8,0},{12,4},{16,24},{20,28},{24,16},{28,20},{1,9},{5... | collective-permute-start | bytes 442376 | tf_op jit(solution)/shard_map/ppermute | solution.py:492
  135.6 29.1 %collective-permute-start.23 = (bf16[96,768]{1,0:T(8,128)(2,1)S(1)}, bf16[96,768]{1,0:T(8,128)(2,1)S(1)}, u32[]{:S(2)}, u32[]{:S(2)}) collective-permute-start(bf16[96,768]{1,0:T(8,128)(2,1)S(1)} %get-tuple-element.156), channel_id=1, source_target_pairs={{0,16},{4,20},{8,24},{12,28},{16,0},{20,4},{24,8},{28,12},{1,17},{... | collective-permute-start | bytes 442376 | tf_op jit(solution)/shard_map/ppermute | solution.py:492
  137.8 26.8 %collective-permute-start.22 = (bf16[96,768]{1,0:T(8,128)(2,1)S(1)}, bf16[96,768]{1,0:T(8,128)(2,1)S(1)}, u32[]{:S(2)}, u32[]{:S(2)}) collective-permute-start(bf16[96,768]{1,0:T(8,128)(2,1)S(1)} %get-tuple-element.157), channel_id=1, source_target_pairs={{0,24},{4,28},{8,16},{12,20},{16,8},{20,12},{24,0},{28,4},{1,25},{... | collective-permute-start | bytes 442376 | tf_op jit(solution)/shard_map/ppermute | solution.py:492
  164.7 0.7 copy-start.18
  165.4 5.6 %copy-start = (bf16[2048,768]{1,0:T(8,128)(2,1)S(1)}, bf16[2048,768]{1,0:T(8,128)(2,1)}, u32[]{:S(2)}) copy-start(bf16[2048,768]{1,0:T(8,128)(2,1)} %get-tuple-element.98) | copy-start | bytes 9437188
  168.1 2.8 %collective-permute-start.26 = (bf16[512,768]{1,0:T(8,128)(2,1)}, bf16[512,768]{1,0:T(8,128)(2,1)}, u32[]{:S(2)}, u32[]{:S(2)}) collective-permute-start(bf16[512,768]{1,0:T(8,128)(2,1)} %get-tuple-element.151), channel_id=1, source_target_pairs={{0,1},{1,0},{2,3},{3,2},{4,5},{5,4},{6,7},{7,6},{8,9},{9,8},{10,11... | collective-permute-start | bytes 2359304 | tf_op jit(solution)/shard_map/ppermute | solution.py:492
  169.3 4.5 %slice-start = ((f32[8,2048]{1,0:T(8,128)}), f32[1,2048]{1,0:T(1,128)S(1)}, s32[]{:S(2)}) async-start(f32[8,2048]{1,0:T(8,128)} %add_add_fusion.2.refs_4_), calls=%async_computation | async-start | bytes 16384 | tf_op jit(solution)/shard_map/slice | solution.py:980
  169.3 9.9 %copy-start.4 = (bf16[768,768]{1,0:T(8,128)(2,1)S(1)}, bf16[768,768]{1,0:T(8,128)(2,1)}, u32[]{:S(2)}) copy-start(bf16[768,768]{1,0:T(8,128)(2,1)} %get-tuple-element.97) | copy-start | bytes 3538948
  169.3 11.8 %copy-start.15 = (bf16[96,768]{1,0:T(8,128)(2,1)S(1)}, bf16[96,768]{1,0:T(8,128)(2,1)}, u32[]{:S(2)}) copy-start(bf16[96,768]{1,0:T(8,128)(2,1)} %copy-done.14) | copy-start | bytes 442372
  169.4 11.7 %copy-start.17 = (bf16[96,768]{1,0:T(8,128)(2,1)S(1)}, bf16[96,768]{1,0:T(8,128)(2,1)}, u32[]{:S(2)}) copy-start(bf16[96,768]{1,0:T(8,128)(2,1)} %copy-done.16) | copy-start | bytes 442372
  169.4 11.7 %copy-start.19 = (bf16[96,768]{1,0:T(8,128)(2,1)S(1)}, bf16[96,768]{1,0:T(8,128)(2,1)}, u32[]{:S(2)}) copy-start(bf16[96,768]{1,0:T(8,128)(2,1)} %copy-done.18) | copy-start | bytes 442372
  169.4 9.9 %collective-permute-start.25 = (bf16[2,96,768]{2,1,0:T(8,128)(2,1)S(1)}, bf16[2,96,768]{2,1,0:T(8,128)(2,1)S(1)}, u32[]{:S(2)}, u32[]{:S(2)}) collective-permute-start(bf16[2,96,768]{2,1,0:T(8,128)(2,1)S(1)} %pad_maximum_fusion.3), channel_id=1, source_target_pairs={{0,4},{4,0},{8,12},{12,8},{16,20},{20,16},{24,28},{28,24},{1,5},{5... | collective-permute-start | bytes 884744 | tf_op jit(solution)/shard_map/ppermute | solution.py:492
  172.3 19.8 %collective-permute-start.31 = (bf16[512,768]{1,0:T(8,128)(2,1)S(1)}, bf16[512,768]{1,0:T(8,128)(2,1)}, u32[]{:S(2)}, u32[]{:S(2)}) collective-permute-start(bf16[512,768]{1,0:T(8,128)(2,1)S(1)} %add_convert_fusion), channel_id=1, source_target_pairs={{0,2},{1,3},{2,0},{3,1},{4,6},{5,7},{6,4},{7,5},{8,10},{9,11},{10,... | collective-permute-start | bytes 2359304 | tf_op jit(solution)/shard_map/ppermute | solution.py:492
  173.8 11.4 %collective-permute-start.30 = (bf16[2,96,768]{2,1,0:T(8,128)(2,1)S(1)}, bf16[2,96,768]{2,1,0:T(8,128)(2,1)S(1)}, u32[]{:S(2)}, u32[]{:S(2)}) collective-permute-start(bf16[2,96,768]{2,1,0:T(8,128)(2,1)S(1)} %pad_maximum_fusion.4), channel_id=1, source_target_pairs={{0,4},{4,0},{8,12},{12,8},{16,20},{20,16},{24,28},{28,24},{1,5},{5... | collective-permute-start | bytes 884744 | tf_op jit(solution)/shard_map/ppermute | solution.py:492
  179.3 13.6 %collective-permute-start.28 = (bf16[96,768]{1,0:T(8,128)(2,1)S(1)}, bf16[96,768]{1,0:T(8,128)(2,1)S(1)}, u32[]{:S(2)}, u32[]{:S(2)}) collective-permute-start(bf16[96,768]{1,0:T(8,128)(2,1)S(1)} %get-tuple-element.159), channel_id=1, source_target_pairs={{0,24},{4,28},{8,16},{12,20},{16,8},{20,12},{24,0},{28,4},{1,25},{... | collective-permute-start | bytes 442376 | tf_op jit(solution)/shard_map/ppermute | solution.py:492
  181.1 11.9 %collective-permute-start.29 = (bf16[96,768]{1,0:T(8,128)(2,1)S(1)}, bf16[96,768]{1,0:T(8,128)(2,1)S(1)}, u32[]{:S(2)}, u32[]{:S(2)}) collective-permute-start(bf16[96,768]{1,0:T(8,128)(2,1)S(1)} %get-tuple-element.158), channel_id=1, source_target_pairs={{0,16},{4,20},{8,24},{12,28},{16,0},{20,4},{24,8},{28,12},{1,17},{... | collective-permute-start | bytes 442376 | tf_op jit(solution)/shard_map/ppermute | solution.py:492
  181.1 21.5 %collective-permute-start.27 = (bf16[512,768]{1,0:T(8,128)(2,1)}, bf16[512,768]{1,0:T(8,128)(2,1)}, u32[]{:S(2)}, u32[]{:S(2)}) collective-permute-start(bf16[512,768]{1,0:T(8,128)(2,1)} %get-tuple-element.101), channel_id=1, source_target_pairs={{0,1},{1,0},{2,3},{3,2},{4,5},{5,4},{6,7},{7,6},{8,9},{9,8},{10,11... | collective-permute-start | bytes 2359304 | tf_op jit(solution)/shard_map/ppermute | solution.py:492
  192.2 5.2 %collective-permute-start.32 = (bf16[96,768]{1,0:T(8,128)(2,1)S(1)}, bf16[96,768]{1,0:T(8,128)(2,1)S(1)}, u32[]{:S(2)}, u32[]{:S(2)}) collective-permute-start(bf16[96,768]{1,0:T(8,128)(2,1)S(1)} %fusion.12), channel_id=1, source_target_pairs={{0,8},{4,12},{8,0},{12,4},{16,24},{20,28},{24,16},{28,20},{1,9},{5... | collective-permute-start | bytes 442376 | tf_op jit(solution)/shard_map/ppermute | solution.py:492
  198.2 10.8 %collective-permute-start.34 = (f32[96,384]{1,0:T(8,128)}, f32[96,384]{1,0:T(8,128)}, u32[]{:S(2)}, u32[]{:S(2)}) collective-permute-start(f32[96,384]{1,0:T(8,128)} %slice.192), channel_id=1, source_target_pairs={{0,2},{1,3},{2,0},{3,1},{4,6},{5,7},{6,4},{7,5},{8,10},{9,11},{10,... | collective-permute-start | bytes 442376 | tf_op jit(solution)/shard_map/ppermute | solution.py:492
  198.9 10.2 %collective-permute-start.35 = (f32[96,384]{1,0:T(8,128)}, f32[96,384]{1,0:T(8,128)}, u32[]{:S(2)}, u32[]{:S(2)}) collective-permute-start(f32[96,384]{1,0:T(8,128)} %slice.192), channel_id=1, source_target_pairs={{0,3},{1,2},{2,1},{3,0},{4,7},{5,6},{6,5},{7,4},{8,11},{9,10},{10,... | collective-permute-start | bytes 442376 | tf_op jit(solution)/shard_map/ppermute | solution.py:492
  198.9 10.2 %collective-permute-start.33 = (f32[96,384]{1,0:T(8,128)}, f32[96,384]{1,0:T(8,128)}, u32[]{:S(2)}, u32[]{:S(2)}) collective-permute-start(f32[96,384]{1,0:T(8,128)} %slice.192), channel_id=1, source_target_pairs={{0,1},{1,0},{2,3},{3,2},{4,5},{5,4},{6,7},{7,6},{8,9},{9,8},{10,11... | collective-permute-start | bytes 442376 | tf_op jit(solution)/shard_map/ppermute | solution.py:492
  202.6 2.4 %copy-start.2 = (bf16[512,1,768]{2,0,1:T(8,128)(2,1)S(1)}, bf16[512,1,768]{2,0,1:T(8,128)(2,1)}, u32[]{:S(2)}) copy-start(bf16[512,1,768]{2,0,1:T(8,128)(2,1)} %param.15) | copy-start | bytes 2359300
  202.6 2.4 %copy-start.8 = (bf16[512,1,768]{2,0,1:T(8,128)(2,1)S(1)}, bf16[512,1,768]{2,0,1:T(8,128)(2,1)}, u32[]{:S(2)}) copy-start(bf16[512,1,768]{2,0,1:T(8,128)(2,1)} %param.16) | copy-start | bytes 2359300
  202.6 2.5 %copy-start.10 = (bf16[512,768]{1,0:T(8,128)(2,1)S(1)}, bf16[512,768]{1,0:T(8,128)(2,1)}, u32[]{:S(2)}) copy-start(bf16[512,768]{1,0:T(8,128)(2,1)} %copy-done.9) | copy-start | bytes 2359300
  202.6 2.5 %copy-start.12 = (bf16[512,768]{1,0:T(8,128)(2,1)S(1)}, bf16[512,768]{1,0:T(8,128)(2,1)}, u32[]{:S(2)}) copy-start(bf16[512,768]{1,0:T(8,128)(2,1)} %copy-done.11) | copy-start | bytes 2359300
  (2 other events, 1.4 us)

commit v3 on v2

--- a/solution.py
+++ b/solution.py
@@ -15,6 +15,7 @@
 GAIN_AT = 12
 GATE_AT = 16
 HEAD_AT = 64
+LOG2E = 1.4426950408889634
 epsilon = 1e-05
 bf16 = jnp.bfloat16
 f32 = jnp.float32
@@ -36,12 +37,21 @@
     return pieces
 
 
-def mm_left_exact(left, right, parts):
-    return sum(mm(left, piece) for piece in split(right, parts))
-
-
-def mm_right_exact(left, right, parts):
-    return sum(mm(piece, right) for piece in split(left, parts))
+def mm_left_exact(left, right):
+    both = mm(left, jnp.concatenate(split(right, 2), axis=1))
+    return both[:, : right.shape[1]] + both[:, right.shape[1] :]
+
+
+def mm_right_exact(left, right):
+    return sum(mm(piece, right) for piece in split(left, 2))
+
+
+def widen(values, expand):
+    half = LANES // 2
+    first = jnp.where(iota(values.shape, 1) < half, values, 0.0)
+    high = first.astype(bf16).astype(f32)
+    packed = (high + pltpu.roll(first - high, half, 1)).astype(bf16)
+    return mm(packed, expand)
 
 
 def sigmoid(values):
@@ -102,27 +112,40 @@
             chosen_ref[...] = ref[...]
 
 
+def place_rows(ref, slot, values):
+    rows = values.shape[0]
+    ref[pl.ds(pl.multiple_of(slot * rows, 16), rows), :] = values
+
+
 def forward_kernel(
     inner,
     state_count,
     heads,
     per_piece,
     pieces,
+    parts,
     info_ref,
     *refs,
 ):
     hidden_refs, refs = refs[:pieces], refs[pieces:]
+    part_refs, refs = refs[:parts], refs[parts:]
+    if parts:
+        refs, weight_ref, scratch = refs[:-4], refs[-4], refs[-3:]
+        refs = refs + scratch
+    else:
+        weight_ref, refs = refs[0], refs[1:]
     (
-        weight_ref,
         choose_ref,
         chan_ref,
         head_ref,
         expand_ref,
         normed_ref,
         pre_ref,
+        step_ref,
         y_ref,
         cum_ref,
         entering_ref,
+        conv_ref,
         rows_ref,
         ext_ref,
         state_ref,
@@ -137,6 +160,15 @@
     def _():
         ext_ref[...] = jnp.zeros_like(ext_ref)
         state_ref[...] = jnp.zeros_like(state_ref)
+        if parts:
+            put = lambda k, value: place_rows(weight_ref, info_ref[4] ^ k, value)
+            own_ref, near_ref, far_ref, beside_ref = part_refs
+            put(0, own_ref[...])
+            put(1, near_ref[...])
+            for at in range(far_ref.shape[0]):
+                k = 2 * (far_ref.shape[0] - at)
+                put(k, far_ref[at])
+                put(k + 1, beside_ref[at])
         rows_ref[...] = mm(weight_ref[:, conv_width:], choose_ref[...], TN)[0:16, :]
 
     pick_piece(block, per_piece, info_ref[3], hidden_refs, hidden_ref)
@@ -145,13 +177,15 @@
     normed = (residual * row_scale * rows_ref[GAIN_AT : GAIN_AT + 1, conv_width:]).astype(bf16)
     normed_ref[...] = normed
     pre = mm(normed, weight_ref[...])
-    pre_ref[...] = pre
+    pre_ref[...] = pre[:, :conv_width].astype(bf16)
+    step_ref[...] = pre[:, conv_width:]
 
     ext_ref[0:8, :] = ext_ref[SPAN : SPAN + 8, :]
     ext_ref[8 : 8 + SPAN, :] = pre[:, :conv_width]
     position = base + iota((SPAN, LANES), 0)
     start = doc_start(position, ends)
     conv = conv_block(ext_ref, rows_ref, position, start, conv_width)
+    conv_ref[...] = conv
     active = conv * sigmoid(conv)
     x_val = active[:, :inner].astype(bf16).astype(f32)
     in_map = active[:, inner : inner + state_count].astype(bf16)
@@ -162,7 +196,7 @@
     row_at = iota((SPAN, SPAN), 0)
     col_at = iota((SPAN, SPAN), 1)
     lower = (col_at <= row_at).astype(f32).astype(bf16)
-    cum = mm_left_exact(lower, log_decay, 3)
+    cum = mm_left_exact(lower, log_decay * LOG2E)
     cum_ref[...] = cum
     cum_rows = cum.T
 
@@ -171,9 +205,9 @@
     tail = (position >= start_last).astype(f32)
     survives = (start_last < base).astype(f32)
     expand = expand_ref[...]
-    step_wide = mm_right_exact(step_size, expand, 2)
-    decay_wide = mm_right_exact(jnp.exp(cum), expand, 2)
-    into_wide = mm_right_exact(jnp.exp(cum[SPAN - 1 :, :] - cum) * tail, expand, 2)
+    step_wide = widen(step_size, expand)
+    decay_wide = widen(jnp.exp2(cum), expand)
+    into_wide = widen(jnp.exp2(cum[SPAN - 1 :, :] - cum) * tail, expand)
 
     x_step = x_val * step_wide
     x_step_low = x_step.astype(bf16)
@@ -183,18 +217,24 @@
     visible = (col_at <= row_at) & (base + col_at >= wide(start, SPAN))
     scores = jnp.where(visible, mm(out_map, in_map, NT), 0.0)
     upper_half = iota((SPAN, LANES), 1) >= LANES // 2
+    half = SPAN // 2
     inside = []
     for pair in range(heads // 2):
         x_pair = x_step_low[:, pair * LANES : (pair + 1) * LANES]
-        total = None
+        tops, bottoms = [], []
         for which in range(2):
             head = 2 * pair + which
-            gap = cum[:, head : head + 1] - cum_rows[head : head + 1, :]
-            mixing = (scores * jnp.exp(jnp.minimum(gap, 0.0))).astype(bf16)
+            column, row = cum[:, head : head + 1], cum_rows[head : head + 1, :]
             chosen = upper_half if which else jnp.logical_not(upper_half)
-            part = mm(mixing, jnp.where(chosen, x_pair, jnp.zeros_like(x_pair)))
-            total = part if total is None else total + part
-        inside.append(total)
+            x_head = jnp.where(chosen, x_pair, jnp.zeros_like(x_pair))
+            decays = jnp.exp2(jnp.minimum(column[:half] - row[:, :half], 0.0))
+            mixing = (scores[:half, :half] * decays).astype(bf16)
+            tops.append(mm(mixing, x_head[:half]))
+            far = jnp.exp2(column[half:] - row[:, :half])
+            near = jnp.exp2(jnp.minimum(column[half:] - row[:, half:], 0.0))
+            mixing = (scores[half:] * jnp.concatenate([far, near], axis=1)).astype(bf16)
+            bottoms.append(mm(mixing, x_head))
+        inside.append(jnp.concatenate([tops[0] + tops[1], bottoms[0] + bottoms[1]], axis=0))
     y_val = jnp.concatenate(inside, axis=1) + outside + chan_ref[0:1, :] * x_val
     y_ref[...] = y_val
 
@@ -223,8 +263,8 @@
 
 
 def product_sums(left, right):
-    ones = jnp.ones((8, left.shape[1]), bf16)
-    return sum(mm(ones, piece, NT) for piece in split(left * right.astype(f32), 3))
+    products = left * right.astype(f32)
+    return sum(products[:, at : at + LANES] for at in range(0, left.shape[1], LANES))
 
 
 def gate_kernel(inner, inner_total, per_piece, pieces, info_ref, *refs):
@@ -275,7 +315,7 @@
     gate_grad = mixed_grad * y_val * (gate_sig * (1.0 + gate * (1.0 - gate_sig)))
     gate_grad = gate_grad.astype(bf16)
     gate_grad_ref[...] = gate_grad
-    y_grad_ref[...] = mixed_grad * gate_act
+    y_grad_ref[...] = (mixed_grad * gate_act).astype(bf16)
     gate_acc[...] += mm(normed_ref[...], gate_grad, TN)
 
     @pl.when(block == pl.num_programs(0) - 1)
@@ -285,13 +325,15 @@
         product_ref[...] = product_sums(gate_acc[...], gate_w_ref[...])
 
 
-def backward_kernel(inner, state_count, heads, blocks, at, final, info_ref, *refs):
+def backward_kernel(inner, state_count, heads, blocks, info_ref, *refs):
     (
         normed_ref,
         weight_ref,
         gate_w_ref,
         pre_ref,
         halo_ref,
+        step_ref,
+        conv_ref,
         y_ref,
         y_grad_ref,
         gate_grad_ref,
@@ -302,48 +344,34 @@
         head_ref,
         expand_ref,
         gather_ref,
-    ) = refs[:15]
-    refs = refs[15:]
-    if at:
-        next_in, state_in, late_in, small_in, head_in, product_ref, choose_ref, extra_ref, _ = refs[:9]
-        refs = refs[9:]
-    total_ref = refs[0]
-    if final:
-        late_ref = refs[1]
-        ext_ref, next_ref, pre_grad_ref, state_grad_ref, late_acc, small_ref, heads_ref = refs[2:]
-    else:
-        next_out, state_grad_ref, late_acc, small_ref, heads_ref = refs[1:6]
-        ext_ref, next_ref, pre_grad_ref = refs[6:]
+    ) = refs[:17]
+    refs = refs[17:]
+    product_ref, choose_ref, extra_ref, total_ref, late_ref = refs[:5]
+    ext_ref, next_ref, pre_grad_ref, state_grad_ref, late_acc, small_ref, heads_ref = refs[5:]
     step = pl.program_id(0)
-    block = blocks - 1 - at - step
+    block = blocks - 1 - step
     base = block * SPAN
     conv_width = inner + 2 * state_count
     ends = [info_ref[k] for k in range(3)]
 
     @pl.when(step == 0)
     def _():
-        if at:
-            next_ref[0:8, :] = next_in[...]
-            state_grad_ref[...] = state_in[...]
-            late_acc[...] = late_in[...]
-            small_ref[...] = small_in[...]
-            heads_ref[...] = head_in[...]
-        else:
-            next_ref[...] = jnp.zeros_like(next_ref)
-            state_grad_ref[...] = jnp.zeros_like(state_grad_ref)
-            late_acc[...] = jnp.zeros_like(late_acc)
-            small_ref[...] = jnp.zeros_like(small_ref)
-            heads_ref[...] = jnp.zeros_like(heads_ref)
+        next_ref[...] = jnp.zeros_like(next_ref)
+        state_grad_ref[...] = jnp.zeros_like(state_grad_ref)
+        late_acc[...] = jnp.zeros_like(late_acc)
+        small_ref[...] = jnp.zeros_like(small_ref)
+        heads_ref[...] = jnp.zeros_like(heads_ref)
 
     skip = chan_ref[0:1, :]
     y_val = y_ref[...]
-    y_grad = y_grad_ref[...]
-
-    ext_ref[0:8, :] = halo_ref[:, :conv_width]
-    ext_ref[8 : 8 + SPAN, :] = pre_ref[:, :conv_width]
+    y_grad_low = y_grad_ref[...]
+    y_grad = y_grad_low.astype(f32)
+
+    ext_ref[0:8, :] = halo_ref[...].astype(f32)[8:16, :]
+    ext_ref[8 : 8 + SPAN, :] = pre_ref[...].astype(f32)
     position = base + iota((SPAN, LANES), 0)
     start = doc_start(position, ends)
-    conv = conv_block(ext_ref, rows_ref, position, start, conv_width)
+    conv = conv_ref[...]
     conv_sig = sigmoid(conv)
     active = conv * conv_sig
     act_slope = conv_sig * (1.0 + conv * (1.0 - conv_sig))
@@ -351,7 +379,7 @@
     in_map = active[:, inner : inner + state_count].astype(bf16)
     out_map = active[:, inner + state_count :].astype(bf16)
 
-    step_pre = pre_ref[:, conv_width:] + head_ref[1:2, :]
+    step_pre = step_ref[...] + head_ref[1:2, :]
     step_size = softplus(step_pre)
     rates = head_ref[0:1, :]
     cum = cum_ref[...]
@@ -361,9 +389,9 @@
     tail = (position >= start_last).astype(f32)
     survives = (start_last < base).astype(f32)
     expand = expand_ref[...]
-    step_wide = mm_right_exact(step_size, expand, 2)
-    decay_wide = mm_right_exact(jnp.exp(cum), expand, 2)
-    into_wide = mm_right_exact(jnp.exp(cum[SPAN - 1 :, :] - cum) * tail, expand, 2)
+    step_wide = widen(step_size, expand)
+    decay_wide = widen(jnp.exp2(cum), expand)
+    into_wide = widen(jnp.exp2(cum[SPAN - 1 :, :] - cum) * tail, expand)
     keep_decay = decay_wide * wide(keep, inner)
     last_decay = decay_wide[SPAN - 1 :, :] * survives
 
@@ -372,7 +400,6 @@
     scaled = (x_step * into_wide).astype(bf16)
     entering = entering_ref[...]
     entering_low = entering.astype(bf16)
-    y_grad_low = y_grad.astype(bf16)
     state_grad = state_grad_ref[...]
     state_grad_low = state_grad.astype(bf16)
 
@@ -389,23 +416,34 @@
     visible = (row_at <= col_at) & (base + row_at >= col_start)
     scores = jnp.where(visible, mm(in_map, out_map, NT), 0.0)
     upper_half = iota((SPAN, LANES), 1) >= LANES // 2
-    score_grad = jnp.zeros((SPAN, SPAN), f32)
+    half = SPAN // 2
+    top_grad = jnp.zeros((half, SPAN), f32)
+    bottom_grad = jnp.zeros((half, half), f32)
     x_step_grads = []
     for pair in range(heads // 2):
         x_pair = x_step_low[:, pair * LANES : (pair + 1) * LANES]
         grad_pair = y_grad_low[:, pair * LANES : (pair + 1) * LANES]
-        total = None
+        tops, bottoms = [], []
         for which in range(2):
             head = 2 * pair + which
+            column, row = cum[:, head : head + 1], cum_rows[head : head + 1, :]
             chosen = upper_half if which else jnp.logical_not(upper_half)
             grad_head = jnp.where(chosen, grad_pair, jnp.zeros_like(grad_pair))
-            gap = cum_rows[head : head + 1, :] - cum[:, head : head + 1]
-            decays = jnp.exp(jnp.minimum(gap, 0.0))
-            score_grad = score_grad + mm(x_pair, grad_head, NT) * decays
-            part = mm((scores * decays).astype(bf16), grad_head)
-            total = part if total is None else total + part
-        x_step_grads.append(total)
+            near = jnp.exp2(jnp.minimum(row[:, :half] - column[:half], 0.0))
+            far = jnp.exp2(row[:, half:] - column[:half])
+            decays = jnp.concatenate([near, far], axis=1)
+            top_grad = top_grad + mm(x_pair[:half], grad_head, NT) * decays
+            tops.append(mm((scores[:half] * decays).astype(bf16), grad_head))
+            decays = jnp.exp2(jnp.minimum(row[:, half:] - column[half:], 0.0))
+            bottom_grad = bottom_grad + mm(x_pair[half:], grad_head[half:], NT) * decays
+            tail_mix = (scores[half:, half:] * decays).astype(bf16)
+            bottoms.append(mm(tail_mix, grad_head[half:]))
+        x_step_grads.append(
+            jnp.concatenate([tops[0] + tops[1], bottoms[0] + bottoms[1]], axis=0)
+        )
     x_step_grad = jnp.concatenate(x_step_grads, axis=1)
+    bottom_grad = jnp.concatenate([jnp.zeros((half, half), f32), bottom_grad], axis=1)
+    score_grad = jnp.concatenate([top_grad, bottom_grad], axis=0)
     score_grad = jnp.where(visible, score_grad, 0.0).astype(bf16)
     in_map_grad = in_map_grad + mm(score_grad, out_map)
     out_map_grad = out_map_grad + mm(score_grad, in_map, TN)
@@ -413,7 +451,7 @@
     inside = y_val - skip * x_val - keep_decay * outside
     into_terms = scaled.astype(f32) * scaled_grad
     cum_terms = (
-        y_grad_low.astype(f32) * inside
+        y_grad * inside
         + outside_grad.astype(f32) * outside
         - x_step_low.astype(f32) * x_step_grad
         - into_terms
@@ -425,10 +463,10 @@
     cum_terms = cum_terms + jnp.where(last_row, last_terms, 0.0)
     x_step_grad = x_step_grad + into_wide * scaled_grad
     gather = gather_ref[...]
-    cum_grad = mm_right_exact(cum_terms, gather, 2)
-    step_grad = mm_right_exact(x_val * x_step_grad, gather, 2)
+    cum_grad = mm_right_exact(cum_terms, gather)
+    step_grad = mm_right_exact(x_val * x_step_grad, gather)
     upper = (row_at <= col_at).astype(f32).astype(bf16)
-    log_grad = mm_left_exact(upper, cum_grad, 3)
+    log_grad = mm_left_exact(upper, cum_grad)
     step_grad = (step_grad + log_grad * rates) * sigmoid(step_pre)
     pre_grad_ref[:, conv_width:] = step_grad.astype(bf16)
     x_grad = skip * y_grad + step_wide * x_step_grad
@@ -467,24 +505,49 @@
 
     @pl.when(step == pl.num_programs(0) - 1)
     def _():
-        if final:
-            late = late_acc[...]
-            sums = product_sums(late, weight_ref[...]) + product_ref[...]
-            gain = rows_ref[GAIN_AT : GAIN_AT + 1, conv_width:]
-            small_ref[GAIN_AT : GAIN_AT + 1, conv_width:] = sums[0:1, :] / gain
-            chosen = small_ref[...].astype(bf16)
-            filler = jnp.zeros((LANES - chosen.shape[0], chosen.shape[1]), bf16)
-            misc = mm(choose_ref[...], jnp.concatenate([chosen, filler], axis=0), NT)
-            totals = heads_ref[...]
-            skips = mm_right_exact(totals, gather_ref[...], 2)
-            per_head = [totals[1:2, :LANES], totals[2:3, :LANES], skips[0:1, :]]
-            for at_head, value in enumerate(per_head):
-                value = jnp.broadcast_to(value, (8, LANES))
-                misc = misc + pltpu.roll(value, HEAD_AT + at_head * heads, 1)[0:1, :]
-            late_ref[:, :conv_width] = late[:, :conv_width].astype(bf16)
-            late_ref[:, conv_width:] = (late[:, conv_width:] + misc + extra_ref[...]).astype(bf16)
-        else:
-            next_out[...] = next_ref[0:8, :]
+        late = late_acc[...]
+        sums = product_sums(late, weight_ref[...]) + product_ref[...]
+        gain = weight_ref[:, conv_width + GAIN_AT : conv_width + GAIN_AT + 1].astype(f32)
+        sums = jnp.sum(sums, axis=1, keepdims=True) / gain
+        chosen = small_ref[...].astype(bf16)
+        filler = jnp.zeros((LANES - chosen.shape[0], chosen.shape[1]), bf16)
+        misc = mm(choose_ref[...], jnp.concatenate([chosen, filler], axis=0), NT)
+        misc = misc + jnp.where(iota(misc.shape, 1) == GAIN_AT, sums, 0.0)
+        totals = heads_ref[...]
+        skips = mm_right_exact(totals, gather_ref[...])
+        per_head = [totals[1:2, :LANES], totals[2:3, :LANES], skips[0:1, :]]
+        for at_head, value in enumerate(per_head):
+            value = jnp.broadcast_to(value, (8, LANES))
+            misc = misc + pltpu.roll(value, HEAD_AT + at_head * heads, 1)[0:1, :]
+        late_ref[:, :conv_width] = late[:, :conv_width].astype(bf16)
+        late_ref[:, conv_width:] = (late[:, conv_width:] + misc + extra_ref[...]).astype(bf16)
+
+
+def weights_kernel(early_count, inner, *refs):
+    early_refs, late_refs = refs[:early_count], refs[early_count:-3]
+    zx_ref, out_ref, rest_ref = refs[-3:]
+    early = tree_sum([ref[...].astype(f32) for ref in early_refs])
+    late = tree_sum([ref[...].astype(f32) for ref in late_refs])
+    zx_ref[0] = early[:, :inner]
+    zx_ref[1] = late[:, :inner]
+    out_ref[...] = early[:, inner:]
+    rest_ref[...] = late[:, inner:]
+
+
+def hidden_kernel(
+    gain_at, hidden_ref, grad_ref, own_ref, near_ref, far_ref, rest_ref, rows_ref, out_ref
+):
+    gain = rows_ref[GAIN_AT : GAIN_AT + 1, gain_at:]
+    half = far_ref.shape[0]
+    for at, part_ref in ((0, far_ref), (half, rest_ref)):
+        rows = slice(at, at + half)
+        total = own_ref[rows, :].astype(f32) + near_ref[rows, :].astype(f32)
+        scaled = (total + part_ref[...].astype(f32)) * gain
+        residual = hidden_ref[rows, :].astype(f32)
+        row_scale = lax.rsqrt(jnp.mean(residual * residual, axis=1, keepdims=True) + epsilon)
+        crossed = jnp.mean(scaled * residual, axis=1, keepdims=True)
+        result = row_scale * scaled - residual * (row_scale * row_scale * row_scale * crossed)
+        out_ref[rows, :] = (result + grad_ref[rows, :].astype(f32)).astype(bf16)
 
 
 def swap(values, axis, bits):
@@ -532,56 +595,31 @@
     return [pieces[k] for k in range(len(pieces))]
 
 
-def scatter_near(pieces, axis):
-    far = {}
-    for k in range(len(pieces) - 2, 0, -2):
-        both = pieces[k].astype(f32) + swap(pieces[k + 1], axis, 1).astype(f32)
-        far[k] = both.astype(bf16)
-    return far
-
-
-def scatter_far(pieces, far, axis, parts=1):
-    near = swap(after(pieces[1], *far.values()), axis, 1)
-    received = None
-    for bit in bits_of(lax.axis_size(axis))[1:]:
-        if received is not None:
-            far = {
-                k: (v.astype(f32) + received[k].astype(f32)).astype(bf16) for k, v in far.items()
-            }
-        if parts > 1 and len(far) == 1:
-            (last,) = far.values()
-            size = last.shape[0] // parts
-            cuts = [last[at : at + size] for at in range(0, last.shape[0], size)]
-            return near, [swap(cut, axis, bit) for cut in cuts]
-        received = {
-            k ^ bit: swap(v, axis, bit) for k, v in far.items() if k & bit
-        }
-        far = {k: v for k, v in far.items() if not k & bit}
-    return near, received[0] if parts == 1 else received
-
-
-def gather_direct(values, axis, other):
+def gather_direct(values, axis, others):
+    size = lax.axis_size(axis)
+    near = swap(values, axis, 1)
+    far = [swap(values, axis, k) for k in range(size - 2, 0, -2)]
+    far = after(jnp.stack(far), *others)
+    return values, near, far, swap(far, axis, 1)
+
+
+def assemble(own, near, far, beside, axis):
     size = lax.axis_size(axis)
     place = lax.axis_index(axis)
-    near = swap(values, axis, 1)
-    far = [swap(values, axis, k) for k in range(size - 2, 0, -2)]
-    far, other = lax.optimization_barrier((jnp.stack(far), other))
-    beside = swap(far, axis, 1)
-    result = jnp.zeros((size,) + values.shape, values.dtype)
-    pieces = {0: values, 1: near}
+    result = jnp.zeros((size,) + own.shape, own.dtype)
+    pieces = {0: own, 1: near}
     for at, k in enumerate(range(size - 2, 0, -2)):
         pieces.update({k: far[at], k + 1: beside[at]})
     for k in range(size):
         result = lax.dynamic_update_slice(
-            result, pieces[k][None], (place ^ k,) + (0,) * values.ndim
+            result, pieces[k][None], (place ^ k,) + (0,) * own.ndim
         )
-    return result.reshape((-1,) + values.shape[1:])
-
-
-def gather_pairs(values, axis):
+    return result.reshape((-1,) + own.shape[1:])
+
+
+def gather_pairs(values, other, axis):
     size = lax.axis_size(axis)
     place = lax.axis_index(axis)
-    other = swap(values, axis, 1)
     first = place % 2 == 0
     pair = jnp.stack([jnp.where(first, values, other), jnp.where(first, other, values)])
     result = jnp.zeros((size // 2,) + pair.shape, values.dtype)
@@ -672,12 +710,6 @@
         ],
         axis=1,
     )
-    shard = jnp.concatenate([zx_weight[1], bc_weight, misc], axis=1)
-    weights = gather_direct(shard, "dp", hidden_far)
-    shard = jnp.concatenate([zx_weight[0], out_weight.T], axis=1)
-    weights_late = gather_pairs(shard, "dp")
-    grad_all = gather_far(after(out_grad, hidden_far)[:, 0, :], "tensor")
-
     channel = np.arange(inner)
     per_dev = head_dim // data
     sources = [
@@ -695,16 +727,31 @@
     head_rows = jnp.pad(
         jnp.stack([-jnp.exp(decay_log), step_bias]), ((0, 6), (0, LANES - heads))
     )
-    expand = (jnp.arange(LANES)[:, None] == jnp.arange(inner)[None, :] // head_dim).astype(bf16)
-    gather = expand.T
+    channel_head = jnp.arange(inner)[None, :] // head_dim
+    expand = (jnp.arange(LANES)[:, None] % (LANES // 2) == channel_head).astype(bf16)
+    gather = (jnp.arange(LANES)[:, None] == channel_head).astype(bf16).T
     lengths = doc_lengths[0].astype(jnp.int32)
     info = jnp.stack(
-        [lengths[0], lengths[0] + lengths[1], lengths[0] + lengths[1] + lengths[2], mine]
+        [lengths[0], lengths[0] + lengths[1], lengths[0] + lengths[1] + lengths[2], mine, place]
     ).astype(jnp.int32)
 
-    limits = pltpu.CompilerParams(
-        dimension_semantics=("arbitrary",), vmem_limit_bytes=56 * 1024 * 1024
-    )
+    late_shard = jnp.concatenate([zx_weight[0], out_weight.T], axis=1)
+    late_other = swap(late_shard, "dp", 1)
+    shard = jnp.concatenate([zx_weight[1], bc_weight, misc], axis=1)
+    weight_parts = gather_direct(
+        shard, "dp", (hidden_far, late_other, choose, chan, head_rows, expand, info)
+    )
+    in_kernel = share % 16 == 0
+    if not in_kernel:
+        weight_parts = (assemble(*weight_parts, "dp"),)
+    weights_late = gather_pairs(late_shard, late_other, "dp")
+    grad_all = gather_far(after(out_grad, hidden_far)[:, 0, :], "tensor")
+
+    def limits(mebi):
+        return pltpu.CompilerParams(
+            dimension_semantics=("arbitrary",), vmem_limit_bytes=mebi * 1024 * 1024
+        )
+
     shaped = jax.ShapeDtypeStruct
 
     def fixed(shape, at=0):
@@ -738,7 +785,7 @@
                 scratch_shapes=scratch,
             ),
             out_shape=out_shape,
-            compiler_params=limits,
+            compiler_params=limits(56 if name == "backward" else 36),
             input_output_aliases=aliases,
             cost_estimate=pl.CostEstimate(
                 flops=int(micros * 1.0e9), bytes_accessed=int(micros * 3.0e6), transcendentals=0
@@ -759,14 +806,22 @@
     state_spec = lambda order: pl.BlockSpec(
         (state_count, inner), lambda i, info: (order(i), 0)
     )
-    normed, pre, y_val, cum, entering, rows_all = call(
-        functools.partial(forward_kernel, inner, state_count, heads, per_piece, tensor),
+    normed, pre, step_pre, y_val, cum, entering, conv, rows_all, *weights = call(
+        functools.partial(
+            forward_kernel,
+            inner,
+            state_count,
+            heads,
+            per_piece,
+            tensor,
+            len(weight_parts) if in_kernel else 0,
+        ),
         "forward",
         22,
         blocks,
         piece_specs()
+        + [fixed(part.shape) for part in weight_parts]
         + [
-            fixed((width, span)),
             fixed(choose.shape),
             fixed(chan.shape),
             fixed(head_rows.shape),
@@ -774,27 +829,34 @@
         ],
         [
             rows(width),
-            rows(span),
+            rows(conv_width),
+            rows(LANES),
             rows(inner),
             rows(LANES),
             state_spec(natural),
+            rows(conv_width),
             fixed((16, conv_width + width)),
-        ],
+        ]
+        + [fixed((width, span))] * in_kernel,
         [
             shaped((full_len, width), bf16),
-            shaped((full_len, span), f32),
+            pltpu.HBM((full_len, conv_width), bf16),
+            pltpu.HBM((full_len, LANES), f32),
             shaped((full_len, inner), f32),
-            shaped((full_len, LANES), f32),
-            shaped((blocks * state_count, inner), f32),
+            pltpu.HBM((full_len, LANES), f32),
+            pltpu.HBM((blocks * state_count, inner), f32),
+            pltpu.HBM((full_len, conv_width), f32),
             shaped((16, conv_width + width), f32),
-        ],
+        ]
+        + [shaped((width, span), bf16)] * in_kernel,
         [
             pltpu.VMEM((SPAN + 8, conv_width), f32),
             pltpu.VMEM((state_count, inner), f32),
             pltpu.VMEM((SPAN, width), bf16),
         ],
-        (*hidden_all, weights, choose, chan, head_rows, expand),
-    )
+        (*hidden_all, *weight_parts, choose, chan, head_rows, expand),
+    )
+    (weights,) = weights or weight_parts
 
     tall = lambda cols: pl.BlockSpec((piece_len, cols), lambda i, info: (i, 0))
     whole_pieces = [fixed((piece_len, width))] * tensor
@@ -816,11 +878,10 @@
         (*grad_all, normed, y_val, weights_late, weights_late, chan),
     )
 
-    cut = lambda values: [
-        values[k * piece_len : (k + 1) * piece_len] for k in range(tensor)
-    ]
-    branch = cut(branch)
-    branch_sums = scatter_near(branch, "tensor")
+    cut = lambda values, k: values[k * piece_len : (k + 1) * piece_len]
+    branch_sum = cut(branch, 2).astype(f32) + swap(cut(branch, 3), "tensor", 1).astype(f32)
+    branch_sum = branch_sum.astype(bf16)
+    branch_near = swap(cut(branch, 1), "tensor", 1)
     stats = sum_over(stats, "tensor")
 
     gate_grad, y_grad, early, gain_grad, product = call(
@@ -843,14 +904,14 @@
             tall(inner),
             fixed((width, 2 * inner)),
             fixed((8, inner)),
-            fixed((8, width)),
+            fixed((width, LANES)),
         ],
         [
             shaped((full_len, inner), bf16),
-            shaped((full_len, inner), f32),
+            shaped((full_len, inner), bf16),
             shaped((width, 2 * inner), bf16),
             shaped((8, inner), f32),
-            shaped((8, width), f32),
+            shaped((width, LANES), f32),
         ],
         [
             pltpu.VMEM((width, inner), f32),
@@ -861,118 +922,127 @@
     )
     far_first = list(range(data - 2, -1, -2))
     early_theirs = fold_pairs(early, "dp", far_first)
-    gate_grad, *held = lax.optimization_barrier(
-        (gate_grad, *branch_sums.values())
-    )
-    branch_sums = dict(zip(branch_sums, held))
-    branch_near, branch_far = scatter_far(branch, branch_sums, "tensor")
+    gate_grad, branch_sum = lax.optimization_barrier((gate_grad, branch_sum))
+    branch_far = swap(branch_sum, "tensor", 2)
 
     small_width = conv_width + width
-    half = blocks // 2
-    carried = [
-        shaped((8, conv_width), f32),
-        shaped((state_count, inner), f32),
-        shaped((width, span), f32),
-        shaped((16, small_width), f32),
-        shaped((8, inner), f32),
-    ]
-
-    def backward(at, steps, final, extra):
-        back = lambda i: blocks - 1 - at - i
-        back_rows = lambda cols: rows(cols, 0, back)
-        extra_specs = [fixed(value.shape) for value in extra[:-1]]
-        extra_specs += [pl.BlockSpec(memory_space=pl.ANY)] * len(extra[-1:])
-        outs = [shaped((width, span), bf16)] if final else carried
-        scratch = [
+    back = lambda i: blocks - 1 - i
+    back_rows = lambda cols: rows(cols, 0, back)
+    gate_lanes = inner // share
+    extra = jnp.tile(gain_grad[0].reshape(gate_lanes, share).T, (data, 1))
+    extra = jnp.pad(extra, ((0, 0), (GATE_AT, LANES - GATE_AT - gate_lanes)))
+    total, late = call(
+        functools.partial(backward_kernel, inner, state_count, heads, blocks),
+        "backward",
+        36,
+        blocks,
+        [
+            back_rows(width),
+            fixed((width, span)),
+            gate_spec,
+            back_rows(conv_width),
+            pl.BlockSpec(
+                (16, conv_width),
+                lambda i, info: (jnp.maximum(back(i) * (SPAN // 16) - 1, 0), 0),
+            ),
+            back_rows(LANES),
+            back_rows(conv_width),
+            back_rows(inner),
+            back_rows(inner),
+            back_rows(inner),
+            back_rows(LANES),
+            state_spec(back),
+            fixed((16, small_width)),
+            fixed(chan.shape),
+            fixed(head_rows.shape),
+            fixed(expand.shape),
+            fixed(gather.shape),
+            fixed((width, LANES)),
+            fixed((width, conv_width)),
+            fixed((width, LANES)),
+        ],
+        [relative(back), fixed((width, span))],
+        [shaped((full_len, width), bf16), shaped((width, span), bf16)],
+        [
             pltpu.VMEM((SPAN + 8, conv_width), f32),
             pltpu.VMEM((SPAN + 8, conv_width), f32),
             pltpu.VMEM((SPAN, span), bf16),
-        ]
-        if final:
-            scratch += [pltpu.VMEM(value.shape, f32) for value in carried[1:]]
-        return call(
-            functools.partial(backward_kernel, inner, state_count, heads, blocks, at, final),
-            "backward",
-            23,
-            steps,
-            [
-                back_rows(width),
-                fixed((width, span)),
-                gate_spec,
-                back_rows(span),
-                pl.BlockSpec(
-                    (8, span), lambda i, info: (jnp.maximum(back(i) * (SPAN // 8) - 1, 0), 0)
-                ),
-                back_rows(inner),
-                back_rows(inner),
-                back_rows(inner),
-                back_rows(LANES),
-                state_spec(back),
-                fixed((16, small_width)),
-                fixed(chan.shape),
-                fixed(head_rows.shape),
-                fixed(expand.shape),
-                fixed(gather.shape),
-            ]
-            + extra_specs,
-            [relative(back)] + [fixed(out.shape) for out in outs],
-            [shaped((full_len, width), bf16)] + outs,
-            scratch,
-            (
-                normed,
-                weights,
-                weights_late,
-                pre,
-                pre,
-                y_val,
-                y_grad,
-                gate_grad,
-                cum,
-                entering,
-                rows_all,
-                chan,
-                head_rows,
-                expand,
-                gather,
-                *extra,
-            ),
-            {24: 0} if extra else {},
-        )
-
-    total, next_rows, *rest = backward(0, half, False, ())
-    next_rows, early_theirs, branch_near, branch_far = lax.optimization_barrier(
-        (next_rows, early_theirs, branch_near, branch_far)
+            pltpu.VMEM((state_count, inner), f32),
+            pltpu.VMEM((width, span), f32),
+            pltpu.VMEM((16, conv_width), f32),
+            pltpu.VMEM((8, inner), f32),
+        ],
+        (
+            normed,
+            weights,
+            weights_late,
+            pre,
+            pre,
+            step_pre,
+            conv,
+            y_val,
+            y_grad,
+            gate_grad,
+            cum,
+            entering,
+            rows_all,
+            chan,
+            head_rows,
+            expand,
+            gather,
+            product,
+            choose,
+            extra,
+        ),
+    )
+
+    total, late, branch_near, branch_far, early_theirs = lax.optimization_barrier(
+        (total, late, branch_near, branch_far, early_theirs)
     )
     early_pieces = send_sums(
         fold_sums(early, early_theirs, "dp", far_first), "dp", far_first
     )
-    gate_lanes = inner // share
-    extra = jnp.tile(gain_grad[0].reshape(gate_lanes, share).T, (data, 1))
-    extra = jnp.pad(extra, ((0, 0), (GATE_AT, LANES - GATE_AT - gate_lanes)))
-    total, late = backward(
-        half, blocks - half, True, (next_rows, *rest, product, choose, extra, total)
-    )
-
-    total, late, *early_pieces = lax.optimization_barrier((total, late, *early_pieces))
-    total = cut(total)
-    total_sums = scatter_near(total, "tensor")
+    total_sum = cut(total, 2).astype(f32) + swap(cut(total, 3), "tensor", 1).astype(f32)
+    total_sum = total_sum.astype(bf16)
     groups = far_first[: len(far_first) // 2], far_first[len(far_first) // 2 :]
     theirs = [fold_pairs(late, "dp", steps) for steps in groups]
-    total_near, total_far = scatter_far(total, total_sums, "tensor")
-    theirs[0] = after(theirs[0], *total_sums.values())
+    total_far = swap(total_sum[: piece_len // 2], "tensor", 2)
+    total_rest = swap(total_sum[piece_len // 2 :], "tensor", 2)
+    theirs[0], total = lax.optimization_barrier((theirs[0], after(total, total_sum)))
     folded = fold_sums(late, theirs[0], "dp", groups[0])
     theirs[1] = after(theirs[1], total_far, *folded)
     folded += fold_sums(late, theirs[1], "dp", groups[1])
-    branch_far, *held = lax.optimization_barrier((branch_far, *early_pieces, folded[0]))
-    early_pieces = held[: len(early_pieces)]
-    late_part = tree_sum([piece.astype(f32) for piece in send_sums(folded, "dp", far_first)])
-    late_part, total_far = lax.optimization_barrier((late_part, total_far))
-    normed_grad = (
-        total[0].astype(f32) + total_near.astype(f32) + total_far.astype(f32)
-    )
-    early_part = tree_sum([piece.astype(f32) for piece in early_pieces])
-    misc_part = late_part[:, conv_width:]
-    shared_part = sum_over(late_part[:, inner:], "tensor")
+    branch_far, _ = lax.optimization_barrier((branch_far, folded[0]))
+    late_pieces = send_sums(folded, "dp", far_first)
+    total_own, total_near = cut(total, 0), swap(cut(total, 1), "tensor", 1)
+
+    def whole(kernel, name, out_shape, args):
+        return pl.pallas_call(
+            kernel, out_shape=out_shape, compiler_params=plain, name=name
+        )(*args)
+
+    plain = pltpu.CompilerParams(vmem_limit_bytes=24 * 1024 * 1024)
+    zx_part, out_part, rest_part = whole(
+        functools.partial(weights_kernel, len(early_pieces), inner),
+        "weight_sums",
+        [
+            shaped((2, share, inner), f32),
+            shaped((share, inner), f32),
+            shaped((share, span - inner), f32),
+        ],
+        (*early_pieces, *late_pieces),
+    )
+    rest_part, total_rest = lax.optimization_barrier((rest_part, total_rest))
+    misc_part = rest_part[:, 2 * state_count :]
+    shared = [rest_part] + [swap(rest_part, "tensor", k) for k in range(1, tensor)]
+    hidden_grad = whole(
+        functools.partial(hidden_kernel, conv_width),
+        "hidden_back",
+        shaped((piece_len, width), bf16),
+        (hidden, grad_all[0], total_own, total_near, total_far, total_rest, rows_all),
+    )
+    hidden_grad, *shared = lax.optimization_barrier((hidden_grad, *shared))
+    shared_part = tree_sum(shared)
     bc_part, misc_shared = shared_part[:, : 2 * state_count], shared_part[:, 2 * state_count :]
 
     residual = hidden.astype(f32)
@@ -980,27 +1050,20 @@
         lax.dynamic_slice_in_dim(stats[0], mine * piece_len, piece_len) / inner_total + epsilon
     )
     branch_local = (
-        branch[0].astype(f32) + branch_near.astype(f32) + branch_far.astype(f32)
+        cut(branch, 0).astype(f32) + branch_near.astype(f32) + branch_far.astype(f32)
     )
     block_out = (residual + branch_local * gate_scale[:, None]).astype(bf16)
-    row_scale = lax.rsqrt(jnp.mean(residual * residual, axis=1, keepdims=True) + epsilon)
-    scaled_grad = normed_grad * rows_all[GAIN_AT : GAIN_AT + 1, conv_width:]
-    hidden_grad = row_scale * scaled_grad - residual * row_scale**3 * jnp.mean(
-        scaled_grad * residual, axis=1, keepdims=True
-    )
-    hidden_grad = (hidden_grad + grad_all[0].astype(f32)).astype(bf16)
-
     taps_at = slice(TAPS_AT, TAPS_AT + CONV)
     head_values = misc_part[0, HEAD_AT : HEAD_AT + 3 * heads]
     return (
         block_out[:, None, :],
         hidden_grad[:, None, :],
-        jnp.stack([early_part[:, :inner], late_part[:, :inner]]),
+        zx_part,
         misc_part[:, :heads],
         bc_part,
         misc_part[:inner_share, taps_at].reshape(conv_inner.shape),
         misc_shared[inner_share : inner_share + shared_share, taps_at].reshape(-1),
-        early_part[:, inner:].T,
+        out_part.T,
         head_values[:heads],
         head_values[heads : 2 * heads],
         head_values[2 * heads :],

time: 215 us -> 187 us (0.87)
  Pallas kernels: 93.9 us -> 73.5 us
  waiting for transfers between devices: 32.9 us -> 26.6 us
  local copies, waits for them, and re-layouts: 26.2 us -> 31 us
  other arithmetic: 20.9 us -> 16.6 us
    pallas_call x5 -> x4, Pallas kernels: 93.9 us -> 70.8 us  [call(): pl.pallas_call(kernel, grid_spec=pltpu.PrefetchScalarGridSpec(num_scalar_...]
    ppermute x36 -> x37, waiting for transfers between devices: 32.9 us -> 26.6 us  [swap(): return lax.ppermute(values, axis, [(i, i ^ bits) for i in range(size)])]
    unnamed x61 -> x64, local copies, waits for them, and re-layouts: 5.16 us -> 10.8 us
    pallas_call x0 -> x2, Pallas kernels: none -> 2.66 us  [whole(): pl.pallas_call(kernel, out_shape=out_shape, compiler_params=plain, name=n...]
    reduce_sum x1 -> x0, other arithmetic: 2.4 us -> none  [per_device(): jnp.mean(residual * residual, axis=1, keepdims=True) + epsilon]
    ppermute x36 -> x37, starting transfers between devices: 36.6 us -> 35.7 us  [swap(): return lax.ppermute(values, axis, [(i, i ^ bits) for i in range(size)])]
  transfers between devices with their start and end apart: 36 -> 37, of which waited for: 9 -> 10; matrix products, arithmetic and copies ran while one was open for 14% -> 18% of each run, Pallas kernels for 39% -> 35%
where the time goes in v3:
time: 187 us; the launch traced here: 186 us
  Pallas kernels  73.5 us (39%)
  starting transfers between devices  35.7 us (19%)
  local copies, waits for them, and re-layouts  31 us (17%)
  waiting for transfers between devices  26.6 us (14%)
  other arithmetic  16.6 us (9%)
  between operations  3.07 us (2%)
    pallas_call x4, Pallas kernels, call(): pl.pallas_call(kernel, grid_spec=pltpu.PrefetchScalarGridSpec(num_scalar_...  70.8 us
    ppermute x37, starting transfers between devices, swap(): return lax.ppermute(values, axis, [(i, i ^ bits) for i in range(size)])  35.7 us
    ppermute x37, waiting for transfers between devices, swap(): return lax.ppermute(values, axis, [(i, i ^ bits) for i in range(size)])  26.6 us
    unnamed x64, local copies, waits for them, and re-layouts  10.8 us
    slice x3, local copies, waits for them, and re-layouts, per_device(): cut = lambda values, k: values[k * piece_len:(k + 1) * piece_len]  4.29 us
  transfers between devices with their start and end apart: 37, of which 10 were waited for; matrix products, arithmetic and copies ran while one was open for 18% of the time, Pallas kernels for 35%

profile of v3, /device:TPU:0, one launch (start us, length us, event | category | flops | bytes accessed | tf_op | source)
XLA Modules:
  0.0 186.4 jit_solution(15949597361047856738)
XLA Ops:
  1.2 2.6 %collective-permute-start = (bf16[512,768]{1,0:T(8,128)(2,1)}, bf16[512,768]{1,0:T(8,128)(2,1)}, u32[]{:S(2)}, u32[]{:S(2)}) collective-permute-start(bf16[512,768]{1,0:T(8,128)(2,1)} %bitcast.89), channel_id=1, source_target_pairs={{0,2},{1,3},{2,0},{3,1},{4,6},{5,7},{6,4},{7,5},{8,10},{9,11},{10,... | collective-permute-start | bytes 2359304 | tf_op jit(solution)/shard_map/ppermute | solution.py:555
  3.7 0.9 slice_bitcast_fusion
  4.7 0.8 copy.45
  5.5 0.8 reshape.144
  6.3 0.8 reshape.143
  7.0 0.8 copy.46
  7.9 0.9 concatenate.10.refs_4_
  8.8 1.6 collective-permute-start.8
  10.4 2.6 %collective-permute-start.7 = (bf16[96,768]{1,0:T(8,128)(2,1)S(1)}, bf16[96,768]{1,0:T(8,128)(2,1)S(1)}, u32[]{:S(2)}, u32[]{:S(2)}) collective-permute-start(bf16[96,768]{1,0:T(8,128)(2,1)S(1)} %concatenate.10.refs_4_), channel_id=1, source_target_pairs={{0,16},{4,20},{8,24},{12,28},{16,0},{20,4},{24,8},{28,12},{1,17},{... | collective-permute-start | bytes 442376 | tf_op jit(solution)/shard_map/ppermute | solution.py:555
  13.2 1.2 negate_bitcast_fusion
  14.4 0.7 compare_convert_fusion.refs_11_.refs_15_
  15.1 1.6 pad_maximum_fusion.5
  18.8 1.5 fusion.refs_8_.refs_18_
  20.3 1.6 fusion.21
  21.8 1.6 collective-permute-start.9
  26.1 1.2 stack.88.info_ref
  28.5 1.1 pad_maximum_fusion.1.refs_6_
  29.6 1.6 collective-permute-start.10
  31.2 1.4 fusion.8.refs_16_
  32.6 1.0 select_bitcast_fusion.1
  33.7 0.7 collective-permute-start.12
  34.5 3.5 %collective-permute-start.13 = (bf16[2,96,768]{2,1,0:T(8,128)(2,1)S(1)}, bf16[2,96,768]{2,1,0:T(8,128)(2,1)S(1)}, u32[]{:S(2)}, u32[]{:S(2)}) collective-permute-start(bf16[2,96,768]{2,1,0:T(8,128)(2,1)S(1)} %pad_maximum_fusion.2), channel_id=1, source_target_pairs={{0,16},{4,20},{8,24},{12,28},{16,0},{20,4},{24,8},{28,12},{1,17},{... | collective-permute-start | bytes 884744 | tf_op jit(solution)/shard_map/ppermute | solution.py:555
  38.2 5.0 %collective-permute-done.10.refs_7_ = bf16[3,96,768]{2,1,0:T(8,128)(2,1)} collective-permute-done((bf16[3,96,768]{2,1,0:T(8,128)(2,1)S(1)}, bf16[3,96,768]{2,1,0:T(8,128)(2,1)}, u32[]{:S(2)}, u32[]{:S(2)}) %collective-permute-start.10) | collective-permute-done | bytes 442400 | tf_op jit(solution)/shard_map/ppermute | solution.py:555
  43.7 0.9 copy-done.9
  45.2 18.9 %forward.1 = (bf16[2048,768]{1,0:T(8,128)(2,1)S(1)}, bf16[2048,640]{1,0:T(8,128)(2,1)}, f32[2048,128]{1,0:T(8,128)}, f32[2048,384]{1,0:T(8,128)S(1)}, f32[2048,1...) custom-call(s32[5]{0:T(128)S(1)} %copy-done.14, ...), custom_call_target="tpu_custom_call" | custom-call | flops 22000001024 | bytes 66000000 | tf_op jit(solution)/shard_map/forward/pallas_call | solution.py:778
  64.2 1.0 copy-done.21
  65.8 1.7 collective-permute-done.11.refs_3_
  67.6 7.9 %branch.1 = (f32[2048,384]{1,0:T(8,128)S(1)}, bf16[2048,768]{1,0:T(8,128)(2,1)S(1)}, f32[8,2048]{1,0:T(8,128)S(1)}) custom-call(s32[5]{0:T(128)S(1)} %copy-done.15, bf16[512,768]{1,0:T(8,128)(2,1)S(1)} %bitcast.99, bf16[512,768]{1,0:T(8,128)(2,1)S(1)} %collective-permute-done.1.refs_1_, bf16[512,768]{1,0:T(8,128)(2,1)S(1)} %collective-permute-done.2.refs_2_, ...), custom_call_target="tpu_custom_call" | custom-call | flops 11000000512 | bytes 33000000 | tf_op jit(solution)/shard_map/branch/pallas_call | solution.py:778
  75.5 1.7 collective-permute-start.16
  77.7 1.2 fusion.19
  79.8 1.7 collective-permute-done.17
  81.6 8.4 %gate_back.1 = (bf16[2048,384]{1,0:T(8,128)(2,1)S(1)}, bf16[2048,384]{1,0:T(8,128)(2,1)S(1)}, bf16[768,768]{1,0:T(8,128)(2,1)S(1)}, f32[8,384]{1,0:T(8,128)S(1)}, f32[768,128]{1,0:T(8,128)S(1)}) custom-call(s32[5]{0:T(128)S(1)} %copy-done.15, bf16[512,768]{1,0:T(8,128)(2,1)S(1)} %bitcast.100, bf16[512,768]{1,0:T(8,128)(2,1)S(1)} %collective-permute-done.1.refs_1_, ...), custom_call_target="tpu_custom_call" | custom-call | flops 12999999488 | bytes 39000000 | tf_op jit(solution)/shard_map/gate_back/pallas_call | solution.py:778
  90.0 1.1 copy-done.18
  91.2 1.2 copy-done.19
  92.4 0.8 copy-done.20
  94.2 0.9 pad.24.refs_19_
  95.1 1.6 add_convert_fusion.2
  96.7 1.3 collective-permute-start.20
  98.0 35.6 %backward.1 = (bf16[2048,768]{1,0:T(8,128)(2,1)}, bf16[768,768]{1,0:T(8,128)(2,1)}) custom-call(s32[5]{0:T(128)} %stack.88.info_ref, bf16[2048,768]{1,0:T(8,128)(2,1)} %copy-done.16, bf16[768,768]{1,0:T(8,128)(2,1)} %copy-done.21, bf16[768,768]{1,0:T(8,128)(2,1)} %bitcast.96, bf16[2048,640]{1,0:T(8,128)(2,1)} %get-tuple-element.65.refs_3_.refs_4_, ...), custom_call_target="tpu_custom_call" | custom-call | flops 35999997952 | bytes 108000000 | tf_op jit(solution)/shard_map/backward/pallas_call | solution.py:778
  133.6 2.1 %slice.143 = bf16[512,768]{1,0:T(8,128)(2,1)} slice(bf16[2048,768]{1,0:T(8,128)(2,1)} %get-tuple-element.88), slice={[1536:2048], [0:768]} | slice | bytes 1572864 | tf_op jit(solution)/shard_map/slice | solution.py:881
  135.7 1.3 dynamic-slice_bitcast_fusion.1
  137.1 0.8 collective-permute-start.22
  138.0 3.7 %collective-permute-start.26 = (bf16[96,768]{1,0:T(8,128)(2,1)S(1)}, bf16[96,768]{1,0:T(8,128)(2,1)S(1)}, u32[]{:S(2)}, u32[]{:S(2)}) collective-permute-start(bf16[96,768]{1,0:T(8,128)(2,1)S(1)} %get-tuple-element.160), channel_id=1, source_target_pairs={{0,24},{4,28},{8,16},{12,20},{16,8},{20,12},{24,0},{28,4},{1,25},{... | collective-permute-start | bytes 442376 | tf_op jit(solution)/shard_map/ppermute | solution.py:555
  141.7 0.8 collective-permute-start.28
  142.5 1.4 collective-permute-start.31
  143.9 1.3 add_convert_fusion.1
  145.3 1.7 collective-permute-done.22
  147.0 0.8 collective-permute-start.25
  147.9 1.0 fusion.18
  148.8 4.0 %collective-permute-done.31 = bf16[2,96,768]{2,1,0:T(8,128)(2,1)S(1)} collective-permute-done((bf16[2,96,768]{2,1,0:T(8,128)(2,1)S(1)}, bf16[2,96,768]{2,1,0:T(8,128)(2,1)S(1)}, u32[]{:S(2)}, u32[]{:S(2)}) %collective-permute-start.31) | collective-permute-done | bytes 294944 | tf_op jit(solution)/shard_map/ppermute | solution.py:555
  152.9 4.4 %collective-permute-done.25.far_ref = bf16[256,768]{1,0:T(8,128)(2,1)S(1)} collective-permute-done((bf16[256,768]{1,0:T(8,128)(2,1)S(1)}, bf16[256,768]{1,0:T(8,128)(2,1)S(1)}, u32[]{:S(2)}, u32[]{:S(2)}) %collective-permute-start.25) | collective-permute-done | bytes 393248 | tf_op jit(solution)/shard_map/ppermute | solution.py:555
  157.3 0.8 collective-permute-start.33
  158.2 3.7 %collective-permute-start.29 = (bf16[96,768]{1,0:T(8,128)(2,1)S(1)}, bf16[96,768]{1,0:T(8,128)(2,1)S(1)}, u32[]{:S(2)}, u32[]{:S(2)}) collective-permute-start(bf16[96,768]{1,0:T(8,128)(2,1)S(1)} %get-tuple-element.164), channel_id=1, source_target_pairs={{0,24},{4,28},{8,16},{12,20},{16,8},{20,12},{24,0},{28,4},{1,25},{... | collective-permute-start | bytes 442376 | tf_op jit(solution)/shard_map/ppermute | solution.py:555
  161.9 0.8 collective-permute-start.32
  162.6 2.9 %fusion.1 = bf16[512,1,768]{2,0,1:T(8,128)(2,1)} fusion(bf16[512,768]{1,0:T(8,128)(2,1)} %collective-permute-done.20, bf16[512,768]{1,0:T(8,128)(2,1)} %collective-permute-done.19, f32[512]{0:T(512)S(1)} %bitcast.109, bf16[2048,768]{1,0:T(8,128)(2,1)} %copy-done.1, bf16[512,1,768]{2,0,1:T(8,128)(2,1)S(1)} %copy-done), kind=kLoop, calls=%fused_computation.5 | loop fusion | flops 3538944 | bytes 3934208 | tf_op jit(solution)/shard_map/broadcast_in_dim | solution.py:1059
  165.6 1.3 collective-permute-done.29.refs_4_
  166.9 5.7 %collective-permute-done.30.refs_5_ = bf16[96,768]{1,0:T(8,128)(2,1)S(1)} collective-permute-done((bf16[96,768]{1,0:T(8,128)(2,1)S(1)}, bf16[96,768]{1,0:T(8,128)(2,1)S(1)}, u32[]{:S(2)}, u32[]{:S(2)}) %collective-permute-start.30) | collective-permute-done | bytes 147488 | tf_op jit(solution)/shard_map/ppermute | solution.py:555
  172.6 0.8 weight_sums.1
  173.4 0.8 copy-done.7
  174.2 1.2 collective-permute-start.35
  178.9 1.0 copy-done.6
  179.9 1.0 copy-done.8
  180.9 1.8 hidden_back.1
  183.3 1.1 add_add_fusion
  (145 shorter events, 15.8 us)
Async XLA Ops:
  0.6 37.3 %collective-permute-start.3 = (bf16[512,768]{1,0:T(8,128)(2,1)}, bf16[512,768]{1,0:T(8,128)(2,1)}, u32[]{:S(2)}, u32[]{:S(2)}) collective-permute-start(bf16[512,768]{1,0:T(8,128)(2,1)} %bitcast.88), channel_id=1, source_target_pairs={{0,1},{1,0},{2,3},{3,2},{4,5},{5,4},{6,7},{7,6},{8,9},{9,8},{10,11... | collective-permute-start | bytes 2359304 | tf_op jit(solution)/shard_map/ppermute | solution.py:555
  1.2 22.3 %collective-permute-start = (bf16[512,768]{1,0:T(8,128)(2,1)}, bf16[512,768]{1,0:T(8,128)(2,1)}, u32[]{:S(2)}, u32[]{:S(2)}) collective-permute-start(bf16[512,768]{1,0:T(8,128)(2,1)} %bitcast.89), channel_id=1, source_target_pairs={{0,2},{1,3},{2,0},{3,1},{4,6},{5,7},{6,4},{7,5},{8,10},{9,11},{10,... | collective-permute-start | bytes 2359304 | tf_op jit(solution)/shard_map/ppermute | solution.py:555
  4.7 14.1 %copy-start.24 = (bf16[96,384]{1,0:T(8,128)(2,1)}, bf16[96,384]{1,0:T(8,128)(2,1)S(1)}, u32[]{:S(2)}) copy-start(bf16[96,384]{1,0:T(8,128)(2,1)S(1)} %get-tuple-element.180) | copy-start | bytes 221188
  8.8 13.1 %collective-permute-start.8 = (bf16[96,768]{1,0:T(8,128)(2,1)S(1)}, bf16[96,768]{1,0:T(8,128)(2,1)S(1)}, u32[]{:S(2)}, u32[]{:S(2)}) collective-permute-start(bf16[96,768]{1,0:T(8,128)(2,1)S(1)} %concatenate.10.refs_4_), channel_id=1, source_target_pairs={{0,8},{4,12},{8,0},{12,4},{16,24},{20,28},{24,16},{28,20},{1,9},{5... | collective-permute-start | bytes 442376 | tf_op jit(solution)/shard_map/ppermute | solution.py:555
  10.4 16.9 %collective-permute-start.7 = (bf16[96,768]{1,0:T(8,128)(2,1)S(1)}, bf16[96,768]{1,0:T(8,128)(2,1)S(1)}, u32[]{:S(2)}, u32[]{:S(2)}) collective-permute-start(bf16[96,768]{1,0:T(8,128)(2,1)S(1)} %concatenate.10.refs_4_), channel_id=1, source_target_pairs={{0,16},{4,20},{8,24},{12,28},{16,0},{20,4},{24,8},{28,12},{1,17},{... | collective-permute-start | bytes 442376 | tf_op jit(solution)/shard_map/ppermute | solution.py:555
  13.0 14.8 %collective-permute-start.6 = (bf16[96,768]{1,0:T(8,128)(2,1)S(1)}, bf16[96,768]{1,0:T(8,128)(2,1)S(1)}, u32[]{:S(2)}, u32[]{:S(2)}) collective-permute-start(bf16[96,768]{1,0:T(8,128)(2,1)S(1)} %concatenate.10.refs_4_), channel_id=1, source_target_pairs={{0,24},{4,28},{8,16},{12,20},{16,8},{20,12},{24,0},{28,4},{1,25},{... | collective-permute-start | bytes 442376 | tf_op jit(solution)/shard_map/ppermute | solution.py:555
  13.2 5.5 %copy-start.28 = (s32[384]{0:T(512)}, s32[384]{0:T(512)S(1)}, u32[]{:S(2)}) copy-start(s32[384]{0:T(512)S(1)} %add_select_fusion) | copy-start | bytes 4612
  18.7 1.5 copy-start.29
  18.8 4.7 %copy-start.30 = (f32[1,6]{1,0:T(1,128)S(1)}, f32[1,6]{1,0:T(1,128)}, u32[]{:S(2)}) copy-start(f32[1,6]{1,0:T(1,128)} %negate_bitcast_fusion) | copy-start | bytes 76
  20.2 43.9 %copy-start.2 = (bf16[768,1408]{1,0:T(8,128)(2,1)}, bf16[768,1408]{1,0:T(8,128)(2,1)S(1)}, u32[]{:S(2)}) copy-start(bf16[768,1408]{1,0:T(8,128)(2,1)S(1)} %fusion.refs_8_.refs_18_) | copy-start | bytes 6488068
  20.2 23.5 %copy-start = (bf16[512,1,768]{2,0,1:T(8,128)(2,1)S(1)}, bf16[512,1,768]{2,0,1:T(8,128)(2,1)}, u32[]{:S(2)}) copy-start(bf16[512,1,768]{2,0,1:T(8,128)(2,1)} %param.15) | copy-start | bytes 2359300
  20.3 61.3 %copy-start.12 = (f32[8,384]{1,0:T(8,128)}, f32[8,384]{1,0:T(8,128)S(1)}, u32[]{:S(2)}) copy-start(f32[8,384]{1,0:T(8,128)S(1)} %select_maximum_fusion.refs_9_.refs_8_.refs_10_.refs_13_) | copy-start | bytes 36868
  21.8 6.0 %copy-start.25 = (bf16[96,768]{1,0:T(8,128)(2,1)}, bf16[96,768]{1,0:T(8,128)(2,1)S(1)}, u32[]{:S(2)}) copy-start(bf16[96,768]{1,0:T(8,128)(2,1)S(1)} %collective-permute-done.8) | copy-start | bytes 442372
  21.8 7.8 %collective-permute-start.9 = (bf16[96,768]{1,0:T(8,128)(2,1)}, bf16[96,768]{1,0:T(8,128)(2,1)}, u32[]{:S(2)}, u32[]{:S(2)}) collective-permute-start(bf16[96,768]{1,0:T(8,128)(2,1)} %pad_maximum_fusion.5), channel_id=1, source_target_pairs={{0,4},{4,0},{8,12},{12,8},{16,20},{20,16},{24,28},{28,24},{1,5},{5... | collective-permute-start | bytes 442376 | tf_op jit(solution)/shard_map/ppermute | solution.py:555
  23.4 19.7 %collective-permute-start.4 = (bf16[512,768]{1,0:T(8,128)(2,1)}, bf16[512,768]{1,0:T(8,128)(2,1)}, u32[]{:S(2)}, u32[]{:S(2)}) collective-permute-start(bf16[512,768]{1,0:T(8,128)(2,1)} %collective-permute-done.refs_2_), channel_id=1, source_target_pairs={{0,1},{1,0},{2,3},{3,2},{4,5},{5,4},{6,7},{7,6},{8,9},{9,8},{10,11... | collective-permute-start | bytes 2359304 | tf_op jit(solution)/shard_map/ppermute | solution.py:555
  24.1 40.0 %copy-start.13 = (f32[8,128]{1,0:T(8,128)}, f32[8,128]{1,0:T(8,128)S(1)}, u32[]{:S(2)}) copy-start(f32[8,128]{1,0:T(8,128)S(1)} %select_maximum_fusion.1.refs_10_.refs_14_) | copy-start | bytes 12292
  27.3 7.1 %collective-permute-start.5 = (bf16[96,768]{1,0:T(8,128)(2,1)S(1)}, bf16[96,768]{1,0:T(8,128)(2,1)}, u32[]{:S(2)}, u32[]{:S(2)}) collective-permute-start(bf16[96,768]{1,0:T(8,128)(2,1)S(1)} %concatenate.10.refs_4_), channel_id=1, source_target_pairs={{0,4},{4,0},{8,12},{12,8},{16,20},{20,16},{24,28},{28,24},{1,5},{5... | collective-permute-start | bytes 442376 | tf_op jit(solution)/shard_map/ppermute | solution.py:555
  29.6 13.5 %collective-permute-start.10 = (bf16[3,96,768]{2,1,0:T(8,128)(2,1)S(1)}, bf16[3,96,768]{2,1,0:T(8,128)(2,1)}, u32[]{:S(2)}, u32[]{:S(2)}) collective-permute-start(bf16[3,96,768]{2,1,0:T(8,128)(2,1)S(1)} %pad_maximum_fusion.1.refs_6_), channel_id=1, source_target_pairs={{0,4},{4,0},{8,12},{12,8},{16,20},{20,16},{24,28},{28,24},{1,5},{5... | collective-permute-start | bytes 1327112 | tf_op jit(solution)/shard_map/ppermute | solution.py:555
  33.7 31.9 %collective-permute-start.12 = (bf16[2,96,768]{2,1,0:T(8,128)(2,1)S(1)}, bf16[2,96,768]{2,1,0:T(8,128)(2,1)S(1)}, u32[]{:S(2)}, u32[]{:S(2)}) collective-permute-start(bf16[2,96,768]{2,1,0:T(8,128)(2,1)S(1)} %pad_maximum_fusion.2), channel_id=1, source_target_pairs={{0,8},{4,12},{8,0},{12,4},{16,24},{20,28},{24,16},{28,20},{1,9},{5... | collective-permute-start | bytes 884744 | tf_op jit(solution)/shard_map/ppermute | solution.py:555
  34.5 31.2 %collective-permute-start.13 = (bf16[2,96,768]{2,1,0:T(8,128)(2,1)S(1)}, bf16[2,96,768]{2,1,0:T(8,128)(2,1)S(1)}, u32[]{:S(2)}, u32[]{:S(2)}) collective-permute-start(bf16[2,96,768]{2,1,0:T(8,128)(2,1)S(1)} %pad_maximum_fusion.2), channel_id=1, source_target_pairs={{0,16},{4,20},{8,24},{12,28},{16,0},{20,4},{24,8},{28,12},{1,17},{... | collective-permute-start | bytes 884744 | tf_op jit(solution)/shard_map/ppermute | solution.py:555
  37.9 27.8 %collective-permute-start.14 = (bf16[2,96,768]{2,1,0:T(8,128)(2,1)S(1)}, bf16[2,96,768]{2,1,0:T(8,128)(2,1)S(1)}, u32[]{:S(2)}, u32[]{:S(2)}) collective-permute-start(bf16[2,96,768]{2,1,0:T(8,128)(2,1)S(1)} %pad_maximum_fusion.2), channel_id=1, source_target_pairs={{0,24},{4,28},{8,16},{12,20},{16,8},{20,12},{24,0},{28,4},{1,25},{... | collective-permute-start | bytes 884744 | tf_op jit(solution)/shard_map/ppermute | solution.py:555
  43.2 22.7 %collective-permute-start.1 = (bf16[512,768]{1,0:T(8,128)(2,1)}, bf16[512,768]{1,0:T(8,128)(2,1)S(1)}, u32[]{:S(2)}, u32[]{:S(2)}) collective-permute-start(bf16[512,768]{1,0:T(8,128)(2,1)} %bitcast.97), channel_id=1, source_target_pairs={{0,1},{1,0},{2,3},{3,2},{4,5},{5,4},{6,7},{7,6},{8,9},{9,8},{10,11... | collective-permute-start | bytes 2359304 | tf_op jit(solution)/shard_map/ppermute | solution.py:555
  43.2 22.0 %collective-permute-start.2 = (bf16[512,768]{1,0:T(8,128)(2,1)}, bf16[512,768]{1,0:T(8,128)(2,1)S(1)}, u32[]{:S(2)}, u32[]{:S(2)}) collective-permute-start(bf16[512,768]{1,0:T(8,128)(2,1)} %bitcast.98), channel_id=1, source_target_pairs={{0,2},{1,3},{2,0},{3,1},{4,6},{5,7},{6,4},{7,5},{8,10},{9,11},{10,... | collective-permute-start | bytes 2359304 | tf_op jit(solution)/shard_map/ppermute | solution.py:555
  43.7 0.9 copy-start.9
  64.1 1.0 copy-start.21
  65.2 16.4 %copy-start.16 = (bf16[2048,768]{1,0:T(8,128)(2,1)}, bf16[2048,768]{1,0:T(8,128)(2,1)S(1)}, u32[]{:S(2)}) copy-start(bf16[2048,768]{1,0:T(8,128)(2,1)S(1)} %get-tuple-element.61.refs_4_.refs_5_.refs_0_) | copy-start | bytes 9437188
  65.2 16.4 %copy-start.17 = (f32[2048,384]{1,0:T(8,128)}, f32[2048,384]{1,0:T(8,128)S(1)}, u32[]{:S(2)}) copy-start(f32[2048,384]{1,0:T(8,128)S(1)} %get-tuple-element.62.refs_5_.refs_9_.refs_7_) | copy-start | bytes 9437188
  65.2 2.4 %copy-start.4 = (bf16[512,1,768]{2,0,1:T(8,128)(2,1)S(1)}, bf16[512,1,768]{2,0,1:T(8,128)(2,1)}, u32[]{:S(2)}) copy-start(bf16[512,1,768]{2,0,1:T(8,128)(2,1)} %param.16) | copy-start | bytes 2359300
  65.2 2.4 %copy-start.15 = (s32[5]{0:T(128)S(1)}, s32[5]{0:T(128)}, u32[]{:S(2)}) copy-start(s32[5]{0:T(128)} %stack.88.info_ref) | copy-start | bytes 64
  65.2 2.4 %collective-permute-start.11 = (bf16[512,768]{1,0:T(8,128)(2,1)S(1)}, bf16[512,768]{1,0:T(8,128)(2,1)S(1)}, u32[]{:S(2)}, u32[]{:S(2)}) collective-permute-start(bf16[512,768]{1,0:T(8,128)(2,1)S(1)} %collective-permute-done.2.refs_2_), channel_id=1, source_target_pairs={{0,1},{1,0},{2,3},{3,2},{4,5},{5,4},{6,7},{7,6},{8,9},{9,8},{10,11... | collective-permute-start | bytes 2359304 | tf_op jit(solution)/shard_map/ppermute | solution.py:555
  65.8 15.8 %copy-start.3 = (bf16[4,2,96,768]{3,2,1,0:T(8,128)(2,1)}, bf16[4,2,96,768]{3,2,1,0:T(8,128)(2,1)S(1)}, u32[]{:S(2)}) copy-start(bf16[4,2,96,768]{3,2,1,0:T(8,128)(2,1)S(1)} %bitcast_dynamic-update-slice_fusion) | copy-start | bytes 3538948
  75.5 3.5 %copy-start.1 = (bf16[2048,768]{1,0:T(8,128)(2,1)}, bf16[2048,768]{1,0:T(8,128)(2,1)S(1)}, u32[]{:S(2)}) copy-start(bf16[2048,768]{1,0:T(8,128)(2,1)S(1)} %get-tuple-element.63) | copy-start | bytes 9437188
  75.5 4.3 %collective-permute-start.16 = (f32[8,2048]{1,0:T(8,128)S(1)}, f32[8,2048]{1,0:T(8,128)S(1)}, u32[]{:S(2)}, u32[]{:S(2)}) collective-permute-start(f32[8,2048]{1,0:T(8,128)S(1)} %get-tuple-element.68), channel_id=1, source_target_pairs={{0,2},{1,3},{2,0},{3,1},{4,6},{5,7},{6,4},{7,5},{8,10},{9,11},{10,... | collective-permute-start | bytes 196616 | tf_op jit(solution)/shard_map/ppermute | solution.py:555
  77.2 4.4 %collective-permute-start.17 = (f32[8,2048]{1,0:T(8,128)S(1)}, f32[8,2048]{1,0:T(8,128)S(1)}, u32[]{:S(2)}, u32[]{:S(2)}) collective-permute-start(f32[8,2048]{1,0:T(8,128)S(1)} %get-tuple-element.68), channel_id=1, source_target_pairs={{0,3},{1,2},{2,1},{3,0},{4,7},{5,6},{6,5},{7,4},{8,11},{9,10},{10,... | collective-permute-start | bytes 196616 | tf_op jit(solution)/shard_map/ppermute | solution.py:555
  77.2 4.4 %collective-permute-start.15 = (f32[8,2048]{1,0:T(8,128)S(1)}, f32[8,2048]{1,0:T(8,128)S(1)}, u32[]{:S(2)}, u32[]{:S(2)}) collective-permute-start(f32[8,2048]{1,0:T(8,128)S(1)} %get-tuple-element.68), channel_id=1, source_target_pairs={{0,1},{1,0},{2,3},{3,2},{4,5},{5,4},{6,7},{7,6},{8,9},{9,8},{10,11... | collective-permute-start | bytes 196616 | tf_op jit(solution)/shard_map/ppermute | solution.py:555
  78.9 16.2 %collective-permute-start.18 = (bf16[512,768]{1,0:T(8,128)(2,1)}, bf16[512,768]{1,0:T(8,128)(2,1)}, u32[]{:S(2)}, u32[]{:S(2)}) collective-permute-start(bf16[512,768]{1,0:T(8,128)(2,1)} %get-tuple-element.156), channel_id=1, source_target_pairs={{0,1},{1,0},{2,3},{3,2},{4,5},{5,4},{6,7},{7,6},{8,9},{9,8},{10,11... | collective-permute-start | bytes 2359304 | tf_op jit(solution)/shard_map/ppermute | solution.py:555
  78.9 54.7 %collective-permute-start.19 = (bf16[512,768]{1,0:T(8,128)(2,1)}, bf16[512,768]{1,0:T(8,128)(2,1)}, u32[]{:S(2)}, u32[]{:S(2)}) collective-permute-start(bf16[512,768]{1,0:T(8,128)(2,1)} %get-tuple-element.155), channel_id=1, source_target_pairs={{0,1},{1,0},{2,3},{3,2},{4,5},{5,4},{6,7},{7,6},{8,9},{9,8},{10,11... | collective-permute-start | bytes 2359304 | tf_op jit(solution)/shard_map/ppermute | solution.py:555
  90.0 1.2 copy-start.18
  91.2 1.2 copy-start.19
  92.4 0.8 copy-start.20
  93.5 40.1 %collective-permute-start.21 = (bf16[4,96,768]{2,1,0:T(8,128)(2,1)S(1)}, bf16[4,96,768]{2,1,0:T(8,128)(2,1)S(1)}, u32[]{:S(2)}, u32[]{:S(2)}) collective-permute-start(bf16[4,96,768]{2,1,0:T(8,128)(2,1)S(1)} %pad_maximum_fusion), channel_id=1, source_target_pairs={{0,4},{4,0},{8,12},{12,8},{16,20},{20,16},{24,28},{28,24},{1,5},{5... | collective-permute-start | bytes 1769480 | tf_op jit(solution)/shard_map/ppermute | solution.py:555
  96.7 36.9 %collective-permute-start.20 = (bf16[512,768]{1,0:T(8,128)(2,1)S(1)}, bf16[512,768]{1,0:T(8,128)(2,1)}, u32[]{:S(2)}, u32[]{:S(2)}) collective-permute-start(bf16[512,768]{1,0:T(8,128)(2,1)S(1)} %add_convert_fusion.2), channel_id=1, source_target_pairs={{0,2},{1,3},{2,0},{3,1},{4,6},{5,7},{6,4},{7,5},{8,10},{9,11},{10,... | collective-permute-start | bytes 2359304 | tf_op jit(solution)/shard_map/ppermute | solution.py:555
  135.7 6.8 %collective-permute-start.23 = (bf16[512,768]{1,0:T(8,128)(2,1)}, bf16[512,768]{1,0:T(8,128)(2,1)}, u32[]{:S(2)}, u32[]{:S(2)}) collective-permute-start(bf16[512,768]{1,0:T(8,128)(2,1)} %slice.143), channel_id=1, source_target_pairs={{0,1},{1,0},{2,3},{3,2},{4,5},{5,4},{6,7},{7,6},{8,9},{9,8},{10,11... | collective-permute-start | bytes 2359304 | tf_op jit(solution)/shard_map/ppermute | solution.py:555
  135.7 8.2 %copy-start.22 = (bf16[2048,768]{1,0:T(8,128)(2,1)S(1)}, bf16[2048,768]{1,0:T(8,128)(2,1)}, u32[]{:S(2)}) copy-start(bf16[2048,768]{1,0:T(8,128)(2,1)} %get-tuple-element.88) | copy-start | bytes 9437188
  137.1 9.9 %collective-permute-start.22 = (bf16[2,96,768]{2,1,0:T(8,128)(2,1)S(1)}, bf16[2,96,768]{2,1,0:T(8,128)(2,1)S(1)}, u32[]{:S(2)}, u32[]{:S(2)}) collective-permute-start(bf16[2,96,768]{2,1,0:T(8,128)(2,1)S(1)} %pad_maximum_fusion.3), channel_id=1, source_target_pairs={{0,4},{4,0},{8,12},{12,8},{16,20},{20,16},{24,28},{28,24},{1,5},{5... | collective-permute-start | bytes 884744 | tf_op jit(solution)/shard_map/ppermute | solution.py:555
  138.0 20.2 %collective-permute-start.26 = (bf16[96,768]{1,0:T(8,128)(2,1)S(1)}, bf16[96,768]{1,0:T(8,128)(2,1)S(1)}, u32[]{:S(2)}, u32[]{:S(2)}) collective-permute-start(bf16[96,768]{1,0:T(8,128)(2,1)S(1)} %get-tuple-element.160), channel_id=1, source_target_pairs={{0,24},{4,28},{8,16},{12,20},{16,8},{20,12},{24,0},{28,4},{1,25},{... | collective-permute-start | bytes 442376 | tf_op jit(solution)/shard_map/ppermute | solution.py:555
  141.7 20.2 %collective-permute-start.27 = (bf16[96,768]{1,0:T(8,128)(2,1)S(1)}, bf16[96,768]{1,0:T(8,128)(2,1)S(1)}, u32[]{:S(2)}, u32[]{:S(2)}) collective-permute-start(bf16[96,768]{1,0:T(8,128)(2,1)S(1)} %get-tuple-element.159), channel_id=1, source_target_pairs={{0,16},{4,20},{8,24},{12,28},{16,0},{20,4},{24,8},{28,12},{1,17},{... | collective-permute-start | bytes 442376 | tf_op jit(solution)/shard_map/ppermute | solution.py:555
  141.7 20.2 %collective-permute-start.28 = (bf16[96,768]{1,0:T(8,128)(2,1)S(1)}, bf16[96,768]{1,0:T(8,128)(2,1)S(1)}, u32[]{:S(2)}, u32[]{:S(2)}) collective-permute-start(bf16[96,768]{1,0:T(8,128)(2,1)S(1)} %get-tuple-element.158), channel_id=1, source_target_pairs={{0,8},{4,12},{8,0},{12,4},{16,24},{20,28},{24,16},{28,20},{1,9},{5... | collective-permute-start | bytes 442376 | tf_op jit(solution)/shard_map/ppermute | solution.py:555
  142.5 5.3 %copy-start.23 = (bf16[768,768]{1,0:T(8,128)(2,1)S(1)}, bf16[768,768]{1,0:T(8,128)(2,1)}, u32[]{:S(2)}) copy-start(bf16[768,768]{1,0:T(8,128)(2,1)} %get-tuple-element.83) | copy-start | bytes 3538948
  142.5 10.4 %collective-permute-start.31 = (bf16[2,96,768]{2,1,0:T(8,128)(2,1)S(1)}, bf16[2,96,768]{2,1,0:T(8,128)(2,1)S(1)}, u32[]{:S(2)}, u32[]{:S(2)}) collective-permute-start(bf16[2,96,768]{2,1,0:T(8,128)(2,1)S(1)} %pad_maximum_fusion.4), channel_id=1, source_target_pairs={{0,4},{4,0},{8,12},{12,8},{16,20},{20,16},{24,28},{28,24},{1,5},{5... | collective-permute-start | bytes 884744 | tf_op jit(solution)/shard_map/ppermute | solution.py:555
  147.0 10.3 %collective-permute-start.25 = (bf16[256,768]{1,0:T(8,128)(2,1)S(1)}, bf16[256,768]{1,0:T(8,128)(2,1)S(1)}, u32[]{:S(2)}, u32[]{:S(2)}) collective-permute-start(bf16[256,768]{1,0:T(8,128)(2,1)S(1)} %get-tuple-element.174), channel_id=1, source_target_pairs={{0,2},{1,3},{2,0},{3,1},{4,6},{5,7},{6,4},{7,5},{8,10},{9,11},{10,... | collective-permute-start | bytes 1179656 | tf_op jit(solution)/shard_map/ppermute | solution.py:555
  152.9 26.0 %collective-permute-start.24 = (bf16[512,768]{1,0:T(8,128)(2,1)}, bf16[512,768]{1,0:T(8,128)(2,1)S(1)}, u32[]{:S(2)}, u32[]{:S(2)}) collective-permute-start(bf16[512,768]{1,0:T(8,128)(2,1)} %get-tuple-element.153), channel_id=1, source_target_pairs={{0,1},{1,0},{2,3},{3,2},{4,5},{5,4},{6,7},{7,6},{8,9},{9,8},{10,11... | collective-permute-start | bytes 2359304 | tf_op jit(solution)/shard_map/ppermute | solution.py:555
  157.3 8.3 %copy-start.5 = (bf16[256,768]{1,0:T(8,128)(2,1)}, bf16[256,768]{1,0:T(8,128)(2,1)S(1)}, u32[]{:S(2)}) copy-start(bf16[256,768]{1,0:T(8,128)(2,1)S(1)} %collective-permute-done.25.far_ref) | copy-start | bytes 1179652
  157.3 16.1 %collective-permute-start.33 = (bf16[256,768]{1,0:T(8,128)(2,1)S(1)}, bf16[256,768]{1,0:T(8,128)(2,1)S(1)}, u32[]{:S(2)}, u32[]{:S(2)}) collective-permute-start(bf16[256,768]{1,0:T(8,128)(2,1)S(1)} %get-tuple-element.173), channel_id=1, source_target_pairs={{0,2},{1,3},{2,0},{3,1},{4,6},{5,7},{6,4},{7,5},{8,10},{9,11},{10,... | collective-permute-start | bytes 1179656 | tf_op jit(solution)/shard_map/ppermute | solution.py:555
  158.2 8.7 %collective-permute-start.29 = (bf16[96,768]{1,0:T(8,128)(2,1)S(1)}, bf16[96,768]{1,0:T(8,128)(2,1)S(1)}, u32[]{:S(2)}, u32[]{:S(2)}) collective-permute-start(bf16[96,768]{1,0:T(8,128)(2,1)S(1)} %get-tuple-element.164), channel_id=1, source_target_pairs={{0,24},{4,28},{8,16},{12,20},{16,8},{20,12},{24,0},{28,4},{1,25},{... | collective-permute-start | bytes 442376 | tf_op jit(solution)/shard_map/ppermute | solution.py:555
  161.9 10.7 %collective-permute-start.30 = (bf16[96,768]{1,0:T(8,128)(2,1)S(1)}, bf16[96,768]{1,0:T(8,128)(2,1)S(1)}, u32[]{:S(2)}, u32[]{:S(2)}) collective-permute-start(bf16[96,768]{1,0:T(8,128)(2,1)S(1)} %get-tuple-element.163), channel_id=1, source_target_pairs={{0,16},{4,20},{8,24},{12,28},{16,0},{20,4},{24,8},{28,12},{1,17},{... | collective-permute-start | bytes 442376 | tf_op jit(solution)/shard_map/ppermute | solution.py:555
  161.9 10.7 %collective-permute-start.32 = (bf16[96,768]{1,0:T(8,128)(2,1)S(1)}, bf16[96,768]{1,0:T(8,128)(2,1)S(1)}, u32[]{:S(2)}, u32[]{:S(2)}) collective-permute-start(bf16[96,768]{1,0:T(8,128)(2,1)S(1)} %get-tuple-element.162), channel_id=1, source_target_pairs={{0,8},{4,12},{8,0},{12,4},{16,24},{20,28},{24,16},{28,20},{1,9},{5... | collective-permute-start | bytes 442376 | tf_op jit(solution)/shard_map/ppermute | solution.py:555
  166.9 11.9 %copy-start.11 = (f32[16,1408]{1,0:T(8,128)S(1)}, f32[16,1408]{1,0:T(8,128)}, u32[]{:S(2)}) copy-start(f32[16,1408]{1,0:T(8,128)} %copy-done.10) | copy-start | bytes 270340
  173.4 0.8 copy-start.7
  174.2 8.5 %collective-permute-start.34 = (f32[96,384]{1,0:T(8,128)S(1)}, f32[96,384]{1,0:T(8,128)}, u32[]{:S(2)}, u32[]{:S(2)}) collective-permute-start(f32[96,384]{1,0:T(8,128)S(1)} %get-tuple-element.96), channel_id=1, source_target_pairs={{0,1},{1,0},{2,3},{3,2},{4,5},{5,4},{6,7},{7,6},{8,9},{9,8},{10,11... | collective-permute-start | bytes 442376 | tf_op jit(solution)/shard_map/ppermute | solution.py:555
  174.2 8.5 %collective-permute-start.35 = (f32[96,384]{1,0:T(8,128)S(1)}, f32[96,384]{1,0:T(8,128)}, u32[]{:S(2)}, u32[]{:S(2)}) collective-permute-start(f32[96,384]{1,0:T(8,128)S(1)} %get-tuple-element.96), channel_id=1, source_target_pairs={{0,2},{1,3},{2,0},{3,1},{4,6},{5,7},{6,4},{7,5},{8,10},{9,11},{10,... | collective-permute-start | bytes 442376 | tf_op jit(solution)/shard_map/ppermute | solution.py:555
  175.4 7.9 %collective-permute-start.36 = (f32[96,384]{1,0:T(8,128)S(1)}, f32[96,384]{1,0:T(8,128)}, u32[]{:S(2)}, u32[]{:S(2)}) collective-permute-start(f32[96,384]{1,0:T(8,128)S(1)} %get-tuple-element.96), channel_id=1, source_target_pairs={{0,3},{1,2},{2,1},{3,0},{4,7},{5,6},{6,5},{7,4},{8,11},{9,10},{10,... | collective-permute-start | bytes 442376 | tf_op jit(solution)/shard_map/ppermute | solution.py:555
  178.9 1.0 copy-start.6
  179.9 1.0 copy-start.8
  (4 other events, 2.6 us)

commit v4 on v3

--- a/solution.py
+++ b/solution.py
@@ -162,11 +162,13 @@
         state_ref[...] = jnp.zeros_like(state_ref)
         if parts:
             put = lambda k, value: place_rows(weight_ref, info_ref[4] ^ k, value)
-            own_ref, near_ref, far_ref, beside_ref = part_refs
+            own_ref, near_ref, far_ref, beside_ref, close_ref, last_ref = part_refs
+            put(2, close_ref[...])
+            put(3, last_ref[...])
             put(0, own_ref[...])
             put(1, near_ref[...])
             for at in range(far_ref.shape[0]):
-                k = 2 * (far_ref.shape[0] - at)
+                k = 2 * (far_ref.shape[0] - at) + 2
                 put(k, far_ref[at])
                 put(k + 1, beside_ref[at])
         rows_ref[...] = mm(weight_ref[:, conv_width:], choose_ref[...], TN)[0:16, :]
@@ -598,17 +600,19 @@
 def gather_direct(values, axis, others):
     size = lax.axis_size(axis)
     near = swap(values, axis, 1)
-    far = [swap(values, axis, k) for k in range(size - 2, 0, -2)]
-    far = after(jnp.stack(far), *others)
-    return values, near, far, swap(far, axis, 1)
-
-
-def assemble(own, near, far, beside, axis):
+    far = [swap(values, axis, k) for k in range(size - 2, 2, -2)]
+    close = swap(values, axis, 2)
+    last = swap(close, axis, 1)
+    far, last = lax.optimization_barrier((jnp.stack(far), last, *others))[:2]
+    return values, near, far, swap(far, axis, 1), close, last
+
+
+def assemble(own, near, far, beside, close, last, axis):
     size = lax.axis_size(axis)
     place = lax.axis_index(axis)
     result = jnp.zeros((size,) + own.shape, own.dtype)
-    pieces = {0: own, 1: near}
-    for at, k in enumerate(range(size - 2, 0, -2)):
+    pieces = {0: own, 1: near, 2: close, 3: last}
+    for at, k in enumerate(range(size - 2, 2, -2)):
         pieces.update({k: far[at], k + 1: beside[at]})
     for k in range(size):
         result = lax.dynamic_update_slice(
@@ -907,8 +911,8 @@
             fixed((width, LANES)),
         ],
         [
-            shaped((full_len, inner), bf16),
-            shaped((full_len, inner), bf16),
+            pltpu.HBM((full_len, inner), bf16),
+            pltpu.HBM((full_len, inner), bf16),
             shaped((width, 2 * inner), bf16),
             shaped((8, inner), f32),
             shaped((width, LANES), f32),

time: 187 us -> 184 us (0.984)
  local copies, waits for them, and re-layouts: 31 us -> 24.3 us
  starting transfers between devices: 35.7 us -> 39.2 us
    ppermute x37 -> x38, starting transfers between devices: 35.7 us -> 39.2 us  [swap(): return lax.ppermute(values, axis, [(i, i ^ bits) for i in range(size)])]
    unnamed x64 -> x56, local copies, waits for them, and re-layouts: 10.8 us -> 7.36 us
    ppermute x37 -> x38, waiting for transfers between devices: 26.6 us -> 28 us  [swap(): return lax.ppermute(values, axis, [(i, i ^ bits) for i in range(size)])]
  transfers between devices with their start and end apart: 37 -> 38, of which waited for: 10 -> 12; matrix products, arithmetic and copies ran while one was open for 18% -> 15% of each run, Pallas kernels for 35% -> 36%
where the time goes in v4:
time: 184 us
  Pallas kernels  73.9 us (40%)
  starting transfers between devices  39.2 us (21%)
  waiting for transfers between devices  28 us (15%)
  local copies, waits for them, and re-layouts  24.3 us (13%)
  other arithmetic  15 us (8%)
  between operations  3.23 us (2%)
    pallas_call x4, Pallas kernels, call(): pl.pallas_call(kernel, grid_spec=pltpu.PrefetchScalarGridSpec(num_scalar_...  71.3 us
    ppermute x38, starting transfers between devices, swap(): return lax.ppermute(values, axis, [(i, i ^ bits) for i in range(size)])  39.2 us
    ppermute x38, waiting for transfers between devices, swap(): return lax.ppermute(values, axis, [(i, i ^ bits) for i in range(size)])  28 us
    unnamed x56, local copies, waits for them, and re-layouts  7.36 us
    slice x3, local copies, waits for them, and re-layouts, per_device(): cut = lambda values, k: values[k * piece_len:(k + 1) * piece_len]  4.28 us
  transfers between devices with their start and end apart: 38, of which 12 were waited for; matrix products, arithmetic and copies ran while one was open for 15% of the time, Pallas kernels for 36%

profile of v4, /device:TPU:0, one launch (start us, length us, event | category | flops | bytes accessed | tf_op | source)
XLA Modules:
  0.0 183.6 jit_solution(3948322700281055380)
XLA Ops:
  1.2 2.6 %collective-permute-start = (bf16[512,768]{1,0:T(8,128)(2,1)}, bf16[512,768]{1,0:T(8,128)(2,1)}, u32[]{:S(2)}, u32[]{:S(2)}) collective-permute-start(bf16[512,768]{1,0:T(8,128)(2,1)} %bitcast.88), channel_id=1, source_target_pairs={{0,2},{1,3},{2,0},{3,1},{4,6},{5,7},{6,4},{7,5},{8,10},{9,11},{10,... | collective-permute-start | bytes 2359304 | tf_op jit(solution)/shard_map/ppermute | solution.py:557
  3.7 0.9 slice_bitcast_fusion
  4.7 0.8 copy.45
  5.5 0.8 reshape.144
  6.2 0.8 reshape.143
  7.0 0.8 copy.46
  7.9 0.9 concatenate.10.refs_4_
  8.8 2.7 %collective-permute-start.7 = (bf16[96,768]{1,0:T(8,128)(2,1)S(1)}, bf16[96,768]{1,0:T(8,128)(2,1)}, u32[]{:S(2)}, u32[]{:S(2)}) collective-permute-start(bf16[96,768]{1,0:T(8,128)(2,1)S(1)} %concatenate.10.refs_4_), channel_id=1, source_target_pairs={{0,16},{4,20},{8,24},{12,28},{16,0},{20,4},{24,8},{28,12},{1,17},{... | collective-permute-start | bytes 442376 | tf_op jit(solution)/shard_map/ppermute | solution.py:557
  11.4 1.3 collective-permute-start.6
  13.7 0.8 fusion.8.refs_16_
  14.4 1.6 pad_maximum_fusion.5
  16.7 0.7 broadcast_in_dim.38
  17.6 1.5 fusion.refs_10_.refs_18_
  19.1 3.0 %collective-permute-done.refs_2_ = bf16[512,768]{1,0:T(8,128)(2,1)} collective-permute-done((bf16[512,768]{1,0:T(8,128)(2,1)}, bf16[512,768]{1,0:T(8,128)(2,1)}, u32[]{:S(2)}, u32[]{:S(2)}) %collective-permute-start) | collective-permute-done | bytes 786464 | tf_op jit(solution)/shard_map/ppermute | solution.py:557
  22.9 1.7 collective-permute-start.10
  27.0 0.7 stack.85.info_ref
  27.8 1.8 collective-permute-start.5
  29.5 1.0 pad_maximum_fusion.1.refs_6_
  30.6 2.5 %collective-permute-done.9.refs_9_ = bf16[96,768]{1,0:T(8,128)(2,1)} collective-permute-done((bf16[96,768]{1,0:T(8,128)(2,1)S(1)}, bf16[96,768]{1,0:T(8,128)(2,1)}, u32[]{:S(2)}, u32[]{:S(2)}) %collective-permute-start.9) | collective-permute-done | bytes 147488 | tf_op jit(solution)/shard_map/ppermute | solution.py:557
  33.0 1.7 collective-permute-start.11
  34.7 1.0 select_bitcast_fusion.1
  35.7 1.6 collective-permute-start.13
  37.4 2.6 %collective-permute-start.14 = (bf16[2,96,768]{2,1,0:T(8,128)(2,1)S(1)}, bf16[2,96,768]{2,1,0:T(8,128)(2,1)S(1)}, u32[]{:S(2)}, u32[]{:S(2)}) collective-permute-start(bf16[2,96,768]{2,1,0:T(8,128)(2,1)S(1)} %pad_maximum_fusion.2), channel_id=1, source_target_pairs={{0,16},{4,20},{8,24},{12,28},{16,0},{20,4},{24,8},{28,12},{1,17},{... | collective-permute-start | bytes 884744 | tf_op jit(solution)/shard_map/ppermute | solution.py:557
  40.2 1.8 collective-permute-done.11.refs_7_
  42.0 1.8 collective-permute-start.2
  43.8 18.9 %forward.1 = (bf16[2048,768]{1,0:T(8,128)(2,1)S(1)}, bf16[2048,640]{1,0:T(8,128)(2,1)}, f32[2048,128]{1,0:T(8,128)}, f32[2048,384]{1,0:T(8,128)S(1)}, f32[2048,1...) custom-call(s32[5]{0:T(128)S(1)} %stack.85.info_ref, ...), custom_call_target="tpu_custom_call" | custom-call | flops 22000001024 | bytes 66000000 | tf_op jit(solution)/shard_map/forward/pallas_call | solution.py:782
  62.7 1.1 copy-done.19
  64.4 1.7 collective-permute-done.12.refs_3_
  66.1 7.8 %branch.1 = (f32[2048,384]{1,0:T(8,128)S(1)}, bf16[2048,768]{1,0:T(8,128)(2,1)S(1)}, f32[8,2048]{1,0:T(8,128)S(1)}) custom-call(s32[5]{0:T(128)S(1)} %stack.85.info_ref, bf16[512,768]{1,0:T(8,128)(2,1)S(1)} %bitcast.98, bf16[512,768]{1,0:T(8,128)(2,1)S(1)} %collective-permute-done.1.refs_1_, bf16[512,768]{1,0:T(8,128)(2,1)S(1)} %collective-permute-done.2.refs_2_, ...), custom_call_target="tpu_custom_call" | custom-call | flops 11000000512 | bytes 33000000 | tf_op jit(solution)/shard_map/branch/pallas_call | solution.py:782
  74.4 1.1 collective-permute-start.18
  76.1 1.2 fusion.19
  77.9 1.0 collective-permute-done.17
  78.9 8.9 %gate_back.1 = (bf16[2048,384]{1,0:T(8,128)(2,1)}, bf16[2048,384]{1,0:T(8,128)(2,1)}, bf16[768,768]{1,0:T(8,128)(2,1)S(1)}, f32[8,384]{1,0:T(8,128)S(1)}, f32[768,128]{1,0:T(8,128)S(1)}) custom-call(s32[5]{0:T(128)S(1)} %stack.85.info_ref, bf16[512,768]{1,0:T(8,128)(2,1)S(1)} %bitcast.99, bf16[512,768]{1,0:T(8,128)(2,1)S(1)} %collective-permute-done.1.refs_1_, ...), custom_call_target="tpu_custom_call" | custom-call | flops 12999999488 | bytes 39000000 | tf_op jit(solution)/shard_map/gate_back/pallas_call | solution.py:782
  87.8 0.8 copy-done.18
  89.0 1.8 collective-permute-start.22
  90.7 0.9 pad.24.refs_19_
  91.7 1.6 add_convert_fusion.2
  93.2 1.3 collective-permute-start.21
  94.6 35.6 %backward.1 = (bf16[2048,768]{1,0:T(8,128)(2,1)}, bf16[768,768]{1,0:T(8,128)(2,1)}) custom-call(s32[5]{0:T(128)} %copy-done.15, bf16[2048,768]{1,0:T(8,128)(2,1)} %copy-done.16, bf16[768,768]{1,0:T(8,128)(2,1)} %copy-done.19, bf16[768,768]{1,0:T(8,128)(2,1)} %bitcast.95, bf16[2048,640]{1,0:T(8,128)(2,1)} %get-tuple-element.67.refs_3_.refs_4_, ...), custom_call_target="tpu_custom_call" | custom-call | flops 35999997952 | bytes 108000000 | tf_op jit(solution)/shard_map/backward/pallas_call | solution.py:782
  130.3 0.8 copy-done.22
  131.1 2.1 %slice.143 = bf16[512,768]{1,0:T(8,128)(2,1)} slice(bf16[2048,768]{1,0:T(8,128)(2,1)} %get-tuple-element.90), slice={[1536:2048], [0:768]} | slice | bytes 1572864 | tf_op jit(solution)/shard_map/slice | solution.py:885
  134.3 3.7 %collective-permute-start.27 = (bf16[96,768]{1,0:T(8,128)(2,1)S(1)}, bf16[96,768]{1,0:T(8,128)(2,1)S(1)}, u32[]{:S(2)}, u32[]{:S(2)}) collective-permute-start(bf16[96,768]{1,0:T(8,128)(2,1)S(1)} %get-tuple-element.162), channel_id=1, source_target_pairs={{0,24},{4,28},{8,16},{12,20},{16,8},{20,12},{24,0},{28,4},{1,25},{... | collective-permute-start | bytes 442376 | tf_op jit(solution)/shard_map/ppermute | solution.py:557
  138.0 0.8 collective-permute-start.29
  138.9 1.2 collective-permute-start.32
  140.1 1.3 add_convert_fusion.1
  141.5 1.6 collective-permute-done.23
  143.1 0.8 collective-permute-start.26
  144.0 1.0 fusion.18
  145.0 4.1 %collective-permute-done.32 = bf16[2,96,768]{2,1,0:T(8,128)(2,1)S(1)} collective-permute-done((bf16[2,96,768]{2,1,0:T(8,128)(2,1)S(1)}, bf16[2,96,768]{2,1,0:T(8,128)(2,1)S(1)}, u32[]{:S(2)}, u32[]{:S(2)}) %collective-permute-start.32) | collective-permute-done | bytes 294944 | tf_op jit(solution)/shard_map/ppermute | solution.py:557
  149.1 4.4 %collective-permute-done.26.far_ref = bf16[256,768]{1,0:T(8,128)(2,1)S(1)} collective-permute-done((bf16[256,768]{1,0:T(8,128)(2,1)S(1)}, bf16[256,768]{1,0:T(8,128)(2,1)S(1)}, u32[]{:S(2)}, u32[]{:S(2)}) %collective-permute-start.26) | collective-permute-done | bytes 393248 | tf_op jit(solution)/shard_map/ppermute | solution.py:557
  153.5 0.8 collective-permute-start.34
  154.2 1.1 convert_add_fusion
  155.3 3.7 %collective-permute-start.30 = (bf16[96,768]{1,0:T(8,128)(2,1)S(1)}, bf16[96,768]{1,0:T(8,128)(2,1)S(1)}, u32[]{:S(2)}, u32[]{:S(2)}) collective-permute-start(bf16[96,768]{1,0:T(8,128)(2,1)S(1)} %get-tuple-element.166), channel_id=1, source_target_pairs={{0,24},{4,28},{8,16},{12,20},{16,8},{20,12},{24,0},{28,4},{1,25},{... | collective-permute-start | bytes 442376 | tf_op jit(solution)/shard_map/ppermute | solution.py:557
  159.0 0.8 collective-permute-start.33
  159.8 2.9 %fusion.1 = bf16[512,1,768]{2,0,1:T(8,128)(2,1)} fusion(bf16[512,768]{1,0:T(8,128)(2,1)} %collective-permute-done.21, bf16[512,768]{1,0:T(8,128)(2,1)} %collective-permute-done.20, f32[512]{0:T(512)S(1)} %bitcast.105, bf16[2048,768]{1,0:T(8,128)(2,1)} %copy-done.1, bf16[512,1,768]{2,0,1:T(8,128)(2,1)S(1)} %copy-done), kind=kLoop, calls=%fused_computation.5 | loop fusion | flops 3538944 | bytes 3934208 | tf_op jit(solution)/shard_map/broadcast_in_dim | solution.py:1063
  162.7 1.2 collective-permute-done.30.refs_4_
  164.0 5.8 %collective-permute-done.31.refs_5_ = bf16[96,768]{1,0:T(8,128)(2,1)S(1)} collective-permute-done((bf16[96,768]{1,0:T(8,128)(2,1)S(1)}, bf16[96,768]{1,0:T(8,128)(2,1)S(1)}, u32[]{:S(2)}, u32[]{:S(2)}) %collective-permute-start.31) | collective-permute-done | bytes 147488 | tf_op jit(solution)/shard_map/ppermute | solution.py:557
  169.8 0.8 weight_sums.1
  170.6 0.8 copy-done.8
  171.3 1.3 collective-permute-start.36
  176.1 1.0 copy-done.7
  177.1 1.0 copy-done.9
  178.0 1.8 hidden_back.1
  180.5 1.1 add_add_fusion
  (139 shorter events, 13.8 us)
Async XLA Ops:
  0.6 39.3 %collective-permute-start.3 = (bf16[512,768]{1,0:T(8,128)(2,1)}, bf16[512,768]{1,0:T(8,128)(2,1)}, u32[]{:S(2)}, u32[]{:S(2)}) collective-permute-start(bf16[512,768]{1,0:T(8,128)(2,1)} %bitcast.87), channel_id=1, source_target_pairs={{0,1},{1,0},{2,3},{3,2},{4,5},{5,4},{6,7},{7,6},{8,9},{9,8},{10,11... | collective-permute-start | bytes 2359304 | tf_op jit(solution)/shard_map/ppermute | solution.py:557
  1.2 21.0 %collective-permute-start = (bf16[512,768]{1,0:T(8,128)(2,1)}, bf16[512,768]{1,0:T(8,128)(2,1)}, u32[]{:S(2)}, u32[]{:S(2)}) collective-permute-start(bf16[512,768]{1,0:T(8,128)(2,1)} %bitcast.88), channel_id=1, source_target_pairs={{0,2},{1,3},{2,0},{3,1},{4,6},{5,7},{6,4},{7,5},{8,10},{9,11},{10,... | collective-permute-start | bytes 2359304 | tf_op jit(solution)/shard_map/ppermute | solution.py:557
  7.8 14.4 %copy-start.25 = (s32[1,4]{1,0:T(1,128)S(1)}, s32[1,4]{1,0:T(1,128)}, u32[]{:S(2)}) copy-start(s32[1,4]{1,0:T(1,128)} %param.17) | copy-start | bytes 52
  7.8 17.1 %copy-start.26 = (f32[6]{0:T(128)S(1)}, f32[6]{0:T(128)}, u32[]{:S(2)}) copy-start(f32[6]{0:T(128)} %param.25) | copy-start | bytes 76
  8.8 14.1 %collective-permute-start.7 = (bf16[96,768]{1,0:T(8,128)(2,1)S(1)}, bf16[96,768]{1,0:T(8,128)(2,1)}, u32[]{:S(2)}, u32[]{:S(2)}) collective-permute-start(bf16[96,768]{1,0:T(8,128)(2,1)S(1)} %concatenate.10.refs_4_), channel_id=1, source_target_pairs={{0,16},{4,20},{8,24},{12,28},{16,0},{20,4},{24,8},{28,12},{1,17},{... | collective-permute-start | bytes 442376 | tf_op jit(solution)/shard_map/ppermute | solution.py:557
  11.4 16.4 %collective-permute-start.6 = (bf16[96,768]{1,0:T(8,128)(2,1)S(1)}, bf16[96,768]{1,0:T(8,128)(2,1)}, u32[]{:S(2)}, u32[]{:S(2)}) collective-permute-start(bf16[96,768]{1,0:T(8,128)(2,1)S(1)} %concatenate.10.refs_4_), channel_id=1, source_target_pairs={{0,24},{4,28},{8,16},{12,20},{16,8},{20,12},{24,0},{28,4},{1,25},{... | collective-permute-start | bytes 442376 | tf_op jit(solution)/shard_map/ppermute | solution.py:557
  12.8 11.8 %collective-permute-start.8 = (bf16[96,768]{1,0:T(8,128)(2,1)S(1)}, bf16[96,768]{1,0:T(8,128)(2,1)S(1)}, u32[]{:S(2)}, u32[]{:S(2)}) collective-permute-start(bf16[96,768]{1,0:T(8,128)(2,1)S(1)} %concatenate.10.refs_4_), channel_id=1, source_target_pairs={{0,8},{4,12},{8,0},{12,4},{16,24},{20,28},{24,16},{28,20},{1,9},{5... | collective-permute-start | bytes 442376 | tf_op jit(solution)/shard_map/ppermute | solution.py:557
  16.0 18.7 %copy-start.24 = (bf16[384,96]{0,1:T(8,128)(2,1)S(1)}, bf16[384,96]{0,1:T(8,128)(2,1)}, u32[]{:S(2)}) copy-start(bf16[384,96]{0,1:T(8,128)(2,1)} %param.23) | copy-start | bytes 221188
  17.6 26.2 %copy-start.10 = (bf16[128,384]{1,0:T(8,128)(2,1)}, bf16[128,384]{1,0:T(8,128)(2,1)S(1)}, u32[]{:S(2)}) copy-start(bf16[128,384]{1,0:T(8,128)(2,1)S(1)} %compare_convert_fusion.refs_13_.refs_15_) | copy-start | bytes 294916
  17.6 26.1 %copy-start = (bf16[512,1,768]{2,0,1:T(8,128)(2,1)S(1)}, bf16[512,1,768]{2,0,1:T(8,128)(2,1)}, u32[]{:S(2)}) copy-start(bf16[512,1,768]{2,0,1:T(8,128)(2,1)} %param.15) | copy-start | bytes 2359300
  19.1 43.6 %copy-start.2 = (bf16[768,1408]{1,0:T(8,128)(2,1)}, bf16[768,1408]{1,0:T(8,128)(2,1)S(1)}, u32[]{:S(2)}) copy-start(bf16[768,1408]{1,0:T(8,128)(2,1)S(1)} %fusion.refs_10_.refs_18_) | copy-start | bytes 6488068
  22.2 19.8 %collective-permute-start.4 = (bf16[512,768]{1,0:T(8,128)(2,1)}, bf16[512,768]{1,0:T(8,128)(2,1)}, u32[]{:S(2)}, u32[]{:S(2)}) collective-permute-start(bf16[512,768]{1,0:T(8,128)(2,1)} %collective-permute-done.refs_2_), channel_id=1, source_target_pairs={{0,1},{1,0},{2,3},{3,2},{4,5},{5,4},{6,7},{7,6},{8,9},{9,8},{10,11... | collective-permute-start | bytes 2359304 | tf_op jit(solution)/shard_map/ppermute | solution.py:557
  22.2 56.7 %copy-start.13 = (f32[8,384]{1,0:T(8,128)}, f32[8,384]{1,0:T(8,128)S(1)}, u32[]{:S(2)}) copy-start(f32[8,384]{1,0:T(8,128)S(1)} %select_maximum_fusion.refs_11_.refs_8_.refs_10_.refs_13_) | copy-start | bytes 36868
  22.9 7.7 %collective-permute-start.10 = (bf16[96,768]{1,0:T(8,128)(2,1)}, bf16[96,768]{1,0:T(8,128)(2,1)}, u32[]{:S(2)}, u32[]{:S(2)}) collective-permute-start(bf16[96,768]{1,0:T(8,128)(2,1)} %pad_maximum_fusion.5), channel_id=1, source_target_pairs={{0,4},{4,0},{8,12},{12,8},{16,20},{20,16},{24,28},{28,24},{1,5},{5... | collective-permute-start | bytes 442376 | tf_op jit(solution)/shard_map/ppermute | solution.py:557
  24.6 8.4 %collective-permute-start.9 = (bf16[96,768]{1,0:T(8,128)(2,1)S(1)}, bf16[96,768]{1,0:T(8,128)(2,1)}, u32[]{:S(2)}, u32[]{:S(2)}) collective-permute-start(bf16[96,768]{1,0:T(8,128)(2,1)S(1)} %collective-permute-done.8.refs_8_), channel_id=1, source_target_pairs={{0,4},{4,0},{8,12},{12,8},{16,20},{20,16},{24,28},{28,24},{1,5},{5... | collective-permute-start | bytes 442376 | tf_op jit(solution)/shard_map/ppermute | solution.py:557
  24.9 37.8 %copy-start.14 = (f32[8,128]{1,0:T(8,128)}, f32[8,128]{1,0:T(8,128)S(1)}, u32[]{:S(2)}) copy-start(f32[8,128]{1,0:T(8,128)S(1)} %select_maximum_fusion.1.refs_12_.refs_14_) | copy-start | bytes 12292
  27.8 51.1 %copy-start.15 = (s32[5]{0:T(128)}, s32[5]{0:T(128)S(1)}, u32[]{:S(2)}) copy-start(s32[5]{0:T(128)S(1)} %stack.85.info_ref) | copy-start | bytes 64
  27.8 14.2 %copy-start.4 = (bf16[512,1,768]{2,0,1:T(8,128)(2,1)S(1)}, bf16[512,1,768]{2,0,1:T(8,128)(2,1)}, u32[]{:S(2)}) copy-start(bf16[512,1,768]{2,0,1:T(8,128)(2,1)} %param.16) | copy-start | bytes 2359300
  27.8 9.6 %collective-permute-start.5 = (bf16[96,768]{1,0:T(8,128)(2,1)S(1)}, bf16[96,768]{1,0:T(8,128)(2,1)S(1)}, u32[]{:S(2)}, u32[]{:S(2)}) collective-permute-start(bf16[96,768]{1,0:T(8,128)(2,1)S(1)} %concatenate.10.refs_4_), channel_id=1, source_target_pairs={{0,4},{4,0},{8,12},{12,8},{16,20},{20,16},{24,28},{28,24},{1,5},{5... | collective-permute-start | bytes 442376 | tf_op jit(solution)/shard_map/ppermute | solution.py:557
  33.0 8.9 %collective-permute-start.11 = (bf16[2,96,768]{2,1,0:T(8,128)(2,1)S(1)}, bf16[2,96,768]{2,1,0:T(8,128)(2,1)S(1)}, u32[]{:S(2)}, u32[]{:S(2)}) collective-permute-start(bf16[2,96,768]{2,1,0:T(8,128)(2,1)S(1)} %pad_maximum_fusion.1.refs_6_), channel_id=1, source_target_pairs={{0,4},{4,0},{8,12},{12,8},{16,20},{20,16},{24,28},{28,24},{1,5},{5... | collective-permute-start | bytes 884744 | tf_op jit(solution)/shard_map/ppermute | solution.py:557
  35.7 28.4 %collective-permute-start.13 = (bf16[2,96,768]{2,1,0:T(8,128)(2,1)S(1)}, bf16[2,96,768]{2,1,0:T(8,128)(2,1)S(1)}, u32[]{:S(2)}, u32[]{:S(2)}) collective-permute-start(bf16[2,96,768]{2,1,0:T(8,128)(2,1)S(1)} %pad_maximum_fusion.2), channel_id=1, source_target_pairs={{0,8},{4,12},{8,0},{12,4},{16,24},{20,28},{24,16},{28,20},{1,9},{5... | collective-permute-start | bytes 884744 | tf_op jit(solution)/shard_map/ppermute | solution.py:557
  37.4 26.8 %collective-permute-start.14 = (bf16[2,96,768]{2,1,0:T(8,128)(2,1)S(1)}, bf16[2,96,768]{2,1,0:T(8,128)(2,1)S(1)}, u32[]{:S(2)}, u32[]{:S(2)}) collective-permute-start(bf16[2,96,768]{2,1,0:T(8,128)(2,1)S(1)} %pad_maximum_fusion.2), channel_id=1, source_target_pairs={{0,16},{4,20},{8,24},{12,28},{16,0},{20,4},{24,8},{28,12},{1,17},{... | collective-permute-start | bytes 884744 | tf_op jit(solution)/shard_map/ppermute | solution.py:557
  40.0 24.3 %collective-permute-start.15 = (bf16[2,96,768]{2,1,0:T(8,128)(2,1)S(1)}, bf16[2,96,768]{2,1,0:T(8,128)(2,1)S(1)}, u32[]{:S(2)}, u32[]{:S(2)}) collective-permute-start(bf16[2,96,768]{2,1,0:T(8,128)(2,1)S(1)} %pad_maximum_fusion.2), channel_id=1, source_target_pairs={{0,24},{4,28},{8,16},{12,20},{16,8},{20,12},{24,0},{28,4},{1,25},{... | collective-permute-start | bytes 884744 | tf_op jit(solution)/shard_map/ppermute | solution.py:557
  42.0 22.5 %collective-permute-start.1 = (bf16[512,768]{1,0:T(8,128)(2,1)S(1)}, bf16[512,768]{1,0:T(8,128)(2,1)S(1)}, u32[]{:S(2)}, u32[]{:S(2)}) collective-permute-start(bf16[512,768]{1,0:T(8,128)(2,1)S(1)} %bitcast.96), channel_id=1, source_target_pairs={{0,1},{1,0},{2,3},{3,2},{4,5},{5,4},{6,7},{7,6},{8,9},{9,8},{10,11... | collective-permute-start | bytes 2359304 | tf_op jit(solution)/shard_map/ppermute | solution.py:557
  42.0 21.8 %collective-permute-start.2 = (bf16[512,768]{1,0:T(8,128)(2,1)S(1)}, bf16[512,768]{1,0:T(8,128)(2,1)S(1)}, u32[]{:S(2)}, u32[]{:S(2)}) collective-permute-start(bf16[512,768]{1,0:T(8,128)(2,1)S(1)} %bitcast.97), channel_id=1, source_target_pairs={{0,2},{1,3},{2,0},{3,1},{4,6},{5,7},{6,4},{7,5},{8,10},{9,11},{10,... | collective-permute-start | bytes 2359304 | tf_op jit(solution)/shard_map/ppermute | solution.py:557
  62.7 1.1 copy-start.19
  63.8 15.1 %copy-start.16 = (bf16[2048,768]{1,0:T(8,128)(2,1)}, bf16[2048,768]{1,0:T(8,128)(2,1)S(1)}, u32[]{:S(2)}) copy-start(bf16[2048,768]{1,0:T(8,128)(2,1)S(1)} %get-tuple-element.63.refs_4_.refs_5_.refs_0_) | copy-start | bytes 9437188
  63.8 15.1 %copy-start.17 = (f32[2048,384]{1,0:T(8,128)}, f32[2048,384]{1,0:T(8,128)S(1)}, u32[]{:S(2)}) copy-start(f32[2048,384]{1,0:T(8,128)S(1)} %get-tuple-element.64.refs_5_.refs_9_.refs_7_) | copy-start | bytes 9437188
  63.8 2.4 %collective-permute-start.12 = (bf16[512,768]{1,0:T(8,128)(2,1)S(1)}, bf16[512,768]{1,0:T(8,128)(2,1)S(1)}, u32[]{:S(2)}, u32[]{:S(2)}) collective-permute-start(bf16[512,768]{1,0:T(8,128)(2,1)S(1)} %collective-permute-done.2.refs_2_), channel_id=1, source_target_pairs={{0,1},{1,0},{2,3},{3,2},{4,5},{5,4},{6,7},{7,6},{8,9},{9,8},{10,11... | collective-permute-start | bytes 2359304 | tf_op jit(solution)/shard_map/ppermute | solution.py:557
  64.4 14.5 %copy-start.3 = (bf16[4,2,96,768]{3,2,1,0:T(8,128)(2,1)}, bf16[4,2,96,768]{3,2,1,0:T(8,128)(2,1)S(1)}, u32[]{:S(2)}) copy-start(bf16[4,2,96,768]{3,2,1,0:T(8,128)(2,1)S(1)} %bitcast_dynamic-update-slice_fusion) | copy-start | bytes 3538948
  73.9 3.5 %copy-start.1 = (bf16[2048,768]{1,0:T(8,128)(2,1)}, bf16[2048,768]{1,0:T(8,128)(2,1)S(1)}, u32[]{:S(2)}) copy-start(bf16[2048,768]{1,0:T(8,128)(2,1)S(1)} %get-tuple-element.65) | copy-start | bytes 9437188
  73.9 4.9 %collective-permute-start.17 = (f32[8,2048]{1,0:T(8,128)S(1)}, f32[8,2048]{1,0:T(8,128)S(1)}, u32[]{:S(2)}, u32[]{:S(2)}) collective-permute-start(f32[8,2048]{1,0:T(8,128)S(1)} %get-tuple-element.70), channel_id=1, source_target_pairs={{0,2},{1,3},{2,0},{3,1},{4,6},{5,7},{6,4},{7,5},{8,10},{9,11},{10,... | collective-permute-start | bytes 196616 | tf_op jit(solution)/shard_map/ppermute | solution.py:557
  74.4 4.4 %collective-permute-start.18 = (f32[8,2048]{1,0:T(8,128)S(1)}, f32[8,2048]{1,0:T(8,128)S(1)}, u32[]{:S(2)}, u32[]{:S(2)}) collective-permute-start(f32[8,2048]{1,0:T(8,128)S(1)} %get-tuple-element.70), channel_id=1, source_target_pairs={{0,3},{1,2},{2,1},{3,0},{4,7},{5,6},{6,5},{7,4},{8,11},{9,10},{10,... | collective-permute-start | bytes 196616 | tf_op jit(solution)/shard_map/ppermute | solution.py:557
  75.5 3.4 %collective-permute-start.16 = (f32[8,2048]{1,0:T(8,128)S(1)}, f32[8,2048]{1,0:T(8,128)S(1)}, u32[]{:S(2)}, u32[]{:S(2)}) collective-permute-start(f32[8,2048]{1,0:T(8,128)S(1)} %get-tuple-element.70), channel_id=1, source_target_pairs={{0,1},{1,0},{2,3},{3,2},{4,5},{5,4},{6,7},{7,6},{8,9},{9,8},{10,11... | collective-permute-start | bytes 196616 | tf_op jit(solution)/shard_map/ppermute | solution.py:557
  77.4 14.3 %collective-permute-start.19 = (bf16[512,768]{1,0:T(8,128)(2,1)}, bf16[512,768]{1,0:T(8,128)(2,1)}, u32[]{:S(2)}, u32[]{:S(2)}) collective-permute-start(bf16[512,768]{1,0:T(8,128)(2,1)} %get-tuple-element.158), channel_id=1, source_target_pairs={{0,1},{1,0},{2,3},{3,2},{4,5},{5,4},{6,7},{7,6},{8,9},{9,8},{10,11... | collective-permute-start | bytes 2359304 | tf_op jit(solution)/shard_map/ppermute | solution.py:557
  77.4 52.9 %collective-permute-start.20 = (bf16[512,768]{1,0:T(8,128)(2,1)}, bf16[512,768]{1,0:T(8,128)(2,1)}, u32[]{:S(2)}, u32[]{:S(2)}) collective-permute-start(bf16[512,768]{1,0:T(8,128)(2,1)} %get-tuple-element.157), channel_id=1, source_target_pairs={{0,1},{1,0},{2,3},{3,2},{4,5},{5,4},{6,7},{7,6},{8,9},{9,8},{10,11... | collective-permute-start | bytes 2359304 | tf_op jit(solution)/shard_map/ppermute | solution.py:557
  87.8 0.8 copy-start.18
  89.0 41.3 %collective-permute-start.22 = (bf16[4,96,768]{2,1,0:T(8,128)(2,1)S(1)}, bf16[4,96,768]{2,1,0:T(8,128)(2,1)S(1)}, u32[]{:S(2)}, u32[]{:S(2)}) collective-permute-start(bf16[4,96,768]{2,1,0:T(8,128)(2,1)S(1)} %pad_maximum_fusion), channel_id=1, source_target_pairs={{0,4},{4,0},{8,12},{12,8},{16,20},{20,16},{24,28},{28,24},{1,5},{5... | collective-permute-start | bytes 1769480 | tf_op jit(solution)/shard_map/ppermute | solution.py:557
  93.2 37.0 %collective-permute-start.21 = (bf16[512,768]{1,0:T(8,128)(2,1)S(1)}, bf16[512,768]{1,0:T(8,128)(2,1)}, u32[]{:S(2)}, u32[]{:S(2)}) collective-permute-start(bf16[512,768]{1,0:T(8,128)(2,1)S(1)} %add_convert_fusion.2), channel_id=1, source_target_pairs={{0,2},{1,3},{2,0},{3,1},{4,6},{5,7},{6,4},{7,5},{8,10},{9,11},{10,... | collective-permute-start | bytes 2359304 | tf_op jit(solution)/shard_map/ppermute | solution.py:557
  130.2 2.9 %copy-start.21 = (bf16[768,768]{1,0:T(8,128)(2,1)S(1)}, bf16[768,768]{1,0:T(8,128)(2,1)}, u32[]{:S(2)}) copy-start(bf16[768,768]{1,0:T(8,128)(2,1)} %get-tuple-element.85) | copy-start | bytes 3538948
  130.2 0.8 copy-start.22
  133.1 5.7 %collective-permute-start.24 = (bf16[512,768]{1,0:T(8,128)(2,1)}, bf16[512,768]{1,0:T(8,128)(2,1)}, u32[]{:S(2)}, u32[]{:S(2)}) collective-permute-start(bf16[512,768]{1,0:T(8,128)(2,1)} %slice.143), channel_id=1, source_target_pairs={{0,1},{1,0},{2,3},{3,2},{4,5},{5,4},{6,7},{7,6},{8,9},{9,8},{10,11... | collective-permute-start | bytes 2359304 | tf_op jit(solution)/shard_map/ppermute | solution.py:557
  133.1 1.1 copy-start.23
  133.2 6.9 %copy-start.20 = (bf16[2048,768]{1,0:T(8,128)(2,1)S(1)}, bf16[2048,768]{1,0:T(8,128)(2,1)}, u32[]{:S(2)}) copy-start(bf16[2048,768]{1,0:T(8,128)(2,1)} %get-tuple-element.90) | copy-start | bytes 9437188
  133.3 9.9 %collective-permute-start.23 = (bf16[2,96,768]{2,1,0:T(8,128)(2,1)S(1)}, bf16[2,96,768]{2,1,0:T(8,128)(2,1)S(1)}, u32[]{:S(2)}, u32[]{:S(2)}) collective-permute-start(bf16[2,96,768]{2,1,0:T(8,128)(2,1)S(1)} %pad_maximum_fusion.3), channel_id=1, source_target_pairs={{0,4},{4,0},{8,12},{12,8},{16,20},{20,16},{24,28},{28,24},{1,5},{5... | collective-permute-start | bytes 884744 | tf_op jit(solution)/shard_map/ppermute | solution.py:557
  134.3 21.0 %collective-permute-start.27 = (bf16[96,768]{1,0:T(8,128)(2,1)S(1)}, bf16[96,768]{1,0:T(8,128)(2,1)S(1)}, u32[]{:S(2)}, u32[]{:S(2)}) collective-permute-start(bf16[96,768]{1,0:T(8,128)(2,1)S(1)} %get-tuple-element.162), channel_id=1, source_target_pairs={{0,24},{4,28},{8,16},{12,20},{16,8},{20,12},{24,0},{28,4},{1,25},{... | collective-permute-start | bytes 442376 | tf_op jit(solution)/shard_map/ppermute | solution.py:557
  138.0 21.0 %collective-permute-start.28 = (bf16[96,768]{1,0:T(8,128)(2,1)S(1)}, bf16[96,768]{1,0:T(8,128)(2,1)S(1)}, u32[]{:S(2)}, u32[]{:S(2)}) collective-permute-start(bf16[96,768]{1,0:T(8,128)(2,1)S(1)} %get-tuple-element.161), channel_id=1, source_target_pairs={{0,16},{4,20},{8,24},{12,28},{16,0},{20,4},{24,8},{28,12},{1,17},{... | collective-permute-start | bytes 442376 | tf_op jit(solution)/shard_map/ppermute | solution.py:557
  138.0 21.0 %collective-permute-start.29 = (bf16[96,768]{1,0:T(8,128)(2,1)S(1)}, bf16[96,768]{1,0:T(8,128)(2,1)S(1)}, u32[]{:S(2)}, u32[]{:S(2)}) collective-permute-start(bf16[96,768]{1,0:T(8,128)(2,1)S(1)} %get-tuple-element.160), channel_id=1, source_target_pairs={{0,8},{4,12},{8,0},{12,4},{16,24},{20,28},{24,16},{28,20},{1,9},{5... | collective-permute-start | bytes 442376 | tf_op jit(solution)/shard_map/ppermute | solution.py:557
  138.9 10.2 %collective-permute-start.32 = (bf16[2,96,768]{2,1,0:T(8,128)(2,1)S(1)}, bf16[2,96,768]{2,1,0:T(8,128)(2,1)S(1)}, u32[]{:S(2)}, u32[]{:S(2)}) collective-permute-start(bf16[2,96,768]{2,1,0:T(8,128)(2,1)S(1)} %pad_maximum_fusion.4), channel_id=1, source_target_pairs={{0,4},{4,0},{8,12},{12,8},{16,20},{20,16},{24,28},{28,24},{1,5},{5... | collective-permute-start | bytes 884744 | tf_op jit(solution)/shard_map/ppermute | solution.py:557
  143.1 10.4 %collective-permute-start.26 = (bf16[256,768]{1,0:T(8,128)(2,1)S(1)}, bf16[256,768]{1,0:T(8,128)(2,1)S(1)}, u32[]{:S(2)}, u32[]{:S(2)}) collective-permute-start(bf16[256,768]{1,0:T(8,128)(2,1)S(1)} %get-tuple-element.176), channel_id=1, source_target_pairs={{0,2},{1,3},{2,0},{3,1},{4,6},{5,7},{6,4},{7,5},{8,10},{9,11},{10,... | collective-permute-start | bytes 1179656 | tf_op jit(solution)/shard_map/ppermute | solution.py:557
  149.1 27.0 %collective-permute-start.25 = (bf16[512,768]{1,0:T(8,128)(2,1)}, bf16[512,768]{1,0:T(8,128)(2,1)S(1)}, u32[]{:S(2)}, u32[]{:S(2)}) collective-permute-start(bf16[512,768]{1,0:T(8,128)(2,1)} %get-tuple-element.155), channel_id=1, source_target_pairs={{0,1},{1,0},{2,3},{3,2},{4,5},{5,4},{6,7},{7,6},{8,9},{9,8},{10,11... | collective-permute-start | bytes 2359304 | tf_op jit(solution)/shard_map/ppermute | solution.py:557
  153.5 6.3 %copy-start.6 = (bf16[256,768]{1,0:T(8,128)(2,1)}, bf16[256,768]{1,0:T(8,128)(2,1)S(1)}, u32[]{:S(2)}) copy-start(bf16[256,768]{1,0:T(8,128)(2,1)S(1)} %collective-permute-done.26.far_ref) | copy-start | bytes 1179652
  153.5 17.1 %collective-permute-start.34 = (bf16[256,768]{1,0:T(8,128)(2,1)S(1)}, bf16[256,768]{1,0:T(8,128)(2,1)S(1)}, u32[]{:S(2)}, u32[]{:S(2)}) collective-permute-start(bf16[256,768]{1,0:T(8,128)(2,1)S(1)} %get-tuple-element.175), channel_id=1, source_target_pairs={{0,2},{1,3},{2,0},{3,1},{4,6},{5,7},{6,4},{7,5},{8,10},{9,11},{10,... | collective-permute-start | bytes 1179656 | tf_op jit(solution)/shard_map/ppermute | solution.py:557
  155.3 8.7 %collective-permute-start.30 = (bf16[96,768]{1,0:T(8,128)(2,1)S(1)}, bf16[96,768]{1,0:T(8,128)(2,1)S(1)}, u32[]{:S(2)}, u32[]{:S(2)}) collective-permute-start(bf16[96,768]{1,0:T(8,128)(2,1)S(1)} %get-tuple-element.166), channel_id=1, source_target_pairs={{0,24},{4,28},{8,16},{12,20},{16,8},{20,12},{24,0},{28,4},{1,25},{... | collective-permute-start | bytes 442376 | tf_op jit(solution)/shard_map/ppermute | solution.py:557
  159.0 10.8 %collective-permute-start.31 = (bf16[96,768]{1,0:T(8,128)(2,1)S(1)}, bf16[96,768]{1,0:T(8,128)(2,1)S(1)}, u32[]{:S(2)}, u32[]{:S(2)}) collective-permute-start(bf16[96,768]{1,0:T(8,128)(2,1)S(1)} %get-tuple-element.165), channel_id=1, source_target_pairs={{0,16},{4,20},{8,24},{12,28},{16,0},{20,4},{24,8},{28,12},{1,17},{... | collective-permute-start | bytes 442376 | tf_op jit(solution)/shard_map/ppermute | solution.py:557
  159.0 10.8 %collective-permute-start.33 = (bf16[96,768]{1,0:T(8,128)(2,1)S(1)}, bf16[96,768]{1,0:T(8,128)(2,1)S(1)}, u32[]{:S(2)}, u32[]{:S(2)}) collective-permute-start(bf16[96,768]{1,0:T(8,128)(2,1)S(1)} %get-tuple-element.164), channel_id=1, source_target_pairs={{0,8},{4,12},{8,0},{12,4},{16,24},{20,28},{24,16},{28,20},{1,9},{5... | collective-permute-start | bytes 442376 | tf_op jit(solution)/shard_map/ppermute | solution.py:557
  162.7 13.3 %copy-start.5 = (bf16[512,1,768]{2,0,1:T(8,128)(2,1)S(1)}, bf16[512,1,768]{2,0,1:T(8,128)(2,1)}, u32[]{:S(2)}) copy-start(bf16[512,1,768]{2,0,1:T(8,128)(2,1)} %param.16) | copy-start | bytes 2359300
  162.7 13.3 %copy-start.12 = (f32[16,1408]{1,0:T(8,128)S(1)}, f32[16,1408]{1,0:T(8,128)}, u32[]{:S(2)}) copy-start(f32[16,1408]{1,0:T(8,128)} %copy-done.11) | copy-start | bytes 270340
  170.6 0.8 copy-start.8
  171.3 8.5 %collective-permute-start.35 = (f32[96,384]{1,0:T(8,128)S(1)}, f32[96,384]{1,0:T(8,128)}, u32[]{:S(2)}, u32[]{:S(2)}) collective-permute-start(f32[96,384]{1,0:T(8,128)S(1)} %get-tuple-element.98), channel_id=1, source_target_pairs={{0,1},{1,0},{2,3},{3,2},{4,5},{5,4},{6,7},{7,6},{8,9},{9,8},{10,11... | collective-permute-start | bytes 442376 | tf_op jit(solution)/shard_map/ppermute | solution.py:557
  171.3 8.5 %collective-permute-start.36 = (f32[96,384]{1,0:T(8,128)S(1)}, f32[96,384]{1,0:T(8,128)}, u32[]{:S(2)}, u32[]{:S(2)}) collective-permute-start(f32[96,384]{1,0:T(8,128)S(1)} %get-tuple-element.98), channel_id=1, source_target_pairs={{0,2},{1,3},{2,0},{3,1},{4,6},{5,7},{6,4},{7,5},{8,10},{9,11},{10,... | collective-permute-start | bytes 442376 | tf_op jit(solution)/shard_map/ppermute | solution.py:557
  172.7 7.8 %collective-permute-start.37 = (f32[96,384]{1,0:T(8,128)S(1)}, f32[96,384]{1,0:T(8,128)}, u32[]{:S(2)}, u32[]{:S(2)}) collective-permute-start(f32[96,384]{1,0:T(8,128)S(1)} %get-tuple-element.98), channel_id=1, source_target_pairs={{0,3},{1,2},{2,1},{3,0},{4,7},{5,6},{6,5},{7,4},{8,11},{9,10},{10,... | collective-permute-start | bytes 442376 | tf_op jit(solution)/shard_map/ppermute | solution.py:557
  176.1 1.0 copy-start.7
  177.1 1.0 copy-start.9
  (1 other events, 0.6 us)

commit v5 on v4

--- a/solution.py
+++ b/solution.py
@@ -789,7 +789,7 @@
                 scratch_shapes=scratch,
             ),
             out_shape=out_shape,
-            compiler_params=limits(56 if name == "backward" else 36),
+            compiler_params=limits({"backward": 44, "forward": 32}.get(name, 28)),
             input_output_aliases=aliases,
             cost_estimate=pl.CostEstimate(
                 flops=int(micros * 1.0e9), bytes_accessed=int(micros * 3.0e6), transcendentals=0

time: 184 us -> 181 us (0.984)
  other arithmetic: 15 us -> 12.5 us
    pallas_call x4, Pallas kernels: 71.3 us -> 68.9 us  [call(): pl.pallas_call(kernel, grid_spec=pltpu.PrefetchScalarGridSpec(num_scalar_...]
    unnamed x56 -> x58, local copies, waits for them, and re-layouts: 7.36 us -> 8.66 us
  transfers between devices with their start and end apart: 38 -> 38, of which waited for: 12 -> 12; matrix products, arithmetic and copies ran while one was open for 15% -> 14% of each run, Pallas kernels for 36% -> 36%
where the time goes in v5:
time: 181 us; the launch traced here: 180 us
  Pallas kernels  72.6 us (40%)
  starting transfers between devices  39.1 us (22%)
  waiting for transfers between devices  27.9 us (15%)
  local copies, waits for them, and re-layouts  24.8 us (14%)
  other arithmetic  12.5 us (7%)
  between operations  3.26 us (2%)
    pallas_call x4, Pallas kernels, call(): pl.pallas_call(kernel, grid_spec=pltpu.PrefetchScalarGridSpec(num_scalar_...  68.9 us
    ppermute x38, starting transfers between devices, swap(): return lax.ppermute(values, axis, [(i, i ^ bits) for i in range(size)])  39.1 us
    ppermute x38, waiting for transfers between devices, swap(): return lax.ppermute(values, axis, [(i, i ^ bits) for i in range(size)])  27.9 us
    unnamed x58, local copies, waits for them, and re-layouts  8.66 us
    slice x3, local copies, waits for them, and re-layouts, per_device(): cut = lambda values, k: values[k * piece_len:(k + 1) * piece_len]  4.28 us
    pallas_call x2, Pallas kernels, whole(): pl.pallas_call(kernel, out_shape=out_shape, compiler_params=plain, name=n...  3.72 us
  transfers between devices with their start and end apart: 38, of which 12 were waited for; matrix products, arithmetic and copies ran while one was open for 14% of the time, Pallas kernels for 36%

profile of v5, /device:TPU:0, one launch (start us, length us, event | category | flops | bytes accessed | tf_op | source)
XLA Modules:
  0.0 180.3 jit_solution(273282902454915503)
XLA Ops:
  1.2 2.6 %collective-permute-start = (bf16[512,768]{1,0:T(8,128)(2,1)}, bf16[512,768]{1,0:T(8,128)(2,1)}, u32[]{:S(2)}, u32[]{:S(2)}) collective-permute-start(bf16[512,768]{1,0:T(8,128)(2,1)} %bitcast.88), channel_id=1, source_target_pairs={{0,2},{1,3},{2,0},{3,1},{4,6},{5,7},{6,4},{7,5},{8,10},{9,11},{10,... | collective-permute-start | bytes 2359304 | tf_op jit(solution)/shard_map/ppermute | solution.py:557
  3.7 0.9 slice_bitcast_fusion
  4.7 0.8 copy.45
  5.5 0.8 reshape.144
  6.2 0.8 reshape.143
  7.0 0.8 copy.46
  7.9 0.9 concatenate.10.refs_4_
  8.8 2.7 %collective-permute-start.7 = (bf16[96,768]{1,0:T(8,128)(2,1)S(1)}, bf16[96,768]{1,0:T(8,128)(2,1)}, u32[]{:S(2)}, u32[]{:S(2)}) collective-permute-start(bf16[96,768]{1,0:T(8,128)(2,1)S(1)} %concatenate.10.refs_4_), channel_id=1, source_target_pairs={{0,16},{4,20},{8,24},{12,28},{16,0},{20,4},{24,8},{28,12},{1,17},{... | collective-permute-start | bytes 442376 | tf_op jit(solution)/shard_map/ppermute | solution.py:557
  11.4 1.3 collective-permute-start.6
  13.8 1.6 pad_maximum_fusion.5
  15.4 0.7 stack.89
  16.0 0.7 broadcast_in_dim.38
  16.9 1.5 fusion.refs_10_.refs_18_
  18.5 3.7 %collective-permute-done.refs_2_ = bf16[512,768]{1,0:T(8,128)(2,1)} collective-permute-done((bf16[512,768]{1,0:T(8,128)(2,1)}, bf16[512,768]{1,0:T(8,128)(2,1)}, u32[]{:S(2)}, u32[]{:S(2)}) %collective-permute-start) | collective-permute-done | bytes 786464 | tf_op jit(solution)/shard_map/ppermute | solution.py:557
  22.9 1.7 collective-permute-start.10
  27.7 0.7 stack.85.info_ref
  28.4 1.7 collective-permute-start.5
  30.2 1.0 pad_maximum_fusion.1.refs_6_
  31.2 1.8 %collective-permute-done.9.refs_9_ = bf16[96,768]{1,0:T(8,128)(2,1)} collective-permute-done((bf16[96,768]{1,0:T(8,128)(2,1)S(1)}, bf16[96,768]{1,0:T(8,128)(2,1)}, u32[]{:S(2)}, u32[]{:S(2)}) %collective-permute-start.9) | collective-permute-done | bytes 147488 | tf_op jit(solution)/shard_map/ppermute | solution.py:557
  33.0 1.7 collective-permute-start.11
  34.7 1.0 select_bitcast_fusion.1
  35.8 1.6 collective-permute-start.13
  37.4 2.6 %collective-permute-start.14 = (bf16[2,96,768]{2,1,0:T(8,128)(2,1)S(1)}, bf16[2,96,768]{2,1,0:T(8,128)(2,1)S(1)}, u32[]{:S(2)}, u32[]{:S(2)}) collective-permute-start(bf16[2,96,768]{2,1,0:T(8,128)(2,1)S(1)} %pad_maximum_fusion.2), channel_id=1, source_target_pairs={{0,16},{4,20},{8,24},{12,28},{16,0},{20,4},{24,8},{28,12},{1,17},{... | collective-permute-start | bytes 884744 | tf_op jit(solution)/shard_map/ppermute | solution.py:557
  40.2 1.7 collective-permute-done.11.refs_7_
  42.0 1.8 collective-permute-start.2
  43.7 18.7 %forward.1 = (bf16[2048,768]{1,0:T(8,128)(2,1)S(1)}, bf16[2048,640]{1,0:T(8,128)(2,1)}, f32[2048,128]{1,0:T(8,128)}, f32[2048,384]{1,0:T(8,128)S(1)}, f32[2048,1...) custom-call(s32[5]{0:T(128)S(1)} %stack.85.info_ref, ...), custom_call_target="tpu_custom_call" | custom-call | flops 22000001024 | bytes 66000000 | tf_op jit(solution)/shard_map/forward/pallas_call | solution.py:782
  62.4 1.1 copy-done.19
  64.1 1.8 %collective-permute-done.12.refs_3_ = bf16[512,768]{1,0:T(8,128)(2,1)S(1)} collective-permute-done((bf16[512,768]{1,0:T(8,128)(2,1)S(1)}, bf16[512,768]{1,0:T(8,128)(2,1)S(1)}, u32[]{:S(2)}, u32[]{:S(2)}) %collective-permute-start.12) | collective-permute-done | bytes 786464 | tf_op jit(solution)/shard_map/ppermute | solution.py:557
  65.9 7.8 %branch.1 = (f32[2048,384]{1,0:T(8,128)S(1)}, bf16[2048,768]{1,0:T(8,128)(2,1)S(1)}, f32[8,2048]{1,0:T(8,128)S(1)}) custom-call(s32[5]{0:T(128)S(1)} %stack.85.info_ref, bf16[512,768]{1,0:T(8,128)(2,1)S(1)} %bitcast.98, bf16[512,768]{1,0:T(8,128)(2,1)S(1)} %collective-permute-done.1.refs_1_, bf16[512,768]{1,0:T(8,128)(2,1)S(1)} %collective-permute-done.2.refs_2_, ...), custom_call_target="tpu_custom_call" | custom-call | flops 11000000512 | bytes 33000000 | tf_op jit(solution)/shard_map/branch/pallas_call | solution.py:782
  74.2 1.1 collective-permute-start.18
  75.9 1.2 fusion.19
  77.7 1.0 collective-permute-done.17
  78.7 8.9 %gate_back.1 = (bf16[2048,384]{1,0:T(8,128)(2,1)}, bf16[2048,384]{1,0:T(8,128)(2,1)}, bf16[768,768]{1,0:T(8,128)(2,1)S(1)}, f32[8,384]{1,0:T(8,128)S(1)}, f32[768,128]{1,0:T(8,128)S(1)}) custom-call(s32[5]{0:T(128)S(1)} %stack.85.info_ref, bf16[512,768]{1,0:T(8,128)(2,1)S(1)} %bitcast.99, bf16[512,768]{1,0:T(8,128)(2,1)S(1)} %collective-permute-done.1.refs_1_, ...), custom_call_target="tpu_custom_call" | custom-call | flops 12999999488 | bytes 39000000 | tf_op jit(solution)/shard_map/gate_back/pallas_call | solution.py:782
  87.9 1.8 collective-permute-start.22
  90.0 1.7 add_convert_fusion.2
  91.7 1.4 collective-permute-start.21
  93.1 1.2 copy-done.21
  94.3 1.2 copy-done.22
  95.5 33.6 %backward.1 = (bf16[2048,768]{1,0:T(8,128)(2,1)}, bf16[768,768]{1,0:T(8,128)(2,1)S(1)}) custom-call(s32[5]{0:T(128)S(1)} %stack.85.info_ref, bf16[2048,768]{1,0:T(8,128)(2,1)} %copy-done.13, bf16[768,768]{1,0:T(8,128)(2,1)S(1)} %copy-done.20, bf16[768,768]{1,0:T(8,128)(2,1)S(1)} %bitcast.95, bf16[2048,640]{1,0:T(8,128)(2,1)} %get-tuple-element.67.refs_3_.refs_4_, ...), custom_call_target="tpu_custom_call" | custom-call | flops 35999997952 | bytes 108000000 | tf_op jit(solution)/shard_map/backward/pallas_call | solution.py:782
  129.1 0.8 copy-done.24
  129.9 2.1 %slice.143 = bf16[512,768]{1,0:T(8,128)(2,1)} slice(bf16[2048,768]{1,0:T(8,128)(2,1)} %get-tuple-element.90), slice={[1536:2048], [0:768]} | slice | bytes 1572864 | tf_op jit(solution)/shard_map/slice | solution.py:885
  133.2 3.7 %collective-permute-start.27 = (bf16[96,768]{1,0:T(8,128)(2,1)S(1)}, bf16[96,768]{1,0:T(8,128)(2,1)S(1)}, u32[]{:S(2)}, u32[]{:S(2)}) collective-permute-start(bf16[96,768]{1,0:T(8,128)(2,1)S(1)} %get-tuple-element.162), channel_id=1, source_target_pairs={{0,24},{4,28},{8,16},{12,20},{16,8},{20,12},{24,0},{28,4},{1,25},{... | collective-permute-start | bytes 442376 | tf_op jit(solution)/shard_map/ppermute | solution.py:557
  136.8 0.8 collective-permute-start.29
  137.7 1.2 collective-permute-start.32
  138.9 1.3 add_convert_fusion.1
  140.3 1.7 collective-permute-done.23
  142.0 0.7 collective-permute-start.26
  142.8 1.0 fusion.18
  143.8 4.1 %collective-permute-done.32 = bf16[2,96,768]{2,1,0:T(8,128)(2,1)S(1)} collective-permute-done((bf16[2,96,768]{2,1,0:T(8,128)(2,1)S(1)}, bf16[2,96,768]{2,1,0:T(8,128)(2,1)S(1)}, u32[]{:S(2)}, u32[]{:S(2)}) %collective-permute-start.32) | collective-permute-done | bytes 294944 | tf_op jit(solution)/shard_map/ppermute | solution.py:557
  147.9 4.4 %collective-permute-done.26.far_ref = bf16[256,768]{1,0:T(8,128)(2,1)S(1)} collective-permute-done((bf16[256,768]{1,0:T(8,128)(2,1)S(1)}, bf16[256,768]{1,0:T(8,128)(2,1)S(1)}, u32[]{:S(2)}, u32[]{:S(2)}) %collective-permute-start.26) | collective-permute-done | bytes 393248 | tf_op jit(solution)/shard_map/ppermute | solution.py:557
  152.3 0.7 collective-permute-start.34
  153.1 3.7 %collective-permute-start.30 = (bf16[96,768]{1,0:T(8,128)(2,1)S(1)}, bf16[96,768]{1,0:T(8,128)(2,1)S(1)}, u32[]{:S(2)}, u32[]{:S(2)}) collective-permute-start(bf16[96,768]{1,0:T(8,128)(2,1)S(1)} %get-tuple-element.166), channel_id=1, source_target_pairs={{0,24},{4,28},{8,16},{12,20},{16,8},{20,12},{24,0},{28,4},{1,25},{... | collective-permute-start | bytes 442376 | tf_op jit(solution)/shard_map/ppermute | solution.py:557
  156.8 0.8 collective-permute-start.33
  157.6 2.9 %fusion.1 = bf16[512,1,768]{2,0,1:T(8,128)(2,1)} fusion(bf16[512,768]{1,0:T(8,128)(2,1)} %collective-permute-done.21, bf16[512,768]{1,0:T(8,128)(2,1)} %collective-permute-done.20, f32[512]{0:T(512)S(1)} %bitcast.105, bf16[2048,768]{1,0:T(8,128)(2,1)} %copy-done.1, bf16[512,1,768]{2,0,1:T(8,128)(2,1)S(1)} %copy-done), kind=kLoop, calls=%fused_computation.5 | loop fusion | flops 3538944 | bytes 3934208 | tf_op jit(solution)/shard_map/broadcast_in_dim | solution.py:1063
  160.5 1.3 collective-permute-done.30.refs_4_
  161.8 5.8 %collective-permute-done.31.refs_5_ = bf16[96,768]{1,0:T(8,128)(2,1)S(1)} collective-permute-done((bf16[96,768]{1,0:T(8,128)(2,1)S(1)}, bf16[96,768]{1,0:T(8,128)(2,1)S(1)}, u32[]{:S(2)}, u32[]{:S(2)}) %collective-permute-start.31) | collective-permute-done | bytes 147488 | tf_op jit(solution)/shard_map/ppermute | solution.py:557
  167.6 0.8 weight_sums.1
  168.4 0.8 copy-done.7
  169.2 1.3 collective-permute-start.36
  171.1 0.7 copy.49
  172.6 0.7 reshape.148
  173.9 1.0 copy-done.8
  174.9 2.9 %hidden_back.1 = bf16[512,768]{1,0:T(8,128)(2,1)} custom-call(bf16[512,768]{1,0:T(8,128)(2,1)S(1)} %bitcast.90, bf16[512,768]{1,0:T(8,128)(2,1)S(1)} %bitcast.100, bf16[512,768]{1,0:T(8,128)(2,1)S(1)} %get-tuple-element.156.own_ref, bf16[512,768]{1,0:T(8,128)(2,1)} %collective-permute-done.25.near_ref, bf16[256,768]{1,0:T(8,128)(2,1)S(1)} %collective-permute-done.26.far_ref, ...), custom_call_target="tpu_custom_call" | custom-call | tf_op jit(solution)/shard_map/hidden_back/pallas_call | solution.py:1024
  179.0 0.7 slice_reduce_fusion
  (141 shorter events, 11.7 us)
Async XLA Ops:
  0.6 39.3 %collective-permute-start.3 = (bf16[512,768]{1,0:T(8,128)(2,1)}, bf16[512,768]{1,0:T(8,128)(2,1)}, u32[]{:S(2)}, u32[]{:S(2)}) collective-permute-start(bf16[512,768]{1,0:T(8,128)(2,1)} %bitcast.87), channel_id=1, source_target_pairs={{0,1},{1,0},{2,3},{3,2},{4,5},{5,4},{6,7},{7,6},{8,9},{9,8},{10,11... | collective-permute-start | bytes 2359304 | tf_op jit(solution)/shard_map/ppermute | solution.py:557
  1.2 21.0 %collective-permute-start = (bf16[512,768]{1,0:T(8,128)(2,1)}, bf16[512,768]{1,0:T(8,128)(2,1)}, u32[]{:S(2)}, u32[]{:S(2)}) collective-permute-start(bf16[512,768]{1,0:T(8,128)(2,1)} %bitcast.88), channel_id=1, source_target_pairs={{0,2},{1,3},{2,0},{3,1},{4,6},{5,7},{6,4},{7,5},{8,10},{9,11},{10,... | collective-permute-start | bytes 2359304 | tf_op jit(solution)/shard_map/ppermute | solution.py:557
  7.8 14.4 %copy-start.26 = (s32[1,4]{1,0:T(1,128)S(1)}, s32[1,4]{1,0:T(1,128)}, u32[]{:S(2)}) copy-start(s32[1,4]{1,0:T(1,128)} %param.17) | copy-start | bytes 52
  7.8 17.8 %copy-start.27 = (f32[6]{0:T(128)S(1)}, f32[6]{0:T(128)}, u32[]{:S(2)}) copy-start(f32[6]{0:T(128)} %param.25) | copy-start | bytes 76
  8.8 14.1 %collective-permute-start.7 = (bf16[96,768]{1,0:T(8,128)(2,1)S(1)}, bf16[96,768]{1,0:T(8,128)(2,1)}, u32[]{:S(2)}, u32[]{:S(2)}) collective-permute-start(bf16[96,768]{1,0:T(8,128)(2,1)S(1)} %concatenate.10.refs_4_), channel_id=1, source_target_pairs={{0,16},{4,20},{8,24},{12,28},{16,0},{20,4},{24,8},{28,12},{1,17},{... | collective-permute-start | bytes 442376 | tf_op jit(solution)/shard_map/ppermute | solution.py:557
  11.4 17.0 %collective-permute-start.6 = (bf16[96,768]{1,0:T(8,128)(2,1)S(1)}, bf16[96,768]{1,0:T(8,128)(2,1)}, u32[]{:S(2)}, u32[]{:S(2)}) collective-permute-start(bf16[96,768]{1,0:T(8,128)(2,1)S(1)} %concatenate.10.refs_4_), channel_id=1, source_target_pairs={{0,24},{4,28},{8,16},{12,20},{16,8},{20,12},{24,0},{28,4},{1,25},{... | collective-permute-start | bytes 442376 | tf_op jit(solution)/shard_map/ppermute | solution.py:557
  12.8 11.8 %collective-permute-start.8 = (bf16[96,768]{1,0:T(8,128)(2,1)S(1)}, bf16[96,768]{1,0:T(8,128)(2,1)S(1)}, u32[]{:S(2)}, u32[]{:S(2)}) collective-permute-start(bf16[96,768]{1,0:T(8,128)(2,1)S(1)} %concatenate.10.refs_4_), channel_id=1, source_target_pairs={{0,8},{4,12},{8,0},{12,4},{16,24},{20,28},{24,16},{28,20},{1,9},{5... | collective-permute-start | bytes 442376 | tf_op jit(solution)/shard_map/ppermute | solution.py:557
  16.9 26.8 %copy-start = (bf16[512,1,768]{2,0,1:T(8,128)(2,1)S(1)}, bf16[512,1,768]{2,0,1:T(8,128)(2,1)}, u32[]{:S(2)}) copy-start(bf16[512,1,768]{2,0,1:T(8,128)(2,1)} %param.15) | copy-start | bytes 2359300
  18.5 43.9 %copy-start.2 = (bf16[768,1408]{1,0:T(8,128)(2,1)}, bf16[768,1408]{1,0:T(8,128)(2,1)S(1)}, u32[]{:S(2)}) copy-start(bf16[768,1408]{1,0:T(8,128)(2,1)S(1)} %fusion.refs_10_.refs_18_) | copy-start | bytes 6488068
  22.2 19.8 %collective-permute-start.4 = (bf16[512,768]{1,0:T(8,128)(2,1)}, bf16[512,768]{1,0:T(8,128)(2,1)}, u32[]{:S(2)}, u32[]{:S(2)}) collective-permute-start(bf16[512,768]{1,0:T(8,128)(2,1)} %collective-permute-done.refs_2_), channel_id=1, source_target_pairs={{0,1},{1,0},{2,3},{3,2},{4,5},{5,4},{6,7},{7,6},{8,9},{9,8},{10,11... | collective-permute-start | bytes 2359304 | tf_op jit(solution)/shard_map/ppermute | solution.py:557
  22.9 8.3 %collective-permute-start.10 = (bf16[96,768]{1,0:T(8,128)(2,1)}, bf16[96,768]{1,0:T(8,128)(2,1)}, u32[]{:S(2)}, u32[]{:S(2)}) collective-permute-start(bf16[96,768]{1,0:T(8,128)(2,1)} %pad_maximum_fusion.5), channel_id=1, source_target_pairs={{0,4},{4,0},{8,12},{12,8},{16,20},{20,16},{24,28},{28,24},{1,5},{5... | collective-permute-start | bytes 442376 | tf_op jit(solution)/shard_map/ppermute | solution.py:557
  24.6 8.4 %collective-permute-start.9 = (bf16[96,768]{1,0:T(8,128)(2,1)S(1)}, bf16[96,768]{1,0:T(8,128)(2,1)}, u32[]{:S(2)}, u32[]{:S(2)}) collective-permute-start(bf16[96,768]{1,0:T(8,128)(2,1)S(1)} %collective-permute-done.8.refs_8_), channel_id=1, source_target_pairs={{0,4},{4,0},{8,12},{12,8},{16,20},{20,16},{24,28},{28,24},{1,5},{5... | collective-permute-start | bytes 442376 | tf_op jit(solution)/shard_map/ppermute | solution.py:557
  28.4 13.5 %copy-start.5 = (bf16[512,1,768]{2,0,1:T(8,128)(2,1)S(1)}, bf16[512,1,768]{2,0,1:T(8,128)(2,1)}, u32[]{:S(2)}) copy-start(bf16[512,1,768]{2,0,1:T(8,128)(2,1)} %param.16) | copy-start | bytes 2359300
  28.4 15.3 %copy-start.12 = (bf16[96,768]{1,0:T(8,128)(2,1)S(1)}, bf16[96,768]{1,0:T(8,128)(2,1)}, u32[]{:S(2)}) copy-start(bf16[96,768]{1,0:T(8,128)(2,1)} %copy-done.11) | copy-start | bytes 442372
  28.4 9.0 %collective-permute-start.5 = (bf16[96,768]{1,0:T(8,128)(2,1)S(1)}, bf16[96,768]{1,0:T(8,128)(2,1)S(1)}, u32[]{:S(2)}, u32[]{:S(2)}) collective-permute-start(bf16[96,768]{1,0:T(8,128)(2,1)S(1)} %concatenate.10.refs_4_), channel_id=1, source_target_pairs={{0,4},{4,0},{8,12},{12,8},{16,20},{20,16},{24,28},{28,24},{1,5},{5... | collective-permute-start | bytes 442376 | tf_op jit(solution)/shard_map/ppermute | solution.py:557
  33.0 8.9 %collective-permute-start.11 = (bf16[2,96,768]{2,1,0:T(8,128)(2,1)S(1)}, bf16[2,96,768]{2,1,0:T(8,128)(2,1)S(1)}, u32[]{:S(2)}, u32[]{:S(2)}) collective-permute-start(bf16[2,96,768]{2,1,0:T(8,128)(2,1)S(1)} %pad_maximum_fusion.1.refs_6_), channel_id=1, source_target_pairs={{0,4},{4,0},{8,12},{12,8},{16,20},{20,16},{24,28},{28,24},{1,5},{5... | collective-permute-start | bytes 884744 | tf_op jit(solution)/shard_map/ppermute | solution.py:557
  35.8 28.2 %collective-permute-start.13 = (bf16[2,96,768]{2,1,0:T(8,128)(2,1)S(1)}, bf16[2,96,768]{2,1,0:T(8,128)(2,1)S(1)}, u32[]{:S(2)}, u32[]{:S(2)}) collective-permute-start(bf16[2,96,768]{2,1,0:T(8,128)(2,1)S(1)} %pad_maximum_fusion.2), channel_id=1, source_target_pairs={{0,8},{4,12},{8,0},{12,4},{16,24},{20,28},{24,16},{28,20},{1,9},{5... | collective-permute-start | bytes 884744 | tf_op jit(solution)/shard_map/ppermute | solution.py:557
  37.4 26.6 %collective-permute-start.14 = (bf16[2,96,768]{2,1,0:T(8,128)(2,1)S(1)}, bf16[2,96,768]{2,1,0:T(8,128)(2,1)S(1)}, u32[]{:S(2)}, u32[]{:S(2)}) collective-permute-start(bf16[2,96,768]{2,1,0:T(8,128)(2,1)S(1)} %pad_maximum_fusion.2), channel_id=1, source_target_pairs={{0,16},{4,20},{8,24},{12,28},{16,0},{20,4},{24,8},{28,12},{1,17},{... | collective-permute-start | bytes 884744 | tf_op jit(solution)/shard_map/ppermute | solution.py:557
  40.0 24.0 %collective-permute-start.15 = (bf16[2,96,768]{2,1,0:T(8,128)(2,1)S(1)}, bf16[2,96,768]{2,1,0:T(8,128)(2,1)S(1)}, u32[]{:S(2)}, u32[]{:S(2)}) collective-permute-start(bf16[2,96,768]{2,1,0:T(8,128)(2,1)S(1)} %pad_maximum_fusion.2), channel_id=1, source_target_pairs={{0,24},{4,28},{8,16},{12,20},{16,8},{20,12},{24,0},{28,4},{1,25},{... | collective-permute-start | bytes 884744 | tf_op jit(solution)/shard_map/ppermute | solution.py:557
  41.9 22.1 %collective-permute-start.1 = (bf16[512,768]{1,0:T(8,128)(2,1)S(1)}, bf16[512,768]{1,0:T(8,128)(2,1)S(1)}, u32[]{:S(2)}, u32[]{:S(2)}) collective-permute-start(bf16[512,768]{1,0:T(8,128)(2,1)S(1)} %bitcast.96), channel_id=1, source_target_pairs={{0,1},{1,0},{2,3},{3,2},{4,5},{5,4},{6,7},{7,6},{8,9},{9,8},{10,11... | collective-permute-start | bytes 2359304 | tf_op jit(solution)/shard_map/ppermute | solution.py:557
  42.0 21.6 %collective-permute-start.2 = (bf16[512,768]{1,0:T(8,128)(2,1)S(1)}, bf16[512,768]{1,0:T(8,128)(2,1)S(1)}, u32[]{:S(2)}, u32[]{:S(2)}) collective-permute-start(bf16[512,768]{1,0:T(8,128)(2,1)S(1)} %bitcast.97), channel_id=1, source_target_pairs={{0,2},{1,3},{2,0},{3,1},{4,6},{5,7},{6,4},{7,5},{8,10},{9,11},{10,... | collective-permute-start | bytes 2359304 | tf_op jit(solution)/shard_map/ppermute | solution.py:557
  62.4 1.1 copy-start.19
  63.5 15.1 %copy-start.13 = (bf16[2048,768]{1,0:T(8,128)(2,1)}, bf16[2048,768]{1,0:T(8,128)(2,1)S(1)}, u32[]{:S(2)}) copy-start(bf16[2048,768]{1,0:T(8,128)(2,1)S(1)} %get-tuple-element.63.refs_4_.refs_5_.refs_0_) | copy-start | bytes 9437188
  63.5 15.1 %copy-start.14 = (f32[2048,384]{1,0:T(8,128)}, f32[2048,384]{1,0:T(8,128)S(1)}, u32[]{:S(2)}) copy-start(f32[2048,384]{1,0:T(8,128)S(1)} %get-tuple-element.64.refs_5_.refs_9_.refs_7_) | copy-start | bytes 9437188
  63.5 29.5 %copy-start.9 = (f32[16,1408]{1,0:T(8,128)}, f32[16,1408]{1,0:T(8,128)S(1)}, u32[]{:S(2)}) copy-start(f32[16,1408]{1,0:T(8,128)S(1)} %get-tuple-element.61.refs_12_.rows_ref) | copy-start | bytes 270340
  63.5 2.4 %collective-permute-start.12 = (bf16[512,768]{1,0:T(8,128)(2,1)S(1)}, bf16[512,768]{1,0:T(8,128)(2,1)S(1)}, u32[]{:S(2)}, u32[]{:S(2)}) collective-permute-start(bf16[512,768]{1,0:T(8,128)(2,1)S(1)} %collective-permute-done.2.refs_2_), channel_id=1, source_target_pairs={{0,1},{1,0},{2,3},{3,2},{4,5},{5,4},{6,7},{7,6},{8,9},{9,8},{10,11... | collective-permute-start | bytes 2359304 | tf_op jit(solution)/shard_map/ppermute | solution.py:557
  64.0 14.6 %copy-start.3 = (bf16[4,2,96,768]{3,2,1,0:T(8,128)(2,1)}, bf16[4,2,96,768]{3,2,1,0:T(8,128)(2,1)S(1)}, u32[]{:S(2)}) copy-start(bf16[4,2,96,768]{3,2,1,0:T(8,128)(2,1)S(1)} %bitcast_dynamic-update-slice_fusion) | copy-start | bytes 3538948
  73.7 3.5 %copy-start.1 = (bf16[2048,768]{1,0:T(8,128)(2,1)}, bf16[2048,768]{1,0:T(8,128)(2,1)S(1)}, u32[]{:S(2)}) copy-start(bf16[2048,768]{1,0:T(8,128)(2,1)S(1)} %get-tuple-element.65) | copy-start | bytes 9437188
  73.7 4.9 %collective-permute-start.17 = (f32[8,2048]{1,0:T(8,128)S(1)}, f32[8,2048]{1,0:T(8,128)S(1)}, u32[]{:S(2)}, u32[]{:S(2)}) collective-permute-start(f32[8,2048]{1,0:T(8,128)S(1)} %get-tuple-element.70), channel_id=1, source_target_pairs={{0,2},{1,3},{2,0},{3,1},{4,6},{5,7},{6,4},{7,5},{8,10},{9,11},{10,... | collective-permute-start | bytes 196616 | tf_op jit(solution)/shard_map/ppermute | solution.py:557
  74.2 4.4 %collective-permute-start.18 = (f32[8,2048]{1,0:T(8,128)S(1)}, f32[8,2048]{1,0:T(8,128)S(1)}, u32[]{:S(2)}, u32[]{:S(2)}) collective-permute-start(f32[8,2048]{1,0:T(8,128)S(1)} %get-tuple-element.70), channel_id=1, source_target_pairs={{0,3},{1,2},{2,1},{3,0},{4,7},{5,6},{6,5},{7,4},{8,11},{9,10},{10,... | collective-permute-start | bytes 196616 | tf_op jit(solution)/shard_map/ppermute | solution.py:557
  75.3 3.4 %collective-permute-start.16 = (f32[8,2048]{1,0:T(8,128)S(1)}, f32[8,2048]{1,0:T(8,128)S(1)}, u32[]{:S(2)}, u32[]{:S(2)}) collective-permute-start(f32[8,2048]{1,0:T(8,128)S(1)} %get-tuple-element.70), channel_id=1, source_target_pairs={{0,1},{1,0},{2,3},{3,2},{4,5},{5,4},{6,7},{7,6},{8,9},{9,8},{10,11... | collective-permute-start | bytes 196616 | tf_op jit(solution)/shard_map/ppermute | solution.py:557
  77.1 12.8 %collective-permute-start.19 = (bf16[512,768]{1,0:T(8,128)(2,1)}, bf16[512,768]{1,0:T(8,128)(2,1)}, u32[]{:S(2)}, u32[]{:S(2)}) collective-permute-start(bf16[512,768]{1,0:T(8,128)(2,1)} %get-tuple-element.158), channel_id=1, source_target_pairs={{0,1},{1,0},{2,3},{3,2},{4,5},{5,4},{6,7},{7,6},{8,9},{9,8},{10,11... | collective-permute-start | bytes 2359304 | tf_op jit(solution)/shard_map/ppermute | solution.py:557
  77.2 51.9 %collective-permute-start.20 = (bf16[512,768]{1,0:T(8,128)(2,1)}, bf16[512,768]{1,0:T(8,128)(2,1)}, u32[]{:S(2)}, u32[]{:S(2)}) collective-permute-start(bf16[512,768]{1,0:T(8,128)(2,1)} %get-tuple-element.157), channel_id=1, source_target_pairs={{0,1},{1,0},{2,3},{3,2},{4,5},{5,4},{6,7},{7,6},{8,9},{9,8},{10,11... | collective-permute-start | bytes 2359304 | tf_op jit(solution)/shard_map/ppermute | solution.py:557
  87.6 2.4 %copy-start.17 = (f32[768,128]{1,0:T(8,128)}, f32[768,128]{1,0:T(8,128)S(1)}, u32[]{:S(2)}) copy-start(f32[768,128]{1,0:T(8,128)S(1)} %get-tuple-element.77.refs_17_) | copy-start | bytes 1179652
  87.8 5.3 %copy-start.20 = (bf16[768,768]{1,0:T(8,128)(2,1)S(1)}, bf16[768,768]{1,0:T(8,128)(2,1)}, u32[]{:S(2)}) copy-start(bf16[768,768]{1,0:T(8,128)(2,1)} %copy-done.19) | copy-start | bytes 3538948
  87.8 5.2 %copy-start.16 = (bf16[2048,384]{1,0:T(8,128)(2,1)S(1)}, bf16[2048,384]{1,0:T(8,128)(2,1)}, u32[]{:S(2)}) copy-start(bf16[2048,384]{1,0:T(8,128)(2,1)} %get-tuple-element.72.refs_8_) | copy-start | bytes 4718596
  87.9 41.1 %collective-permute-start.22 = (bf16[4,96,768]{2,1,0:T(8,128)(2,1)S(1)}, bf16[4,96,768]{2,1,0:T(8,128)(2,1)S(1)}, u32[]{:S(2)}, u32[]{:S(2)}) collective-permute-start(bf16[4,96,768]{2,1,0:T(8,128)(2,1)S(1)} %pad_maximum_fusion), channel_id=1, source_target_pairs={{0,4},{4,0},{8,12},{12,8},{16,20},{20,16},{24,28},{28,24},{1,5},{5... | collective-permute-start | bytes 1769480 | tf_op jit(solution)/shard_map/ppermute | solution.py:557
  89.7 3.3 %copy-start.4 = (bf16[4,2,96,768]{3,2,1,0:T(8,128)(2,1)S(1)}, bf16[4,2,96,768]{3,2,1,0:T(8,128)(2,1)}, u32[]{:S(2)}) copy-start(bf16[4,2,96,768]{3,2,1,0:T(8,128)(2,1)} %copy-done.3) | copy-start | bytes 3538948
  89.8 3.3 %copy-start.15 = (bf16[2048,384]{1,0:T(8,128)(2,1)S(1)}, bf16[2048,384]{1,0:T(8,128)(2,1)}, u32[]{:S(2)}) copy-start(bf16[2048,384]{1,0:T(8,128)(2,1)} %get-tuple-element.74.refs_9_) | copy-start | bytes 4718596
  90.0 3.1 %copy-start.18 = (f32[768,128]{1,0:T(8,128)S(1)}, f32[768,128]{1,0:T(8,128)}, u32[]{:S(2)}) copy-start(f32[768,128]{1,0:T(8,128)} %copy-done.17) | copy-start | bytes 1179652
  91.7 37.4 %collective-permute-start.21 = (bf16[512,768]{1,0:T(8,128)(2,1)S(1)}, bf16[512,768]{1,0:T(8,128)(2,1)}, u32[]{:S(2)}, u32[]{:S(2)}) collective-permute-start(bf16[512,768]{1,0:T(8,128)(2,1)S(1)} %add_convert_fusion.2), channel_id=1, source_target_pairs={{0,2},{1,3},{2,0},{3,1},{4,6},{5,7},{6,4},{7,5},{8,10},{9,11},{10,... | collective-permute-start | bytes 2359304 | tf_op jit(solution)/shard_map/ppermute | solution.py:557
  93.1 1.2 copy-start.21
  94.3 1.2 copy-start.22
  129.1 0.8 copy-start.24
  132.0 5.7 %collective-permute-start.24 = (bf16[512,768]{1,0:T(8,128)(2,1)}, bf16[512,768]{1,0:T(8,128)(2,1)}, u32[]{:S(2)}, u32[]{:S(2)}) collective-permute-start(bf16[512,768]{1,0:T(8,128)(2,1)} %slice.143), channel_id=1, source_target_pairs={{0,1},{1,0},{2,3},{3,2},{4,5},{5,4},{6,7},{7,6},{8,9},{9,8},{10,11... | collective-permute-start | bytes 2359304 | tf_op jit(solution)/shard_map/ppermute | solution.py:557
  132.0 1.1 copy-start.25
  132.0 6.9 %copy-start.23 = (bf16[2048,768]{1,0:T(8,128)(2,1)S(1)}, bf16[2048,768]{1,0:T(8,128)(2,1)}, u32[]{:S(2)}) copy-start(bf16[2048,768]{1,0:T(8,128)(2,1)} %get-tuple-element.90) | copy-start | bytes 9437188
  132.1 9.9 %collective-permute-start.23 = (bf16[2,96,768]{2,1,0:T(8,128)(2,1)S(1)}, bf16[2,96,768]{2,1,0:T(8,128)(2,1)S(1)}, u32[]{:S(2)}, u32[]{:S(2)}) collective-permute-start(bf16[2,96,768]{2,1,0:T(8,128)(2,1)S(1)} %pad_maximum_fusion.3), channel_id=1, source_target_pairs={{0,4},{4,0},{8,12},{12,8},{16,20},{20,16},{24,28},{28,24},{1,5},{5... | collective-permute-start | bytes 884744 | tf_op jit(solution)/shard_map/ppermute | solution.py:557
  133.2 20.0 %collective-permute-start.27 = (bf16[96,768]{1,0:T(8,128)(2,1)S(1)}, bf16[96,768]{1,0:T(8,128)(2,1)S(1)}, u32[]{:S(2)}, u32[]{:S(2)}) collective-permute-start(bf16[96,768]{1,0:T(8,128)(2,1)S(1)} %get-tuple-element.162), channel_id=1, source_target_pairs={{0,24},{4,28},{8,16},{12,20},{16,8},{20,12},{24,0},{28,4},{1,25},{... | collective-permute-start | bytes 442376 | tf_op jit(solution)/shard_map/ppermute | solution.py:557
  136.8 20.0 %collective-permute-start.28 = (bf16[96,768]{1,0:T(8,128)(2,1)S(1)}, bf16[96,768]{1,0:T(8,128)(2,1)S(1)}, u32[]{:S(2)}, u32[]{:S(2)}) collective-permute-start(bf16[96,768]{1,0:T(8,128)(2,1)S(1)} %get-tuple-element.161), channel_id=1, source_target_pairs={{0,16},{4,20},{8,24},{12,28},{16,0},{20,4},{24,8},{28,12},{1,17},{... | collective-permute-start | bytes 442376 | tf_op jit(solution)/shard_map/ppermute | solution.py:557
  136.8 20.0 %collective-permute-start.29 = (bf16[96,768]{1,0:T(8,128)(2,1)S(1)}, bf16[96,768]{1,0:T(8,128)(2,1)S(1)}, u32[]{:S(2)}, u32[]{:S(2)}) collective-permute-start(bf16[96,768]{1,0:T(8,128)(2,1)S(1)} %get-tuple-element.160), channel_id=1, source_target_pairs={{0,8},{4,12},{8,0},{12,4},{16,24},{20,28},{24,16},{28,20},{1,9},{5... | collective-permute-start | bytes 442376 | tf_op jit(solution)/shard_map/ppermute | solution.py:557
  137.7 10.2 %collective-permute-start.32 = (bf16[2,96,768]{2,1,0:T(8,128)(2,1)S(1)}, bf16[2,96,768]{2,1,0:T(8,128)(2,1)S(1)}, u32[]{:S(2)}, u32[]{:S(2)}) collective-permute-start(bf16[2,96,768]{2,1,0:T(8,128)(2,1)S(1)} %pad_maximum_fusion.4), channel_id=1, source_target_pairs={{0,4},{4,0},{8,12},{12,8},{16,20},{20,16},{24,28},{28,24},{1,5},{5... | collective-permute-start | bytes 884744 | tf_op jit(solution)/shard_map/ppermute | solution.py:557
  142.0 10.4 %collective-permute-start.26 = (bf16[256,768]{1,0:T(8,128)(2,1)S(1)}, bf16[256,768]{1,0:T(8,128)(2,1)S(1)}, u32[]{:S(2)}, u32[]{:S(2)}) collective-permute-start(bf16[256,768]{1,0:T(8,128)(2,1)S(1)} %get-tuple-element.176), channel_id=1, source_target_pairs={{0,2},{1,3},{2,0},{3,1},{4,6},{5,7},{6,4},{7,5},{8,10},{9,11},{10,... | collective-permute-start | bytes 1179656 | tf_op jit(solution)/shard_map/ppermute | solution.py:557
  147.9 26.0 %collective-permute-start.25 = (bf16[512,768]{1,0:T(8,128)(2,1)}, bf16[512,768]{1,0:T(8,128)(2,1)}, u32[]{:S(2)}, u32[]{:S(2)}) collective-permute-start(bf16[512,768]{1,0:T(8,128)(2,1)} %get-tuple-element.155), channel_id=1, source_target_pairs={{0,1},{1,0},{2,3},{3,2},{4,5},{5,4},{6,7},{7,6},{8,9},{9,8},{10,11... | collective-permute-start | bytes 2359304 | tf_op jit(solution)/shard_map/ppermute | solution.py:557
  152.3 16.1 %collective-permute-start.34 = (bf16[256,768]{1,0:T(8,128)(2,1)S(1)}, bf16[256,768]{1,0:T(8,128)(2,1)S(1)}, u32[]{:S(2)}, u32[]{:S(2)}) collective-permute-start(bf16[256,768]{1,0:T(8,128)(2,1)S(1)} %get-tuple-element.175), channel_id=1, source_target_pairs={{0,2},{1,3},{2,0},{3,1},{4,6},{5,7},{6,4},{7,5},{8,10},{9,11},{10,... | collective-permute-start | bytes 1179656 | tf_op jit(solution)/shard_map/ppermute | solution.py:557
  153.1 8.7 %collective-permute-start.30 = (bf16[96,768]{1,0:T(8,128)(2,1)S(1)}, bf16[96,768]{1,0:T(8,128)(2,1)S(1)}, u32[]{:S(2)}, u32[]{:S(2)}) collective-permute-start(bf16[96,768]{1,0:T(8,128)(2,1)S(1)} %get-tuple-element.166), channel_id=1, source_target_pairs={{0,24},{4,28},{8,16},{12,20},{16,8},{20,12},{24,0},{28,4},{1,25},{... | collective-permute-start | bytes 442376 | tf_op jit(solution)/shard_map/ppermute | solution.py:557
  156.8 10.8 %collective-permute-start.31 = (bf16[96,768]{1,0:T(8,128)(2,1)S(1)}, bf16[96,768]{1,0:T(8,128)(2,1)S(1)}, u32[]{:S(2)}, u32[]{:S(2)}) collective-permute-start(bf16[96,768]{1,0:T(8,128)(2,1)S(1)} %get-tuple-element.165), channel_id=1, source_target_pairs={{0,16},{4,20},{8,24},{12,28},{16,0},{20,4},{24,8},{28,12},{1,17},{... | collective-permute-start | bytes 442376 | tf_op jit(solution)/shard_map/ppermute | solution.py:557
  156.8 10.8 %collective-permute-start.33 = (bf16[96,768]{1,0:T(8,128)(2,1)S(1)}, bf16[96,768]{1,0:T(8,128)(2,1)S(1)}, u32[]{:S(2)}, u32[]{:S(2)}) collective-permute-start(bf16[96,768]{1,0:T(8,128)(2,1)S(1)} %get-tuple-element.164), channel_id=1, source_target_pairs={{0,8},{4,12},{8,0},{12,4},{16,24},{20,28},{24,16},{28,20},{1,9},{5... | collective-permute-start | bytes 442376 | tf_op jit(solution)/shard_map/ppermute | solution.py:557
  160.5 13.4 %copy-start.6 = (bf16[512,1,768]{2,0,1:T(8,128)(2,1)S(1)}, bf16[512,1,768]{2,0,1:T(8,128)(2,1)}, u32[]{:S(2)}) copy-start(bf16[512,1,768]{2,0,1:T(8,128)(2,1)} %param.16) | copy-start | bytes 2359300
  160.5 13.4 %copy-start.10 = (f32[16,1408]{1,0:T(8,128)S(1)}, f32[16,1408]{1,0:T(8,128)}, u32[]{:S(2)}) copy-start(f32[16,1408]{1,0:T(8,128)} %copy-done.9) | copy-start | bytes 270340
  169.2 8.6 %collective-permute-start.35 = (f32[96,384]{1,0:T(8,128)S(1)}, f32[96,384]{1,0:T(8,128)S(1)}, u32[]{:S(2)}, u32[]{:S(2)}) collective-permute-start(f32[96,384]{1,0:T(8,128)S(1)} %get-tuple-element.98), channel_id=1, source_target_pairs={{0,1},{1,0},{2,3},{3,2},{4,5},{5,4},{6,7},{7,6},{8,9},{9,8},{10,11... | collective-permute-start | bytes 442376 | tf_op jit(solution)/shard_map/ppermute | solution.py:557
  169.2 8.6 %collective-permute-start.36 = (f32[96,384]{1,0:T(8,128)S(1)}, f32[96,384]{1,0:T(8,128)S(1)}, u32[]{:S(2)}, u32[]{:S(2)}) collective-permute-start(f32[96,384]{1,0:T(8,128)S(1)} %get-tuple-element.98), channel_id=1, source_target_pairs={{0,2},{1,3},{2,0},{3,1},{4,6},{5,7},{6,4},{7,5},{8,10},{9,11},{10,... | collective-permute-start | bytes 442376 | tf_op jit(solution)/shard_map/ppermute | solution.py:557
  170.5 7.7 %collective-permute-start.37 = (f32[96,384]{1,0:T(8,128)S(1)}, f32[96,384]{1,0:T(8,128)S(1)}, u32[]{:S(2)}, u32[]{:S(2)}) collective-permute-start(f32[96,384]{1,0:T(8,128)S(1)} %get-tuple-element.98), channel_id=1, source_target_pairs={{0,3},{1,2},{2,1},{3,0},{4,7},{5,6},{6,5},{7,4},{8,11},{9,10},{10,... | collective-permute-start | bytes 442376 | tf_op jit(solution)/shard_map/ppermute | solution.py:557
  173.9 1.0 copy-start.8
  (2 other events, 1.4 us)
